TPU v7x, 32 devices: a whole 2x2x4 slice. The times are simulated.
32 devices in a mesh: tm: 8 (over z, core), lat: 4 (over y, x).
Axes of the slice: x: 2, y: 2, z: 4, core: 2. Of those that a mesh axis runs over, the one named last changes fastest.
Arguments:
- control: float32 [8, 128, 4096], P('tm', 'lat'), may hold values from -6 to 6
- scales: float32 [8, 128, 4096], P('tm', 'lat'), may hold values from 0.25 to 2
- courant: float32 [8, 128, 4096], P('tm', 'lat'), may hold values from -0.7 to 0.7
- diffusion: float32 [8, 128, 4096], P('tm', 'lat'), may hold values from 0.01 to 0.075
- pacing: float32 [8, 16], P('tm'), may hold values from 0.5 to 1
Outputs:
- defect: float32 [8, 128, 4096], P('tm', 'lat')
- final_state: float32 [8, 128, 4096], P('tm', 'lat')
All inputs are finite; a program needn't handle non-finite values.
Results may differ from a plain program's by a relative error of at most 0.00002.
Values sent between devices are 32-bit elements; how exact they have to be, the bound alone decides.
No kernel may reach another device: no remote copies, remote signals or barrier semaphores. Data moves between devices by JAX's collectives and lax.ppermute only.
A program may use at most 64 MiB of HBM per device.

v0:
```python
import jax
import jax.numpy as jnp
from jax import lax
from jax.sharding import PartitionSpec as P

STEPS = 16
DEPTH = 4


def prefix(value, axis, join, neutral):
    count, mine = (lax.axis_size(axis), lax.axis_index(axis))
    pieces = lax.all_gather(value, axis)
    so_far = jnp.full_like(value, 0) + jnp.asarray(neutral, value.dtype)

    def turn(position, so_far):
        longer = join(so_far, pieces[position])
        return jnp.where(position < mine, longer, so_far)

    return lax.fori_loop(0, count - 1, turn, so_far)


def extended_2(shard, sides, width):
    for axis, dim in sides:
        count, length = (lax.axis_size(axis), shard.shape[dim])
        up = [(i, (i + 1) % count) for i in range(count - 1)]
        down = [(j, i) for i, j in up]
        last = lax.slice_in_dim(shard, length - width, length, axis=dim)
        first = lax.slice_in_dim(shard, 0, width, axis=dim)
        before = lax.ppermute(last, axis, up)
        after = lax.ppermute(first, axis, down)
        shard = jnp.concatenate([before, shard, after], axis=dim)
    return shard


def passed_along(value, axis, steps):
    count = lax.axis_size(axis)
    first, last = (max(0, -steps), min(count, count - steps))
    return lax.ppermute(value, axis, [(source, source + steps) for source in range(first, last)])


def advance(extended, courant, diffusion_now):
    centre = extended[:, 1:-1]
    southern = extended[:, :-2]
    northern = extended[:, 2:]
    eastern = jnp.roll(centre, -1, axis=2)
    western = jnp.roll(centre, 1, axis=2)
    upwind_pos = jnp.maximum(courant, 0.0)
    upwind_neg = jnp.minimum(courant, 0.0)
    return (
        centre
        - upwind_pos * (centre - southern)
        - upwind_neg * (northern - centre)
        + diffusion_now * (northern + southern + eastern + western - 4.0 * centre)
    )


def summed(earlier, later):
    return earlier + later


def on_device(control, scales, courant, diffusion, pacing):
    increment = scales * control
    before = prefix(increment, "tm", summed, jnp.zeros_like(increment))
    start_state = before + increment
    current = start_state
    row_count = current.shape[1]
    margin = DEPTH - 1
    coefficients = extended_2(jnp.concatenate([courant, diffusion], axis=0), (("lat", 1),), margin)
    for block_index in range(STEPS // DEPTH):
        extended = extended_2(current, (("lat", 1),), DEPTH)
        for inner_index in range(DEPTH):
            turn_index = block_index * DEPTH + inner_index
            span_rows = row_count + 2 * (margin - inner_index)
            window = coefficients[:, inner_index : inner_index + span_rows]
            extended = advance(
                extended, window[:1], window[1:] * pacing[:, turn_index][:, None, None]
            )
        current = extended
    previous = passed_along(current, "tm", 1)
    return (start_state - previous, current)


def solution(mesh):
    return jax.shard_map(
        on_device,
        mesh=mesh,
        in_specs=(
            P("tm", "lat", None),
            P("tm", "lat", None),
            P("tm", "lat", None),
            P("tm", "lat", None),
            P("tm", None),
        ),
        out_specs=(P("tm", "lat", None), P("tm", "lat", None)),
        check_vma=False,
    )
```

profile of v0, /device:TPU:16, one launch (start us, length us, event | category | flops | bytes accessed | tf_op | source)
XLA Modules:
  0.0 146.0 jit_solution(8053173625995005905)
XLA Ops:
  7.2 2.1 %mul.355 = f32[1,32,4096]{2,1,0:T(8,128)} multiply(f32[1,32,4096]{2,1,0:T(8,128)} %param.8, f32[1,32,4096]{2,1,0:T(8,128)} %param.7) | non-fusion elementwise | flops 131072 | bytes 1572864 | tf_op jit(solution)/shard_map/mul | solution.py:62
  9.5 0.7 fusion.76
  10.2 3.4 %collective-permute-start.2 = (f32[2,3,4096]{2,1,0:T(4,128)}, f32[2,3,4096]{2,1,0:T(4,128)S(1)}, u32[]{:S(2)}, u32[]{:S(2)}) collective-permute-start(f32[2,3,4096]{2,1,0:T(4,128)} %get-tuple-element.113), channel_id=1, source_target_pairs={{0,1},{1,2},{2,3},{4,5},{5,6},{6,7},{8,9},{9,10},{10,11},{12,13},{... | collective-permute-start | bytes 294920 | tf_op jit(solution)/shard_map/ppermute | solution.py:29
  13.6 1.3 collective-permute-start.3
  14.9 0.7 fusion.109
  15.6 41.4 %all-gather.3.cloned.1.call-done = f32[8,32,4096]{2,1,0:T(8,128)} async-done(((f32[1,32,4096]{2,1,0:T(8,128)}), f32[8,32,4096]{2,1,0:T(8,128)}) %all-gather.3.cloned.1.call-update) | async-done | bytes 4194320 | tf_op jit(solution)/shard_map/all_gather | solution.py:12
  57.1 8.7 %while.14 = (s32[]{:T(128)}, f32[1,32,4096]{2,1,0:T(8,128)S(1)}, s32[]{:T(128)}, f32[8,1,32,4096]{3,2,1,0:T(8,128)}, s32[]{:T(128)}, /*index=5*/s32[]{:T(128)}) while((s32[]{:T(128)}, f32[1,32,4096]{2,1,0:T(8,128)S(1)}, s32[]{:T(128)}, f32[8,1,32,4096]{3,2,1,0:T(8,128)}, s32[]{:T(128)}, /*index=5*/s32[]{:T(128)}) %tuple.91), condition=%wide.region_1.2_spmd.clone, body=%wide.region_0.1_spmd.clone.sunk | while | flops 393220 | bytes 1572957 | solution.py:19
  57.1 1.3 add_select_fusion.2
  58.4 1.2 add_select_fusion.2
  59.6 1.2 add_select_fusion.2
  60.9 1.2 add_select_fusion.2
  62.1 1.2 add_select_fusion.2
  63.3 1.2 add_select_fusion.2
  64.6 1.2 add_select_fusion.2
  65.9 3.4 %collective-permute-start = (f32[1,4,4096]{2,1,0:T(4,128)S(1)}, f32[1,4,4096]{2,1,0:T(4,128)S(1)}, u32[]{:S(2)}, u32[]{:S(2)}) collective-permute-start(f32[1,4,4096]{2,1,0:T(4,128)S(1)} %get-tuple-element.177), channel_id=1, source_target_pairs={{0,1},{1,2},{2,3},{4,5},{5,6},{6,7},{8,9},{9,10},{10,11},{12,13},{... | collective-permute-start | bytes 196616 | tf_op jit(solution)/shard_map/ppermute | solution.py:29
  69.3 1.3 collective-permute-start.1
  71.2 4.3 %collective-permute-done.1 = f32[1,4,4096]{2,1,0:T(4,128)S(1)} collective-permute-done((f32[1,4,4096]{2,1,0:T(4,128)S(1)}, f32[1,4,4096]{2,1,0:T(4,128)S(1)}, u32[]{:S(2)}, u32[]{:S(2)}) %collective-permute-start.1) | collective-permute-done | bytes 65568 | tf_op jit(solution)/shard_map/ppermute | solution.py:30
  75.8 1.1 fusion.25
  77.2 1.1 fusion.31
  78.7 1.3 fusion.35
  80.2 1.0 fusion.63
  81.3 4.3 %collective-permute-start.4 = (f32[1,4,4096]{2,1,0:T(4,128)S(1)}, f32[1,4,4096]{2,1,0:T(4,128)S(1)}, u32[]{:S(2)}, u32[]{:S(2)}) collective-permute-start(f32[1,4,4096]{2,1,0:T(4,128)S(1)} %get-tuple-element.175), channel_id=1, source_target_pairs={{0,1},{1,2},{2,3},{4,5},{5,6},{6,7},{8,9},{9,10},{10,11},{12,13},{... | collective-permute-start | bytes 196616 | tf_op jit(solution)/shard_map/ppermute | solution.py:29
  85.6 1.3 collective-permute-start.5
  86.9 0.6 collective-permute-done.4
  87.4 4.3 %collective-permute-done.5 = f32[1,4,4096]{2,1,0:T(4,128)S(1)} collective-permute-done((f32[1,4,4096]{2,1,0:T(4,128)S(1)}, f32[1,4,4096]{2,1,0:T(4,128)S(1)}, u32[]{:S(2)}, u32[]{:S(2)}) %collective-permute-start.5) | collective-permute-done | bytes 65568 | tf_op jit(solution)/shard_map/ppermute | solution.py:30
  92.0 1.1 fusion.18
  93.5 1.2 fusion.39
  95.0 1.2 fusion.43
  96.5 1.0 fusion.67
  97.6 3.4 %collective-permute-start.6 = (f32[1,4,4096]{2,1,0:T(4,128)S(1)}, f32[1,4,4096]{2,1,0:T(4,128)S(1)}, u32[]{:S(2)}, u32[]{:S(2)}) collective-permute-start(f32[1,4,4096]{2,1,0:T(4,128)S(1)} %get-tuple-element.173), channel_id=1, source_target_pairs={{0,1},{1,2},{2,3},{4,5},{5,6},{6,7},{8,9},{9,10},{10,11},{12,13},{... | collective-permute-start | bytes 196616 | tf_op jit(solution)/shard_map/ppermute | solution.py:29
  101.0 1.3 collective-permute-start.7
  102.3 0.6 collective-permute-done.6
  102.8 4.3 %collective-permute-done.7 = f32[1,4,4096]{2,1,0:T(4,128)S(1)} collective-permute-done((f32[1,4,4096]{2,1,0:T(4,128)S(1)}, f32[1,4,4096]{2,1,0:T(4,128)S(1)}, u32[]{:S(2)}, u32[]{:S(2)}) %collective-permute-start.7) | collective-permute-done | bytes 65568 | tf_op jit(solution)/shard_map/ppermute | solution.py:30
  107.4 1.1 fusion.11
  108.9 1.2 fusion.47
  110.4 1.2 fusion.51
  111.9 1.0 fusion.71
  113.0 2.8 %collective-permute-start.8 = (f32[1,4,4096]{2,1,0:T(4,128)S(1)}, f32[1,4,4096]{2,1,0:T(4,128)S(1)}, u32[]{:S(2)}, u32[]{:S(2)}) collective-permute-start(f32[1,4,4096]{2,1,0:T(4,128)S(1)} %get-tuple-element.171), channel_id=1, source_target_pairs={{0,1},{1,2},{2,3},{4,5},{5,6},{6,7},{8,9},{9,10},{10,11},{12,13},{... | collective-permute-start | bytes 196616 | tf_op jit(solution)/shard_map/ppermute | solution.py:29
  115.8 1.5 %collective-permute-start.9 = (f32[1,4,4096]{2,1,0:T(4,128)S(1)}, f32[1,4,4096]{2,1,0:T(4,128)S(1)}, u32[]{:S(2)}, u32[]{:S(2)}) collective-permute-start(f32[1,4,4096]{2,1,0:T(4,128)S(1)} %get-tuple-element.172), channel_id=1, source_target_pairs={{1,0},{2,1},{3,2},{5,4},{6,5},{7,6},{9,8},{10,9},{11,10},{13,12},{... | collective-permute-start | bytes 196616 | tf_op jit(solution)/shard_map/ppermute | solution.py:30
  117.3 0.4 collective-permute-done.8
  117.7 4.3 %collective-permute-done.9 = f32[1,4,4096]{2,1,0:T(4,128)S(1)} collective-permute-done((f32[1,4,4096]{2,1,0:T(4,128)S(1)}, f32[1,4,4096]{2,1,0:T(4,128)S(1)}, u32[]{:S(2)}, u32[]{:S(2)}) %collective-permute-start.9) | collective-permute-done | bytes 65568 | tf_op jit(solution)/shard_map/ppermute | solution.py:30
  122.3 1.1 fusion.4
  123.7 1.2 fusion.55
  125.3 1.2 fusion.59
  126.8 1.0 fusion.75
  127.8 1.9 %collective-permute-start.10 = (f32[1,32,4096]{2,1,0:T(8,128)S(1)}, f32[1,32,4096]{2,1,0:T(8,128)S(1)}, u32[]{:S(2)}, u32[]{:S(2)}) collective-permute-start(f32[1,32,4096]{2,1,0:T(8,128)S(1)} %fusion.75), channel_id=1, source_target_pairs={{0,4},{4,8},{8,12},{12,16},{16,20},{20,24},{24,28},{1,5},{5,9},{9,... | collective-permute-start | bytes 1572872 | tf_op jit(solution)/shard_map/ppermute | solution.py:38
  129.7 8.6 %collective-permute-done.10 = f32[1,32,4096]{2,1,0:T(8,128)S(1)} collective-permute-done((f32[1,32,4096]{2,1,0:T(8,128)S(1)}, f32[1,32,4096]{2,1,0:T(8,128)S(1)}, u32[]{:S(2)}, u32[]{:S(2)}) %collective-permute-start.10) | collective-permute-done | bytes 524320 | tf_op jit(solution)/shard_map/ppermute | solution.py:38
  138.3 0.9 sub.323
  (56 shorter events, 5.8 us)
Async XLA Ops:
  7.2 2.2 %copy-start = (f32[1,32,4096]{2,1,0:T(8,128)S(1)}, f32[1,32,4096]{2,1,0:T(8,128)}, u32[]{:S(2)}) copy-start(f32[1,32,4096]{2,1,0:T(8,128)} %param.9) | copy-start | bytes 1572868
  7.2 2.3 %copy-start.1 = (f32[1,32,4096]{2,1,0:T(8,128)S(1)}, f32[1,32,4096]{2,1,0:T(8,128)}, u32[]{:S(2)}) copy-start(f32[1,32,4096]{2,1,0:T(8,128)} %param.10) | copy-start | bytes 1572868
  7.2 49.9 %all-gather.3.cloned.1.call-start = ((), (), s32[]{:S(2)}) async-start(), calls=%async_computation | async-start | bytes 4718592 | tf_op jit(solution)/shard_map/all_gather | solution.py:12
  9.4 5.5 %copy-start.4 = (f32[1,16]{1,0:T(1,128)S(1)}, f32[1,16]{1,0:T(1,128)}, u32[]{:S(2)}) copy-start(f32[1,16]{1,0:T(1,128)} %param.11) | copy-start | bytes 196
  10.2 60.4 %collective-permute-start.2 = (f32[2,3,4096]{2,1,0:T(4,128)}, f32[2,3,4096]{2,1,0:T(4,128)S(1)}, u32[]{:S(2)}, u32[]{:S(2)}) collective-permute-start(f32[2,3,4096]{2,1,0:T(4,128)} %get-tuple-element.113), channel_id=1, source_target_pairs={{0,1},{1,2},{2,3},{4,5},{5,6},{6,7},{8,9},{9,10},{10,11},{12,13},{... | collective-permute-start | bytes 294920 | tf_op jit(solution)/shard_map/ppermute | solution.py:29
  13.6 57.0 %collective-permute-start.3 = (f32[2,3,4096]{2,1,0:T(4,128)S(1)}, f32[2,3,4096]{2,1,0:T(4,128)S(1)}, u32[]{:S(2)}, u32[]{:S(2)}) collective-permute-start(f32[2,3,4096]{2,1,0:T(4,128)S(1)} %get-tuple-element.114), channel_id=1, source_target_pairs={{1,0},{2,1},{3,2},{5,4},{6,5},{7,6},{9,8},{10,9},{11,10},{13,12},{... | collective-permute-start | bytes 294920 | tf_op jit(solution)/shard_map/ppermute | solution.py:30
  57.1 8.7 %copy-start.2 = (f32[1,32,4096]{2,1,0:T(8,128)S(1)}, f32[1,32,4096]{2,1,0:T(8,128)}, u32[]{:S(2)}) copy-start(f32[1,32,4096]{2,1,0:T(8,128)} %mul.355) | copy-start | bytes 1572868
  65.9 5.3 %collective-permute-start = (f32[1,4,4096]{2,1,0:T(4,128)S(1)}, f32[1,4,4096]{2,1,0:T(4,128)S(1)}, u32[]{:S(2)}, u32[]{:S(2)}) collective-permute-start(f32[1,4,4096]{2,1,0:T(4,128)S(1)} %get-tuple-element.177), channel_id=1, source_target_pairs={{0,1},{1,2},{2,3},{4,5},{5,6},{6,7},{8,9},{9,10},{10,11},{12,13},{... | collective-permute-start | bytes 196616 | tf_op jit(solution)/shard_map/ppermute | solution.py:29
  69.3 6.2 %collective-permute-start.1 = (f32[1,4,4096]{2,1,0:T(4,128)S(1)}, f32[1,4,4096]{2,1,0:T(4,128)S(1)}, u32[]{:S(2)}, u32[]{:S(2)}) collective-permute-start(f32[1,4,4096]{2,1,0:T(4,128)S(1)} %get-tuple-element.178), channel_id=1, source_target_pairs={{1,0},{2,1},{3,2},{5,4},{6,5},{7,6},{9,8},{10,9},{11,10},{13,12},{... | collective-permute-start | bytes 196616 | tf_op jit(solution)/shard_map/ppermute | solution.py:30
  81.3 6.2 %collective-permute-start.4 = (f32[1,4,4096]{2,1,0:T(4,128)S(1)}, f32[1,4,4096]{2,1,0:T(4,128)S(1)}, u32[]{:S(2)}, u32[]{:S(2)}) collective-permute-start(f32[1,4,4096]{2,1,0:T(4,128)S(1)} %get-tuple-element.175), channel_id=1, source_target_pairs={{0,1},{1,2},{2,3},{4,5},{5,6},{6,7},{8,9},{9,10},{10,11},{12,13},{... | collective-permute-start | bytes 196616 | tf_op jit(solution)/shard_map/ppermute | solution.py:29
  85.6 6.2 %collective-permute-start.5 = (f32[1,4,4096]{2,1,0:T(4,128)S(1)}, f32[1,4,4096]{2,1,0:T(4,128)S(1)}, u32[]{:S(2)}, u32[]{:S(2)}) collective-permute-start(f32[1,4,4096]{2,1,0:T(4,128)S(1)} %get-tuple-element.176), channel_id=1, source_target_pairs={{1,0},{2,1},{3,2},{5,4},{6,5},{7,6},{9,8},{10,9},{11,10},{13,12},{... | collective-permute-start | bytes 196616 | tf_op jit(solution)/shard_map/ppermute | solution.py:30
  97.6 5.3 %collective-permute-start.6 = (f32[1,4,4096]{2,1,0:T(4,128)S(1)}, f32[1,4,4096]{2,1,0:T(4,128)S(1)}, u32[]{:S(2)}, u32[]{:S(2)}) collective-permute-start(f32[1,4,4096]{2,1,0:T(4,128)S(1)} %get-tuple-element.173), channel_id=1, source_target_pairs={{0,1},{1,2},{2,3},{4,5},{5,6},{6,7},{8,9},{9,10},{10,11},{12,13},{... | collective-permute-start | bytes 196616 | tf_op jit(solution)/shard_map/ppermute | solution.py:29
  101.0 6.2 %collective-permute-start.7 = (f32[1,4,4096]{2,1,0:T(4,128)S(1)}, f32[1,4,4096]{2,1,0:T(4,128)S(1)}, u32[]{:S(2)}, u32[]{:S(2)}) collective-permute-start(f32[1,4,4096]{2,1,0:T(4,128)S(1)} %get-tuple-element.174), channel_id=1, source_target_pairs={{1,0},{2,1},{3,2},{5,4},{6,5},{7,6},{9,8},{10,9},{11,10},{13,12},{... | collective-permute-start | bytes 196616 | tf_op jit(solution)/shard_map/ppermute | solution.py:30
  113.0 4.7 %collective-permute-start.8 = (f32[1,4,4096]{2,1,0:T(4,128)S(1)}, f32[1,4,4096]{2,1,0:T(4,128)S(1)}, u32[]{:S(2)}, u32[]{:S(2)}) collective-permute-start(f32[1,4,4096]{2,1,0:T(4,128)S(1)} %get-tuple-element.171), channel_id=1, source_target_pairs={{0,1},{1,2},{2,3},{4,5},{5,6},{6,7},{8,9},{9,10},{10,11},{12,13},{... | collective-permute-start | bytes 196616 | tf_op jit(solution)/shard_map/ppermute | solution.py:29
  115.8 6.2 %collective-permute-start.9 = (f32[1,4,4096]{2,1,0:T(4,128)S(1)}, f32[1,4,4096]{2,1,0:T(4,128)S(1)}, u32[]{:S(2)}, u32[]{:S(2)}) collective-permute-start(f32[1,4,4096]{2,1,0:T(4,128)S(1)} %get-tuple-element.172), channel_id=1, source_target_pairs={{1,0},{2,1},{3,2},{5,4},{6,5},{7,6},{9,8},{10,9},{11,10},{13,12},{... | collective-permute-start | bytes 196616 | tf_op jit(solution)/shard_map/ppermute | solution.py:30
  127.8 11.4 %copy-start.3 = (f32[1,32,4096]{2,1,0:T(8,128)}, f32[1,32,4096]{2,1,0:T(8,128)S(1)}, u32[]{:S(2)}) copy-start(f32[1,32,4096]{2,1,0:T(8,128)S(1)} %fusion.75) | copy-start | bytes 1572868
  127.8 10.5 %collective-permute-start.10 = (f32[1,32,4096]{2,1,0:T(8,128)S(1)}, f32[1,32,4096]{2,1,0:T(8,128)S(1)}, u32[]{:S(2)}, u32[]{:S(2)}) collective-permute-start(f32[1,32,4096]{2,1,0:T(8,128)S(1)} %fusion.75), channel_id=1, source_target_pairs={{0,4},{4,8},{8,12},{12,16},{16,20},{20,24},{24,28},{1,5},{5,9},{9,... | collective-permute-start | bytes 1572872 | tf_op jit(solution)/shard_map/ppermute | solution.py:38
Sparse Core Ops, SparseCore 0:
  10.2 46.8 all-gather.2
where the time goes:
time: 147 us; the launch traced here: 146 us
  waiting for transfers between devices  69.1 us (47%)
  other arithmetic  30.2 us (21%)
  starting transfers between devices  25.8 us (18%)
  between operations  14.4 us (10%)
  local copies, waits for them, and re-layouts  6.27 us (4%)
    all_gather x1, waiting for transfers between devices, prefix(): pieces = lax.all_gather(value, axis)  41.4 us
    add x16, other arithmetic, advance(): centre - upwind_pos * (centre - southern) - upwind_neg * (northern - centre)  18.2 us
    ppermute x5, starting transfers between devices, extended_2(): before = lax.ppermute(last, axis, up)  17.2 us
    ppermute x5, waiting for transfers between devices, extended_2(): after = lax.ppermute(first, axis, down)  17.1 us
    ppermute x1, waiting for transfers between devices, passed_along(): lax.ppermute(value, axis, [(source, source + steps) for source in range(f...  8.57 us
    select_n x7, other arithmetic, turn(): return jnp.where(position < mine, longer, so_far)  8.57 us
    ppermute x5, starting transfers between devices, extended_2(): after = lax.ppermute(first, axis, down)  6.64 us
    slice x28, local copies, waits for them, and re-layouts, advance(): western = jnp.roll(centre, 1, axis=2)  4.64 us
  transfers between devices with their start and end apart: 12, of which 10 were waited for; matrix products, arithmetic and copies ran while one was open for 7% of the time, Pallas kernels for 0%

commit v1 on v0

v1 whole, which is shorter than its diff:
```python
import functools

import jax
import jax.numpy as jnp
from jax import lax
from jax.experimental import pallas as pl
from jax.experimental.pallas import tpu as pltpu
from jax.sharding import PartitionSpec as P

LANES = 128
SUBLANES = 8


def up_to(value, multiple):
    return -(-value // multiple) * multiple


def steps_kernel(steps, rows, places, own, other, before, after, courant, diffusion, coef_before,
                 coef_after, pacing, out, even, odd, c_all, d_all):
    halves, tiles = 2, courant.shape[1] // LANES
    half = tiles // halves
    base = SUBLANES
    total = rows + 2 * steps
    core, has_before, has_after = places[0], places[1], places[2]
    here = slice(base + steps, base + steps + rows)
    south = slice(base, base + steps)
    north = slice(base + steps + rows, base + total)
    for t in range(half):
        cols = slice(t * LANES, (t + 1) * LANES)
        for which, source in ((0, own), (1, other)):
            to = 1 + t + half * jnp.where(core == which, 0, 1)
            even[to, here, :] = source[:, cols]
            even[to, south, :] = jnp.where(has_before > 0, before[which, :, cols], 0.0)
            even[to, north, :] = jnp.where(has_after > 0, after[which, :, cols], 0.0)
    for t in range(tiles):
        cols = slice(t * LANES, (t + 1) * LANES)
        for which, source, scratch in ((0, courant, c_all), (1, diffusion, d_all)):
            scratch[t, here, :] = source[:, cols]
            scratch[t, south, :] = jnp.where(has_before > 0, coef_before[which, :, cols], 0.0)
            scratch[t, north, :] = jnp.where(has_after > 0, coef_after[which, :, cols], 0.0)
    for step in range(1, steps + 1):
        old, new = (even, odd) if step % 2 else (odd, even)
        count = up_to(total - 2 * step, SUBLANES)
        first = base + step
        pace = pacing[0, step - 1]
        old[0, :, :] = old[tiles, :, :]
        old[tiles + 1, :, :] = old[1, :, :]
        lane = lax.broadcasted_iota(jnp.int32, (count, LANES), 1)
        window = slice(first, first + count)
        for t in range(1, tiles + 1):
            x = old[t, window, :]
            east = pltpu.roll(jnp.where(lane == 0, old[t + 1, window, :], x), LANES - 1, 1)
            west = pltpu.roll(jnp.where(lane == LANES - 1, old[t - 1, window, :], x), 1, 1)
            ahead = old[t, first + 1 : first + 1 + count, :] - x
            behind = x - old[t, first - 1 : first - 1 + count, :]
            c = c_all[t - 1, window, :]
            d = d_all[t - 1, window, :]
            spread = ((east - x) + (west - x)) + (ahead - behind)
            new[t, window, :] = x + (d * pace) * spread - c * jnp.where(c > 0, behind, ahead)
    last = odd if steps % 2 else even
    for t in range(tiles):
        out[:, t * LANES : (t + 1) * LANES] = last[t + 1, here, :]


def run_steps(steps, places, own, other, before, after, courant, diffusion, coef_before, coef_after, pacing):
    rows, columns = courant.shape
    tiles = columns // LANES
    depth = SUBLANES + rows + 2 * steps + 2 * SUBLANES
    smem = pl.BlockSpec(memory_space=pltpu.SMEM)
    vmem = pl.BlockSpec(memory_space=pltpu.VMEM)
    return pl.pallas_call(
        functools.partial(steps_kernel, steps, rows),
        out_shape=jax.ShapeDtypeStruct((rows, columns), jnp.float32),
        in_specs=[smem] + [vmem] * 8 + [smem],
        out_specs=vmem,
        scratch_shapes=[pltpu.VMEM((tiles + 2, depth, LANES), jnp.float32)] * 2
        + [pltpu.VMEM((tiles, depth, LANES), jnp.float32)] * 2,
        compiler_params=pltpu.CompilerParams(vmem_limit_bytes=40 * 2**20),
    )(places, own, other, before, after, courant, diffusion, coef_before, coef_after, pacing)


def on_device(control, scales, courant, diffusion, pacing):
    control, scales, courant, diffusion = (v[0] for v in (control, scales, courant, diffusion))
    steps = pacing.shape[1]
    rows, columns = control.shape
    half = columns // 2
    windows, bands = lax.axis_size("tm"), lax.axis_size("lat")
    window, band = lax.axis_index("tm"), lax.axis_index("lat")
    core, chip = window % 2, window // 2
    is_first = core == 0
    onward = [(i, (i + 1) % bands) for i in range(bands)]
    backward = [(j, i) for i, j in onward]
    partner = [(i, i ^ 1) for i in range(windows)]

    increment = scales * control
    left, right = increment[:, :half], increment[:, half:]
    own = jnp.where(is_first, left, right)
    other = jnp.where(is_first, right, left)

    coefficients = jnp.stack([courant, diffusion])
    coef_before = lax.ppermute(coefficients[:, rows - steps :], "lat", onward)
    coef_after = lax.ppermute(coefficients[:, :steps], "lat", backward)

    pair = own + lax.ppermute(other, "tm", partner)
    total, before = pair, jnp.zeros_like(pair)
    distance = 1
    while 2 * distance < windows:
        swap = [(i, i ^ (2 * distance)) for i in range(windows)]
        arrived = lax.ppermute(total, "tm", swap)
        before = before + jnp.where((chip // distance) % 2 == 1, arrived, 0.0)
        total = total + arrived
        distance *= 2
    through_first = before + own
    arrived = lax.ppermute(jnp.where(is_first, through_first, before), "tm", partner)
    start_own = jnp.where(is_first, through_first, before + pair)
    start_other = arrived + other

    start_before = lax.ppermute(jnp.stack([start_own[rows - steps :], start_other[rows - steps :]]), "lat", onward)
    start_after = lax.ppermute(jnp.stack([start_own[:steps], start_other[:steps]]), "lat", backward)
    places = jnp.stack([core, band, bands - 1 - band]).astype(jnp.int32)
    final = run_steps(steps, places, start_own, start_other, start_before, start_after, courant, diffusion,
                      coef_before, coef_after, pacing)
    previous = lax.ppermute(final, "tm", [(i, i + 1) for i in range(windows - 1)])
    start = jnp.where(is_first, jnp.concatenate([start_own, start_other], axis=1),
                      jnp.concatenate([start_other, start_own], axis=1))
    return (start - previous)[None], final[None]


def solution(mesh):
    whole = P("tm", "lat", None)
    return jax.shard_map(
        on_device,
        mesh=mesh,
        in_specs=(whole, whole, whole, whole, P("tm", None)),
        out_specs=(whole, whole),
        check_vma=False,
    )
```

time: 147 us -> 74.3 us (0.51)
  the two profiles are of different devices: /device:TPU:16 before, /device:TPU:10 now
where the time goes in v1:
time: 74.3 us; the launch traced here: 74.1 us
  waiting for transfers between devices  46.9 us (63%)
  starting transfers between devices  10.2 us (14%)
  Pallas kernels  9.64 us (13%)
  other arithmetic  3.91 us (5%)
  local copies, waits for them, and re-layouts  2.73 us (4%)
    ppermute x2, waiting for transfers between devices, on_device(): arrived = lax.ppermute(total, 'tm', swap)  14.4 us
    ppermute x1, waiting for transfers between devices, on_device(): coef_before = lax.ppermute(coefficients[:, rows - steps:], 'lat', onward)  11.3 us
    pallas_call x1, Pallas kernels, run_steps(): pl.pallas_call(functools.partial(steps_kernel, steps, rows), out_shape=ja...  9.64 us
    ppermute x1, waiting for transfers between devices, on_device(): lax.ppermute(final, 'tm', [(i, i + 1) for i in range(windows - 1)])  8.78 us
    ppermute x1, waiting for transfers between devices, on_device(): lax.ppermute(jnp.stack([start_own[rows - steps:], start_other[rows - step...  5.62 us
    ppermute x1, waiting for transfers between devices, on_device(): lax.ppermute(jnp.stack([start_own[:steps], start_other[:steps]]), 'lat',...  3.56 us
    ppermute x2, starting transfers between devices, on_device(): arrived = lax.ppermute(total, 'tm', swap)  3.17 us
    ppermute x1, starting transfers between devices, on_device(): coef_before = lax.ppermute(coefficients[:, rows - steps:], 'lat', onward)  2.39 us
  transfers between devices with their start and end apart: 9, of which 9 were waited for; matrix products, arithmetic and copies ran while one was open for 4% of the time, Pallas kernels for 0%

profile of v1, /device:TPU:10, one launch (start us, length us, event | category | flops | bytes accessed | tf_op | source)
XLA Modules:
  0.0 74.1 jit_solution(2993866369104806339)
XLA Ops:
  0.6 1.3 %multiply_bitcast_fusion = f32[32,4096]{1,0:T(8,128)S(1)} fusion(f32[1,32,4096]{2,1,0:T(8,128)} %param.6, f32[1,32,4096]{2,1,0:T(8,128)} %param.5), kind=kLoop, calls=%fused_computation.3 | loop fusion | flops 131072 | bytes 1572864 | tf_op jit(solution)/shard_map/mul | solution.py:95
  1.9 0.0 copy-start
  2.0 0.1 collective-permute-start
  2.0 0.9 %copy-done = f32[1,32,4096]{2,1,0:T(8,128)S(1)} copy-done((f32[1,32,4096]{2,1,0:T(8,128)S(1)}, f32[1,32,4096]{2,1,0:T(8,128)}, u32[]{:S(2)}) %copy-start) | copy-done | bytes 524312
  3.0 0.0 copy-start.1
  3.0 0.6 collective-permute-done
  3.6 0.1 fusion.2
  3.6 0.5 collective-permute-start.1
  4.1 0.0 copy-done.1
  4.2 7.9 %collective-permute-done.1 = f32[32,2048]{1,0:T(8,128)S(1)} collective-permute-done((f32[32,2048]{1,0:T(8,128)S(1)}, f32[32,2048]{1,0:T(8,128)S(1)}, u32[]{:S(2)}, u32[]{:S(2)}) %collective-permute-start.1) | collective-permute-done | bytes 262176 | tf_op jit(solution)/shard_map/ppermute | solution.py:109
  12.1 2.7 %collective-permute-start.2 = (f32[32,2048]{1,0:T(8,128)S(1)}, f32[32,2048]{1,0:T(8,128)}, u32[]{:S(2)}, u32[]{:S(2)}) collective-permute-start(f32[32,2048]{1,0:T(8,128)S(1)} %add.35), channel_id=1, source_target_pairs={{0,16},{4,20},{8,24},{12,28},{16,0},{20,4},{24,8},{28,12},{1,17},{... | collective-permute-start | bytes 786440 | tf_op jit(solution)/shard_map/ppermute | solution.py:109
  14.7 1.0 %fusion.3 = (f32[2,16,4096]{2,1,0:T(8,128)}, f32[2,16,4096]{2,1,0:T(8,128)}) fusion(f32[2,32,4096]{2,1,0:T(8,128)S(1)} %constant_dynamic-update-slice_fusion), kind=kLoop, calls=%fused_computation.19 | loop fusion | bytes 2097152 | tf_op jit(solution)/shard_map/slice | solution.py:102
  15.8 0.5 collective-permute-start.7
  16.3 2.4 %collective-permute-start.6 = (f32[2,16,4096]{2,1,0:T(8,128)}, f32[2,16,4096]{2,1,0:T(8,128)S(1)}, u32[]{:S(2)}, u32[]{:S(2)}) collective-permute-start(f32[2,16,4096]{2,1,0:T(8,128)} %get-tuple-element.3), channel_id=1, source_target_pairs={{0,1},{1,2},{2,3},{3,0},{4,5},{5,6},{6,7},{7,4},{8,9},{9,10},{10,1... | collective-permute-start | bytes 1572872 | tf_op jit(solution)/shard_map/ppermute | solution.py:101
  18.7 6.6 %collective-permute-done.2 = f32[32,2048]{1,0:T(8,128)} collective-permute-done((f32[32,2048]{1,0:T(8,128)S(1)}, f32[32,2048]{1,0:T(8,128)}, u32[]{:S(2)}, u32[]{:S(2)}) %collective-permute-start.2) | collective-permute-done | bytes 262176 | tf_op jit(solution)/shard_map/ppermute | solution.py:109
  25.3 0.1 add_select_fusion.1
  25.3 0.1 collective-permute-start.3
  25.4 1.5 %collective-permute-done.3 = f32[32,2048]{1,0:T(8,128)S(1)} collective-permute-done((f32[32,2048]{1,0:T(8,128)S(1)}, f32[32,2048]{1,0:T(8,128)S(1)}, u32[]{:S(2)}, u32[]{:S(2)}) %collective-permute-start.3) | collective-permute-done | bytes 262176 | tf_op jit(solution)/shard_map/ppermute | solution.py:114
  26.9 0.1 fusion.4.other
  27.0 0.7 pad_maximum_fusion
  27.7 1.5 %collective-permute-start.4 = (f32[2,16,2048]{2,1,0:T(8,128)}, f32[2,16,2048]{2,1,0:T(8,128)S(1)}, u32[]{:S(2)}, u32[]{:S(2)}) collective-permute-start(f32[2,16,2048]{2,1,0:T(8,128)} %pad_maximum_fusion), channel_id=1, source_target_pairs={{0,1},{1,2},{2,3},{3,0},{4,5},{5,6},{6,7},{7,4},{8,9},{9,10},{10,1... | collective-permute-start | bytes 786440 | tf_op jit(solution)/shard_map/ppermute | solution.py:118
  29.2 0.7 pad_maximum_fusion.1
  30.0 0.5 collective-permute-start.5
  30.5 0.1 pad_add_fusion.places
  30.6 1.2 %collective-permute-done.7.coef_after = f32[2,16,4096]{2,1,0:T(8,128)S(1)} collective-permute-done((f32[2,16,4096]{2,1,0:T(8,128)}, f32[2,16,4096]{2,1,0:T(8,128)S(1)}, u32[]{:S(2)}, u32[]{:S(2)}) %collective-permute-start.7) | collective-permute-done | bytes 524320 | tf_op jit(solution)/shard_map/ppermute | solution.py:102
  31.7 11.3 %collective-permute-done.6.coef_before = f32[2,16,4096]{2,1,0:T(8,128)S(1)} collective-permute-done((f32[2,16,4096]{2,1,0:T(8,128)}, f32[2,16,4096]{2,1,0:T(8,128)S(1)}, u32[]{:S(2)}, u32[]{:S(2)}) %collective-permute-start.6) | collective-permute-done | bytes 524320 | tf_op jit(solution)/shard_map/ppermute | solution.py:101
  43.0 5.6 %collective-permute-done.4.before = f32[2,16,2048]{2,1,0:T(8,128)S(1)} collective-permute-done((f32[2,16,2048]{2,1,0:T(8,128)}, f32[2,16,2048]{2,1,0:T(8,128)S(1)}, u32[]{:S(2)}, u32[]{:S(2)}) %collective-permute-start.4) | collective-permute-done | bytes 262176 | tf_op jit(solution)/shard_map/ppermute | solution.py:118
  48.6 3.6 %collective-permute-done.5.after = f32[2,16,2048]{2,1,0:T(8,128)S(1)} collective-permute-done((f32[2,16,2048]{2,1,0:T(8,128)}, f32[2,16,2048]{2,1,0:T(8,128)S(1)}, u32[]{:S(2)}, u32[]{:S(2)}) %collective-permute-start.5) | collective-permute-done | bytes 262176 | tf_op jit(solution)/shard_map/ppermute | solution.py:119
  52.2 0.0 copy-start.2
  52.2 0.7 copy-done.2
  52.9 9.6 %shard_map.68 = f32[32,4096]{1,0:T(8,128)} custom-call(s32[3]{0:T(128)S(1)} %pad_add_fusion.places, f32[32,2048]{1,0:T(8,128)S(1)} %get-tuple-element.5.own, f32[32,2048]{1,0:T(8,128)S(1)} %fusion.4.other, f32[2,16,2048]{2,1,0:T(8,128)S(1)} %collective-permute-done.4.before, f32[2,16,2048]{2,1,0:T(8,128)S(1)} %collective-permute-done.5.after, ...), custom_call_target="tpu_custom_call" | custom-call | tf_op jit(solution)/shard_map/pallas_call | solution.py:71
  62.5 1.9 %collective-permute-start.8 = (f32[32,4096]{1,0:T(8,128)}, f32[32,4096]{1,0:T(8,128)S(1)}, u32[]{:S(2)}, u32[]{:S(2)}) collective-permute-start(f32[32,4096]{1,0:T(8,128)} %shard_map.68), channel_id=1, source_target_pairs={{0,4},{4,8},{8,12},{12,16},{16,20},{20,24},{24,28},{1,5},{5,9},{9,... | collective-permute-start | bytes 1572872 | tf_op jit(solution)/shard_map/ppermute | solution.py:123
  64.4 8.8 %collective-permute-done.8 = f32[32,4096]{1,0:T(8,128)S(1)} collective-permute-done((f32[32,4096]{1,0:T(8,128)}, f32[32,4096]{1,0:T(8,128)S(1)}, u32[]{:S(2)}, u32[]{:S(2)}) %collective-permute-start.8) | collective-permute-done | bytes 524320 | tf_op jit(solution)/shard_map/ppermute | solution.py:123
  73.2 0.9 %fusion.1 = f32[1,32,4096]{2,1,0:T(8,128)} fusion(f32[32,4096]{1,0:T(8,128)S(1)} %collective-permute-done.8, f32[32,2048]{1,0:T(8,128)S(1)} %fusion.4.other, f32[32,2048]{1,0:T(8,128)S(1)} %get-tuple-element.5.own, pred[]{:T(512)S(6)} %eq.13), kind=kLoop, calls=%fused_computation.2 | loop fusion | flops 524288 | bytes 1572865 | tf_op jit(solution)/shard_map/broadcast_in_dim | solution.py:126
  (6 shorter events, 0.2 us)
Async XLA Ops:
  1.9 1.0 %copy-start = (f32[1,32,4096]{2,1,0:T(8,128)S(1)}, f32[1,32,4096]{2,1,0:T(8,128)}, u32[]{:S(2)}) copy-start(f32[1,32,4096]{2,1,0:T(8,128)} %param.7) | copy-start | bytes 1572868
  2.0 1.6 %collective-permute-start = (f32[32,2048]{1,0:T(8,128)S(1)}, f32[32,2048]{1,0:T(8,128)S(1)}, u32[]{:S(2)}, u32[]{:S(2)}) collective-permute-start(f32[32,2048]{1,0:T(8,128)S(1)} %slice_select_fusion), channel_id=1, source_target_pairs={{0,4},{4,0},{8,12},{12,8},{16,20},{20,16},{24,28},{28,24},{1,5},{5... | collective-permute-start | bytes 786440 | tf_op jit(solution)/shard_map/ppermute | solution.py:104
  3.0 1.1 %copy-start.1 = (f32[1,32,4096]{2,1,0:T(8,128)S(1)}, f32[1,32,4096]{2,1,0:T(8,128)}, u32[]{:S(2)}) copy-start(f32[1,32,4096]{2,1,0:T(8,128)} %param.8) | copy-start | bytes 1572868
  3.6 8.4 %collective-permute-start.1 = (f32[32,2048]{1,0:T(8,128)S(1)}, f32[32,2048]{1,0:T(8,128)S(1)}, u32[]{:S(2)}, u32[]{:S(2)}) collective-permute-start(f32[32,2048]{1,0:T(8,128)S(1)} %fusion.2), channel_id=1, source_target_pairs={{0,8},{4,12},{8,0},{12,4},{16,24},{20,28},{24,16},{28,20},{1,9},{5... | collective-permute-start | bytes 786440 | tf_op jit(solution)/shard_map/ppermute | solution.py:109
  12.1 13.2 %collective-permute-start.2 = (f32[32,2048]{1,0:T(8,128)S(1)}, f32[32,2048]{1,0:T(8,128)}, u32[]{:S(2)}, u32[]{:S(2)}) collective-permute-start(f32[32,2048]{1,0:T(8,128)S(1)} %add.35), channel_id=1, source_target_pairs={{0,16},{4,20},{8,24},{12,28},{16,0},{20,4},{24,8},{28,12},{1,17},{... | collective-permute-start | bytes 786440 | tf_op jit(solution)/shard_map/ppermute | solution.py:109
  15.8 16.0 %collective-permute-start.7 = (f32[2,16,4096]{2,1,0:T(8,128)}, f32[2,16,4096]{2,1,0:T(8,128)S(1)}, u32[]{:S(2)}, u32[]{:S(2)}) collective-permute-start(f32[2,16,4096]{2,1,0:T(8,128)} %get-tuple-element.2), channel_id=1, source_target_pairs={{1,0},{2,1},{3,2},{0,3},{5,4},{6,5},{7,6},{4,7},{9,8},{10,9},{11,1... | collective-permute-start | bytes 1572872 | tf_op jit(solution)/shard_map/ppermute | solution.py:102
  16.3 26.7 %collective-permute-start.6 = (f32[2,16,4096]{2,1,0:T(8,128)}, f32[2,16,4096]{2,1,0:T(8,128)S(1)}, u32[]{:S(2)}, u32[]{:S(2)}) collective-permute-start(f32[2,16,4096]{2,1,0:T(8,128)} %get-tuple-element.3), channel_id=1, source_target_pairs={{0,1},{1,2},{2,3},{3,0},{4,5},{5,6},{6,7},{7,4},{8,9},{9,10},{10,1... | collective-permute-start | bytes 1572872 | tf_op jit(solution)/shard_map/ppermute | solution.py:101
  25.3 1.6 %collective-permute-start.3 = (f32[32,2048]{1,0:T(8,128)S(1)}, f32[32,2048]{1,0:T(8,128)S(1)}, u32[]{:S(2)}, u32[]{:S(2)}) collective-permute-start(f32[32,2048]{1,0:T(8,128)S(1)} %get-tuple-element.4), channel_id=1, source_target_pairs={{0,4},{4,0},{8,12},{12,8},{16,20},{20,16},{24,28},{28,24},{1,5},{5... | collective-permute-start | bytes 786440 | tf_op jit(solution)/shard_map/ppermute | solution.py:114
  27.7 20.9 %collective-permute-start.4 = (f32[2,16,2048]{2,1,0:T(8,128)}, f32[2,16,2048]{2,1,0:T(8,128)S(1)}, u32[]{:S(2)}, u32[]{:S(2)}) collective-permute-start(f32[2,16,2048]{2,1,0:T(8,128)} %pad_maximum_fusion), channel_id=1, source_target_pairs={{0,1},{1,2},{2,3},{3,0},{4,5},{5,6},{6,7},{7,4},{8,9},{9,10},{10,1... | collective-permute-start | bytes 786440 | tf_op jit(solution)/shard_map/ppermute | solution.py:118
  30.0 22.2 %collective-permute-start.5 = (f32[2,16,2048]{2,1,0:T(8,128)}, f32[2,16,2048]{2,1,0:T(8,128)S(1)}, u32[]{:S(2)}, u32[]{:S(2)}) collective-permute-start(f32[2,16,2048]{2,1,0:T(8,128)} %pad_maximum_fusion.1), channel_id=1, source_target_pairs={{1,0},{2,1},{3,2},{0,3},{5,4},{6,5},{7,6},{4,7},{9,8},{10,9},{11,1... | collective-permute-start | bytes 786440 | tf_op jit(solution)/shard_map/ppermute | solution.py:119
  52.2 0.7 copy-start.2
  62.5 10.7 %collective-permute-start.8 = (f32[32,4096]{1,0:T(8,128)}, f32[32,4096]{1,0:T(8,128)S(1)}, u32[]{:S(2)}, u32[]{:S(2)}) collective-permute-start(f32[32,4096]{1,0:T(8,128)} %shard_map.68), channel_id=1, source_target_pairs={{0,4},{4,8},{8,12},{12,16},{16,20},{20,24},{24,28},{1,5},{5,9},{9,... | collective-permute-start | bytes 1572872 | tf_op jit(solution)/shard_map/ppermute | solution.py:123

commit v2 on v1

v2 whole, which is shorter than its diff:
```python
import functools

import jax
import jax.numpy as jnp
from jax import lax
from jax.experimental import pallas as pl
from jax.experimental.pallas import tpu as pltpu
from jax.sharding import PartitionSpec as P

LANES = 128
VMEM = pl.BlockSpec(memory_space=pltpu.VMEM)


def call(kernel, out_shapes, args, aliases=None, work=0):
    return pl.pallas_call(
        kernel,
        out_shape=tuple(pltpu.VMEM(shape, jnp.float32) for shape in out_shapes),
        in_specs=[VMEM] * len(args),
        out_specs=(VMEM,) * len(out_shapes),
        input_output_aliases=aliases or {},
        cost_estimate=pl.CostEstimate(flops=work, bytes_accessed=0, transcendentals=0),
        compiler_params=pltpu.CompilerParams(vmem_limit_bytes=4 * 2**20),
    )(*(pltpu.with_memory_space_constraint(v, pltpu.VMEM) for v in args))


def has_band_before():
    return lax.axis_index("lat") > 0


def has_band_after():
    return lax.axis_index("lat") < lax.axis_size("lat") - 1


def columns_of(tile):
    return slice(tile * LANES, (tile + 1) * LANES)


def advance_rows(steps, rows_of, old_and_new, c_all, d_all, paces):
    tiles = c_all.shape[0]
    for step in range(1, steps + 1):
        first, stop = rows_of(step)
        if first >= stop:
            continue
        old, new = old_and_new if step % 2 else old_and_new[::-1]
        pace = paces[step - 1 : step, :]
        lane = lax.broadcasted_iota(jnp.int32, (stop - first, LANES), 1)
        for t in range(tiles):
            x = old[t, first:stop, :]
            east = pltpu.roll(jnp.where(lane == 0, old[(t + 1) % tiles, first:stop, :], x), LANES - 1, 1)
            west = pltpu.roll(jnp.where(lane == LANES - 1, old[(t - 1) % tiles, first:stop, :], x), 1, 1)
            ahead = old[t, first + 1 : stop + 1, :] - x
            behind = x - old[t, first - 1 : stop - 1, :]
            c = c_all[t, first:stop, :]
            d = d_all[t, first:stop, :]
            spread = ((east - x) + (west - x)) + (ahead - behind)
            new[t, first:stop, :] = x + (d * pace) * spread - c * jnp.where(c > 0, behind, ahead)


def coefficients_kernel(steps, courant, diffusion, *rest):
    outer, (c_all, d_all) = rest[:4], rest[4:]
    rows, tiles = courant.shape[0], c_all.shape[0]
    has_before, has_after = has_band_before(), has_band_after()
    for t in range(tiles):
        for field, south, north, whole in ((courant, *outer[:2], c_all), (diffusion, *outer[2:], d_all)):
            whole[t, steps : steps + rows, :] = field[:, columns_of(t)]
            whole[t, :steps, :] = jnp.where(has_before, south[:, columns_of(t)], 0.0)
            whole[t, steps + rows :, :] = jnp.where(has_after, north[:, columns_of(t)], 0.0)


def place_halves(own, other, rows, whole):
    half = whole.shape[0] // 2
    for t in range(half):
        for which, source in ((0, own), (1, other)):
            to = t + half * jnp.where(lax.axis_index("tm") % 2 == which, 0, 1)
            whole[to, rows, :] = source(columns_of(t))


def inner_kernel(steps, paces, own, other, c_all, d_all, even, odd):
    rows = own.shape[0]
    place_halves(lambda cols: own[:, cols], lambda cols: other[:, cols], slice(steps, steps + rows), even)
    advance_rows(steps, lambda n: (steps + n, steps + rows - n), (even, odd), c_all, d_all, paces)


def south_kernel(steps, paces, halo, c_all, d_all, even_in, odd_in, even, odd, outer, final):
    del even_in, odd_in
    exists = has_band_before()
    place_halves(lambda cols: jnp.where(exists, halo[:steps, cols], 0.0),
                 lambda cols: jnp.where(exists, halo[steps:, cols], 0.0), slice(0, steps), even)
    advance_rows(steps, lambda n: (n, steps + n), (even, odd), c_all, d_all, paces)
    last = odd if steps % 2 else even
    for t in range(last.shape[0]):
        outer[:, columns_of(t)] = last[t, steps : 2 * steps, :]
        final[:steps, columns_of(t)] = last[t, steps : 2 * steps, :]


def north_kernel(steps, paces, halo, c_all, d_all, even_in, odd_in, final_in, even, odd, outer, final):
    del even_in, odd_in, final_in
    exists = has_band_after()
    rows = final.shape[0]
    place_halves(lambda cols: jnp.where(exists, halo[:steps, cols], 0.0),
                 lambda cols: jnp.where(exists, halo[steps:, cols], 0.0), slice(steps + rows, 2 * steps + rows), even)
    advance_rows(steps, lambda n: (steps + rows - n, 2 * steps + rows - n), (even, odd), c_all, d_all, paces)
    last = odd if steps % 2 else even
    for t in range(last.shape[0]):
        outer[:, columns_of(t)] = last[t, rows : steps + rows, :]
        final[steps:, columns_of(t)] = last[t, rows : steps + rows, :]


def on_device(control, scales, courant, diffusion, pacing):
    control, scales, courant, diffusion = (v[0] for v in (control, scales, courant, diffusion))
    steps = pacing.shape[1]
    rows, columns = control.shape
    half, tiles = columns // 2, columns // LANES
    windows, bands = lax.axis_size("tm"), lax.axis_size("lat")
    window = lax.axis_index("tm")
    is_first, chip = window % 2 == 0, window // 2
    onward = [(i, (i + 1) % bands) for i in range(bands)]
    backward = [(j, i) for i, j in onward]
    partner = [(i, i ^ 1) for i in range(windows)]
    following = [(i, i + 1) for i in range(windows - 1)]
    paces = jnp.broadcast_to(pacing.reshape(steps, 1), (steps, LANES))

    increment = scales * control
    left, right = increment[:, :half], increment[:, half:]
    own = jnp.where(is_first, left, right)
    other = jnp.where(is_first, right, left)

    outer = [
        lax.ppermute(part, "lat", way)
        for v in (courant, diffusion)
        for part, way in ((v[rows - steps :], onward), (v[:steps], backward))
    ]

    pair = own + lax.ppermute(other, "tm", partner)
    total, before = pair, jnp.zeros_like(pair)
    distance = 1
    while 2 * distance < windows:
        swap = [(i, i ^ (2 * distance)) for i in range(windows)]
        arrived = lax.ppermute(total, "tm", swap)
        before = before + jnp.where((chip // distance) % 2 == 1, arrived, 0.0)
        total = total + arrived
        distance *= 2
    before, outer = lax.optimization_barrier((before, outer))
    through_first = before + own
    arrived = lax.ppermute(jnp.where(is_first, through_first, before), "tm", partner)
    start_own = jnp.where(is_first, through_first, before + pair)
    start_other = arrived + other

    south = lax.ppermute(jnp.concatenate([start_own[rows - steps :], start_other[rows - steps :]]), "lat", onward)
    north = lax.ppermute(jnp.concatenate([start_own[:steps], start_other[:steps]]), "lat", backward)

    field = (tiles, rows + 2 * steps, LANES)
    part, band_shape = (steps, columns), (rows, columns)
    c_all, d_all = call(functools.partial(coefficients_kernel, steps), [field] * 2,
                        (courant, diffusion, *outer))
    work = 16 * steps * steps * columns
    even, odd = call(functools.partial(inner_kernel, steps), [field] * 2,
                     (paces, start_own, start_other, c_all, d_all), work=work)
    even, odd, final_south, final = call(
        functools.partial(south_kernel, steps), [field, field, part, band_shape],
        (paces, south, c_all, d_all, even, odd), {4: 0, 5: 1}, work=work)
    previous_south = lax.ppermute(final_south, "tm", following)
    _, _, final_north, final = call(
        functools.partial(north_kernel, steps), [field, field, part, band_shape],
        (paces, north, c_all, d_all, even, odd, final), {4: 0, 5: 1, 6: 3}, work=work)
    previous_north = lax.ppermute(final_north, "tm", following)
    start = jnp.where(is_first, jnp.concatenate([start_own, start_other], axis=1),
                      jnp.concatenate([start_other, start_own], axis=1))
    return (start - jnp.concatenate([previous_south, previous_north]))[None], final[None]


def solution(mesh):
    whole = P("tm", "lat", None)
    return jax.shard_map(
        on_device,
        mesh=mesh,
        in_specs=(whole, whole, whole, whole, P("tm", None)),
        out_specs=(whole, whole),
        check_vma=False,
    )
```

time: 74.3 us -> 62.2 us (0.84)
  the two profiles are of different devices: /device:TPU:10 before, /device:TPU:16 now
where the time goes in v2:
time: 62.2 us; the launch traced here: 62 us
  waiting for transfers between devices  28.6 us (46%)
  starting transfers between devices  14.5 us (23%)
  Pallas kernels  11.5 us (18%)
  other arithmetic  3.39 us (5%)
  local copies, waits for them, and re-layouts  3.22 us (5%)
  between operations  0.8 us (1%)
    pallas_call x4, Pallas kernels, call(): pl.pallas_call(kernel, out_shape=tuple((pltpu.VMEM(shape, jnp.float32) fo...  11.5 us
    ppermute x2, waiting for transfers between devices, on_device(): arrived = lax.ppermute(total, 'tm', swap)  11 us
    ppermute x4, waiting for transfers between devices, on_device(): lax.ppermute(part, 'lat', way)  7.9 us
    ppermute x4, starting transfers between devices, on_device(): lax.ppermute(part, 'lat', way)  5.06 us
    ppermute x1, waiting for transfers between devices, on_device(): previous_north = lax.ppermute(final_north, 'tm', following)  4.42 us
    ppermute x1, starting transfers between devices, on_device(): previous_north = lax.ppermute(final_north, 'tm', following)  2.46 us
    ppermute x1, waiting for transfers between devices, on_device(): lax.ppermute(jnp.concatenate([start_own[rows - steps:], start_other[rows...  2.22 us
    ppermute x1, starting transfers between devices, on_device(): previous_south = lax.ppermute(final_south, 'tm', following)  1.92 us
  transfers between devices with their start and end apart: 12, of which 8 were waited for; matrix products, arithmetic and copies ran while one was open for 6% of the time, Pallas kernels for 19%

profile of v2, /device:TPU:16, one launch (start us, length us, event | category | flops | bytes accessed | tf_op | source)
XLA Modules:
  0.0 62.0 jit_solution(7171691571118169257)
XLA Ops:
  0.6 1.3 %multiply_bitcast_fusion = f32[32,4096]{1,0:T(8,128)S(1)} fusion(f32[1,32,4096]{2,1,0:T(8,128)} %param.6, f32[1,32,4096]{2,1,0:T(8,128)} %param.5), kind=kLoop, calls=%fused_computation.2 | loop fusion | flops 131072 | bytes 1572864 | tf_op jit(solution)/shard_map/mul | solution.py:123
  1.9 0.0 copy-start
  2.0 0.1 collective-permute-start
  2.0 1.5 %collective-permute-done = f32[32,2048]{1,0:T(8,128)S(1)} collective-permute-done((f32[32,2048]{1,0:T(8,128)S(1)}, f32[32,2048]{1,0:T(8,128)S(1)}, u32[]{:S(2)}, u32[]{:S(2)}) %collective-permute-start) | collective-permute-done | bytes 262176 | tf_op jit(solution)/shard_map/ppermute | solution.py:134
  3.6 1.6 %collective-permute-start.1 = (f32[32,2048]{1,0:T(8,128)S(1)}, f32[32,2048]{1,0:T(8,128)S(1)}, u32[]{:S(2)}, u32[]{:S(2)}) collective-permute-start(f32[32,2048]{1,0:T(8,128)S(1)} %fusion.1), channel_id=1, source_target_pairs={{0,8},{4,12},{8,0},{12,4},{16,24},{20,28},{24,16},{28,20},{1,9},{5... | collective-permute-start | bytes 786440 | tf_op jit(solution)/shard_map/ppermute | solution.py:139
  5.2 0.0 copy-done
  5.2 0.8 %slice_bitcast_fusion.2 = (f32[16,4096]{1,0:T(8,128)}, f32[16,4096]{1,0:T(8,128)}) fusion(f32[1,32,4096]{2,1,0:T(8,128)S(1)} %copy-done), kind=kLoop, calls=%fused_computation.8 | loop fusion | bytes 1048576 | tf_op jit(solution)/shard_map/slice | solution.py:131
  6.1 0.0 copy-start.1
  6.1 2.4 %collective-permute-start.4 = (f32[16,4096]{1,0:T(8,128)}, f32[16,4096]{1,0:T(8,128)S(1)}, u32[]{:S(2)}, u32[]{:S(2)}) collective-permute-start(f32[16,4096]{1,0:T(8,128)} %get-tuple-element.36), channel_id=1, source_target_pairs={{1,0},{2,1},{3,2},{0,3},{5,4},{6,5},{7,6},{4,7},{9,8},{10,9},{11,1... | collective-permute-start | bytes 786440 | tf_op jit(solution)/shard_map/ppermute | solution.py:129
  8.5 0.0 collective-permute-start.3
  8.5 3.5 %collective-permute-done.1 = f32[32,2048]{1,0:T(8,128)S(1)} collective-permute-done((f32[32,2048]{1,0:T(8,128)S(1)}, f32[32,2048]{1,0:T(8,128)S(1)}, u32[]{:S(2)}, u32[]{:S(2)}) %collective-permute-start.1) | collective-permute-done | bytes 262176 | tf_op jit(solution)/shard_map/ppermute | solution.py:139
  12.0 0.2 collective-permute-start.2
  12.3 0.0 copy-done.1
  12.3 0.8 %slice_bitcast_fusion = (f32[16,4096]{1,0:T(8,128)}, f32[16,4096]{1,0:T(8,128)}) fusion(f32[1,32,4096]{2,1,0:T(8,128)S(1)} %copy-done.1), kind=kLoop, calls=%fused_computation.6 | loop fusion | bytes 1048576 | tf_op jit(solution)/shard_map/slice | solution.py:131
  13.1 2.6 %collective-permute-start.6 = (f32[16,4096]{1,0:T(8,128)}, f32[16,4096]{1,0:T(8,128)S(1)}, u32[]{:S(2)}, u32[]{:S(2)}) collective-permute-start(f32[16,4096]{1,0:T(8,128)} %get-tuple-element.34), channel_id=1, source_target_pairs={{1,0},{2,1},{3,2},{0,3},{5,4},{6,5},{7,6},{4,7},{9,8},{10,9},{11,1... | collective-permute-start | bytes 786440 | tf_op jit(solution)/shard_map/ppermute | solution.py:129
  15.7 0.0 collective-permute-start.5
  15.7 7.5 %collective-permute-done.2 = f32[32,2048]{1,0:T(8,128)} collective-permute-done((f32[32,2048]{1,0:T(8,128)S(1)}, f32[32,2048]{1,0:T(8,128)}, u32[]{:S(2)}, u32[]{:S(2)}) %collective-permute-start.2) | collective-permute-done | bytes 262176 | tf_op jit(solution)/shard_map/ppermute | solution.py:139
  23.3 1.0 %select_add_fusion = f32[32,2048]{1,0:T(8,128)S(1)} fusion(f32[32,2048]{1,0:T(8,128)} %collective-permute-done.2, f32[32,2048]{1,0:T(8,128)S(1)} %collective-permute-done.1, pred[]{:T(512)S(6)} %eq.15, pred[]{:T(512)S(6)} %eq.14), kind=kLoop, calls=%fused_computation.10 | loop fusion | flops 196608 | bytes 786434 | tf_op jit(solution)/shard_map/add | solution.py:140
  24.2 0.0 collective-permute-done.4.rest_1_
  24.3 0.0 collective-permute-done.3.rest_0_
  24.3 2.5 %collective-permute-done.6.rest_3_ = f32[16,4096]{1,0:T(8,128)S(1)} collective-permute-done((f32[16,4096]{1,0:T(8,128)}, f32[16,4096]{1,0:T(8,128)S(1)}, u32[]{:S(2)}, u32[]{:S(2)}) %collective-permute-start.6) | collective-permute-done | bytes 262176 | tf_op jit(solution)/shard_map/ppermute | solution.py:129
  26.8 5.4 %collective-permute-done.5.rest_2_ = f32[16,4096]{1,0:T(8,128)S(1)} collective-permute-done((f32[16,4096]{1,0:T(8,128)}, f32[16,4096]{1,0:T(8,128)S(1)}, u32[]{:S(2)}, u32[]{:S(2)}) %collective-permute-start.5) | collective-permute-done | bytes 262176 | tf_op jit(solution)/shard_map/ppermute | solution.py:129
  32.2 0.1 add_select_fusion
  32.2 0.1 collective-permute-start.7
  32.3 1.5 %collective-permute-done.7 = f32[32,2048]{1,0:T(8,128)S(1)} collective-permute-done((f32[32,2048]{1,0:T(8,128)S(1)}, f32[32,2048]{1,0:T(8,128)S(1)}, u32[]{:S(2)}, u32[]{:S(2)}) %collective-permute-start.7) | collective-permute-done | bytes 262176 | tf_op jit(solution)/shard_map/ppermute | solution.py:145
  33.8 0.1 fusion.4.other
  34.0 1.5 %collective-permute-start.8 = (f32[32,2048]{1,0:T(8,128)S(1)}, f32[32,2048]{1,0:T(8,128)S(1)}, u32[]{:S(2)}, u32[]{:S(2)}) collective-permute-start(f32[32,2048]{1,0:T(8,128)S(1)} %pad_maximum_fusion), channel_id=1, source_target_pairs={{0,1},{1,2},{2,3},{3,0},{4,5},{5,6},{6,7},{7,4},{8,9},{9,10},{10,1... | collective-permute-start | bytes 786440 | tf_op jit(solution)/shard_map/ppermute | solution.py:149
  35.5 1.5 %collective-permute-start.10 = (f32[32,2048]{1,0:T(8,128)S(1)}, f32[32,2048]{1,0:T(8,128)S(1)}, u32[]{:S(2)}, u32[]{:S(2)}) collective-permute-start(f32[32,2048]{1,0:T(8,128)S(1)} %pad_maximum_fusion.1), channel_id=1, source_target_pairs={{1,0},{2,1},{3,2},{0,3},{5,4},{6,5},{7,6},{4,7},{9,8},{10,9},{11,1... | collective-permute-start | bytes 786440 | tf_op jit(solution)/shard_map/ppermute | solution.py:150
  37.0 0.2 shard_map.68
  37.2 0.0 copy-start.2
  37.2 0.6 %copy-done.2 = f32[1,16]{1,0:T(1,128)S(1)} copy-done((f32[1,16]{1,0:T(1,128)S(1)}, f32[1,16]{1,0:T(1,128)}, u32[]{:S(2)}) %copy-start.2) | copy-done | bytes 88
  37.8 0.1 broadcast_in_dim.18.paces
  37.9 3.9 %shard_map.69 = (f32[32,64,128]{2,1,0:T(8,128)S(1)}, f32[32,64,128]{2,1,0:T(8,128)S(1)}) custom-call(f32[16,128]{1,0:T(8,128)S(1)} %broadcast_in_dim.18.paces, f32[32,2048]{1,0:T(8,128)S(1)} %get-tuple-element.32.own, f32[32,2048]{1,0:T(8,128)S(1)} %fusion.4.other, f32[32,64,128]{2,1,0:T(8,128)S(1)} %get-tuple-element.22.c_all, ...), custom_call_target="tpu_custom_call" | custom-call | flops 16777216 | tf_op jit(solution)/shard_map/pallas_call | solution.py:15
  41.8 2.2 %collective-permute-done.8.halo = f32[32,2048]{1,0:T(8,128)S(1)} collective-permute-done((f32[32,2048]{1,0:T(8,128)S(1)}, f32[32,2048]{1,0:T(8,128)S(1)}, u32[]{:S(2)}, u32[]{:S(2)}) %collective-permute-start.8) | collective-permute-done | bytes 262176 | tf_op jit(solution)/shard_map/ppermute | solution.py:149
  44.1 3.7 %shard_map.70 = (f32[32,64,128]{2,1,0:T(8,128)S(1)}, f32[32,64,128]{2,1,0:T(8,128)S(1)}, f32[16,4096]{1,0:T(8,128)S(1)}, f32[32,4096]{1,0:T(8,128)S(1)}) custom-call(f32[16,128]{1,0:T(8,128)S(1)} %broadcast_in_dim.18.paces, f32[32,2048]{1,0:T(8,128)S(1)} %collective-permute-done.8.halo, ...), custom_call_target="tpu_custom_call", output_to_operand_aliasing={{0}: (4, {}), {1}: (5, {})} | custom-call | flops 16777216 | tf_op jit(solution)/shard_map/pallas_call | solution.py:15
  47.7 1.9 %collective-permute-start.9 = (f32[16,4096]{1,0:T(8,128)S(1)}, f32[16,4096]{1,0:T(8,128)S(1)}, u32[]{:S(2)}, u32[]{:S(2)}) collective-permute-start(f32[16,4096]{1,0:T(8,128)S(1)} %get-tuple-element.26), channel_id=1, source_target_pairs={{0,4},{4,8},{8,12},{12,16},{16,20},{20,24},{24,28},{1,5},{5,9},{9,... | collective-permute-start | bytes 786440 | tf_op jit(solution)/shard_map/ppermute | solution.py:162
  49.7 0.0 collective-permute-done.10.halo
  49.7 3.8 %shard_map.71 = (f32[32,64,128]{2,1,0:T(8,128)S(1)}, f32[32,64,128]{2,1,0:T(8,128)S(1)}, f32[16,4096]{1,0:T(8,128)S(1)}, f32[32,4096]{1,0:T(8,128)S(1)}) custom-call(f32[16,128]{1,0:T(8,128)S(1)} %broadcast_in_dim.18.paces, f32[32,2048]{1,0:T(8,128)S(1)} %collective-permute-done.10.halo, ...), custom_call_target="tpu_custom_call", output_to_operand_aliasing={{0}: (4, {}), {1}: (5, {}), {3}: (6, {})} | custom-call | flops 16777216 | tf_op jit(solution)/shard_map/pallas_call | solution.py:15
  53.4 2.5 %collective-permute-start.11 = (f32[16,4096]{1,0:T(8,128)S(1)}, f32[16,4096]{1,0:T(8,128)S(1)}, u32[]{:S(2)}, u32[]{:S(2)}) collective-permute-start(f32[16,4096]{1,0:T(8,128)S(1)} %get-tuple-element.30), channel_id=1, source_target_pairs={{0,4},{4,8},{8,12},{12,16},{16,20},{20,24},{24,28},{1,5},{5,9},{9,... | collective-permute-start | bytes 786440 | tf_op jit(solution)/shard_map/ppermute | solution.py:166
  55.9 0.8 %copy.17 = f32[1,32,4096]{2,1,0:T(8,128)} copy(f32[1,32,4096]{2,1,0:T(8,128)S(1)} %bitcast.18) | data formatting | bytes 1048576
  56.7 0.0 collective-permute-done.9
  56.7 4.4 %collective-permute-done.11 = f32[16,4096]{1,0:T(8,128)S(1)} collective-permute-done((f32[16,4096]{1,0:T(8,128)S(1)}, f32[16,4096]{1,0:T(8,128)S(1)}, u32[]{:S(2)}, u32[]{:S(2)}) %collective-permute-start.11) | collective-permute-done | bytes 262176 | tf_op jit(solution)/shard_map/ppermute | solution.py:166
  61.1 0.9 %fusion = f32[1,32,4096]{2,1,0:T(8,128)} fusion(f32[1,32,2048]{2,1,0:T(8,128)S(1)} %bitcast.20, f32[1,32,2048]{2,1,0:T(8,128)S(1)} %bitcast.19, f32[1,16,4096]{2,1,0:T(8,128)S(1)} %bitcast.24, f32[1,16,4096]{2,1,0:T(8,128)S(1)} %bitcast.23, pred[]{:T(512)S(6)} %eq.13), kind=kLoop, calls=%fused_computation.1 | loop fusion | flops 655360 | bytes 1572865 | tf_op jit(solution)/shard_map/sub | solution.py:169
  (7 shorter events, 0.2 us)
Async XLA Ops:
  1.9 3.3 %copy-start = (f32[1,32,4096]{2,1,0:T(8,128)S(1)}, f32[1,32,4096]{2,1,0:T(8,128)}, u32[]{:S(2)}) copy-start(f32[1,32,4096]{2,1,0:T(8,128)} %param.7) | copy-start | bytes 1572868
  2.0 1.6 %collective-permute-start = (f32[32,2048]{1,0:T(8,128)S(1)}, f32[32,2048]{1,0:T(8,128)S(1)}, u32[]{:S(2)}, u32[]{:S(2)}) collective-permute-start(f32[32,2048]{1,0:T(8,128)S(1)} %slice_select_fusion), channel_id=1, source_target_pairs={{0,4},{4,0},{8,12},{12,8},{16,20},{20,16},{24,28},{28,24},{1,5},{5... | collective-permute-start | bytes 786440 | tf_op jit(solution)/shard_map/ppermute | solution.py:134
  3.6 8.4 %collective-permute-start.1 = (f32[32,2048]{1,0:T(8,128)S(1)}, f32[32,2048]{1,0:T(8,128)S(1)}, u32[]{:S(2)}, u32[]{:S(2)}) collective-permute-start(f32[32,2048]{1,0:T(8,128)S(1)} %fusion.1), channel_id=1, source_target_pairs={{0,8},{4,12},{8,0},{12,4},{16,24},{20,28},{24,16},{28,20},{1,9},{5... | collective-permute-start | bytes 786440 | tf_op jit(solution)/shard_map/ppermute | solution.py:139
  6.1 6.2 %copy-start.1 = (f32[1,32,4096]{2,1,0:T(8,128)S(1)}, f32[1,32,4096]{2,1,0:T(8,128)}, u32[]{:S(2)}) copy-start(f32[1,32,4096]{2,1,0:T(8,128)} %param.8) | copy-start | bytes 1572868
  6.1 18.2 %collective-permute-start.4 = (f32[16,4096]{1,0:T(8,128)}, f32[16,4096]{1,0:T(8,128)S(1)}, u32[]{:S(2)}, u32[]{:S(2)}) collective-permute-start(f32[16,4096]{1,0:T(8,128)} %get-tuple-element.36), channel_id=1, source_target_pairs={{1,0},{2,1},{3,2},{0,3},{5,4},{6,5},{7,6},{4,7},{9,8},{10,9},{11,1... | collective-permute-start | bytes 786440 | tf_op jit(solution)/shard_map/ppermute | solution.py:129
  8.5 15.7 %collective-permute-start.3 = (f32[16,4096]{1,0:T(8,128)}, f32[16,4096]{1,0:T(8,128)S(1)}, u32[]{:S(2)}, u32[]{:S(2)}) collective-permute-start(f32[16,4096]{1,0:T(8,128)} %get-tuple-element.37), channel_id=1, source_target_pairs={{0,1},{1,2},{2,3},{3,0},{4,5},{5,6},{6,7},{7,4},{8,9},{9,10},{10,1... | collective-permute-start | bytes 786440 | tf_op jit(solution)/shard_map/ppermute | solution.py:129
  12.0 11.2 %collective-permute-start.2 = (f32[32,2048]{1,0:T(8,128)S(1)}, f32[32,2048]{1,0:T(8,128)}, u32[]{:S(2)}, u32[]{:S(2)}) collective-permute-start(f32[32,2048]{1,0:T(8,128)S(1)} %add.35), channel_id=1, source_target_pairs={{0,16},{4,20},{8,24},{12,28},{16,0},{20,4},{24,8},{28,12},{1,17},{... | collective-permute-start | bytes 786440 | tf_op jit(solution)/shard_map/ppermute | solution.py:139
  13.1 13.7 %collective-permute-start.6 = (f32[16,4096]{1,0:T(8,128)}, f32[16,4096]{1,0:T(8,128)S(1)}, u32[]{:S(2)}, u32[]{:S(2)}) collective-permute-start(f32[16,4096]{1,0:T(8,128)} %get-tuple-element.34), channel_id=1, source_target_pairs={{1,0},{2,1},{3,2},{0,3},{5,4},{6,5},{7,6},{4,7},{9,8},{10,9},{11,1... | collective-permute-start | bytes 786440 | tf_op jit(solution)/shard_map/ppermute | solution.py:129
  15.7 16.4 %collective-permute-start.5 = (f32[16,4096]{1,0:T(8,128)}, f32[16,4096]{1,0:T(8,128)S(1)}, u32[]{:S(2)}, u32[]{:S(2)}) collective-permute-start(f32[16,4096]{1,0:T(8,128)} %get-tuple-element.35), channel_id=1, source_target_pairs={{0,1},{1,2},{2,3},{3,0},{4,5},{5,6},{6,7},{7,4},{8,9},{9,10},{10,1... | collective-permute-start | bytes 786440 | tf_op jit(solution)/shard_map/ppermute | solution.py:129
  32.2 1.6 %collective-permute-start.7 = (f32[32,2048]{1,0:T(8,128)S(1)}, f32[32,2048]{1,0:T(8,128)S(1)}, u32[]{:S(2)}, u32[]{:S(2)}) collective-permute-start(f32[32,2048]{1,0:T(8,128)S(1)} %get-tuple-element.33), channel_id=1, source_target_pairs={{0,4},{4,0},{8,12},{12,8},{16,20},{20,16},{24,28},{28,24},{1,5},{5... | collective-permute-start | bytes 786440 | tf_op jit(solution)/shard_map/ppermute | solution.py:145
  34.0 10.1 %collective-permute-start.8 = (f32[32,2048]{1,0:T(8,128)S(1)}, f32[32,2048]{1,0:T(8,128)S(1)}, u32[]{:S(2)}, u32[]{:S(2)}) collective-permute-start(f32[32,2048]{1,0:T(8,128)S(1)} %pad_maximum_fusion), channel_id=1, source_target_pairs={{0,1},{1,2},{2,3},{3,0},{4,5},{5,6},{6,7},{7,4},{8,9},{9,10},{10,1... | collective-permute-start | bytes 786440 | tf_op jit(solution)/shard_map/ppermute | solution.py:149
  35.5 14.2 %collective-permute-start.10 = (f32[32,2048]{1,0:T(8,128)S(1)}, f32[32,2048]{1,0:T(8,128)S(1)}, u32[]{:S(2)}, u32[]{:S(2)}) collective-permute-start(f32[32,2048]{1,0:T(8,128)S(1)} %pad_maximum_fusion.1), channel_id=1, source_target_pairs={{1,0},{2,1},{3,2},{0,3},{5,4},{6,5},{7,6},{4,7},{9,8},{10,9},{11,1... | collective-permute-start | bytes 786440 | tf_op jit(solution)/shard_map/ppermute | solution.py:150
  37.2 0.7 %copy-start.2 = (f32[1,16]{1,0:T(1,128)S(1)}, f32[1,16]{1,0:T(1,128)}, u32[]{:S(2)}) copy-start(f32[1,16]{1,0:T(1,128)} %param.9) | copy-start | bytes 196
  47.7 9.0 %collective-permute-start.9 = (f32[16,4096]{1,0:T(8,128)S(1)}, f32[16,4096]{1,0:T(8,128)S(1)}, u32[]{:S(2)}, u32[]{:S(2)}) collective-permute-start(f32[16,4096]{1,0:T(8,128)S(1)} %get-tuple-element.26), channel_id=1, source_target_pairs={{0,4},{4,8},{8,12},{12,16},{16,20},{20,24},{24,28},{1,5},{5,9},{9,... | collective-permute-start | bytes 786440 | tf_op jit(solution)/shard_map/ppermute | solution.py:162
  53.4 7.7 %collective-permute-start.11 = (f32[16,4096]{1,0:T(8,128)S(1)}, f32[16,4096]{1,0:T(8,128)S(1)}, u32[]{:S(2)}, u32[]{:S(2)}) collective-permute-start(f32[16,4096]{1,0:T(8,128)S(1)} %get-tuple-element.30), channel_id=1, source_target_pairs={{0,4},{4,8},{8,12},{12,16},{16,20},{20,24},{24,28},{1,5},{5,9},{9,... | collective-permute-start | bytes 786440 | tf_op jit(solution)/shard_map/ppermute | solution.py:166

commit v3 on v2

v3 whole, which is shorter than its diff:
```python
import functools

import jax
import jax.numpy as jnp
from jax import lax
from jax.experimental import pallas as pl
from jax.experimental.pallas import tpu as pltpu
from jax.sharding import PartitionSpec as P

LANES = 128
MOVED = 64 * 2**20
VMEM = pl.BlockSpec(memory_space=pltpu.VMEM)


def call(kernel, out_shapes, args, aliases=None, work=0, moved=0):
    return pl.pallas_call(
        kernel,
        out_shape=tuple(pltpu.VMEM(shape, jnp.float32) for shape in out_shapes),
        in_specs=[VMEM] * len(args),
        out_specs=(VMEM,) * len(out_shapes),
        input_output_aliases=aliases or {},
        cost_estimate=pl.CostEstimate(flops=work, bytes_accessed=moved, transcendentals=0),
        compiler_params=pltpu.CompilerParams(vmem_limit_bytes=4 * 2**20),
    )(*(pltpu.with_memory_space_constraint(v, pltpu.VMEM) for v in args))


def has_band_before():
    return lax.axis_index("lat") > 0


def has_band_after():
    return lax.axis_index("lat") < lax.axis_size("lat") - 1


def columns_of(tile):
    return slice(tile * LANES, (tile + 1) * LANES)


def advance_rows(steps, rows_of, old_and_new, c_all, d_all, paces):
    tiles = c_all.shape[0]
    for step in range(1, steps + 1):
        first, stop = rows_of(step)
        if first >= stop:
            continue
        old, new = old_and_new if step % 2 else old_and_new[::-1]
        pace = paces[step - 1 : step, :]
        lane = lax.broadcasted_iota(jnp.int32, (stop - first, LANES), 1)
        for t in range(tiles):
            x = old[t, first:stop, :]
            east = pltpu.roll(jnp.where(lane == 0, old[(t + 1) % tiles, first:stop, :], x), LANES - 1, 1)
            west = pltpu.roll(jnp.where(lane == LANES - 1, old[(t - 1) % tiles, first:stop, :], x), 1, 1)
            ahead = old[t, first + 1 : stop + 1, :] - x
            behind = x - old[t, first - 1 : stop - 1, :]
            c = c_all[t, first:stop, :]
            d = d_all[t, first:stop, :]
            spread = ((east - x) + (west - x)) + (ahead - behind)
            new[t, first:stop, :] = x + (d * pace) * spread - c * jnp.where(c > 0, behind, ahead)


def pack_kernel(steps, courant, diffusion, onward, backward):
    rows = courant.shape[0]
    for at, field in ((0, courant), (steps, diffusion)):
        onward[at : at + steps, :] = field[rows - steps :, :]
        backward[at : at + steps, :] = field[:steps, :]


def coefficients_kernel(steps, courant, diffusion, south, north, c_all, d_all):
    rows, tiles = courant.shape[0], c_all.shape[0]
    has_before, has_after = has_band_before(), has_band_after()
    for t in range(tiles):
        for at, field, whole in ((0, courant, c_all), (steps, diffusion, d_all)):
            whole[t, steps : steps + rows, :] = field[:, columns_of(t)]
            whole[t, :steps, :] = jnp.where(has_before, south[at : at + steps, columns_of(t)], 0.0)
            whole[t, steps + rows :, :] = jnp.where(has_after, north[at : at + steps, columns_of(t)], 0.0)


def place_halves(own, other, rows, whole):
    half = whole.shape[0] // 2
    for t in range(half):
        for which, source in ((0, own), (1, other)):
            to = t + half * jnp.where(lax.axis_index("tm") % 2 == which, 0, 1)
            whole[to, rows, :] = source(columns_of(t))


def inner_kernel(steps, paces, own, other, c_all, d_all, even, odd):
    rows = own.shape[0]
    place_halves(lambda cols: own[:, cols], lambda cols: other[:, cols], slice(steps, steps + rows), even)
    advance_rows(steps, lambda n: (steps + n, steps + rows - n), (even, odd), c_all, d_all, paces)


def south_kernel(steps, paces, halo, c_all, d_all, even_in, odd_in, even, odd, part):
    del even_in, odd_in
    exists = has_band_before()
    place_halves(lambda cols: jnp.where(exists, halo[:steps, cols], 0.0),
                 lambda cols: jnp.where(exists, halo[steps:, cols], 0.0), slice(0, steps), even)
    advance_rows(steps, lambda n: (n, steps + n), (even, odd), c_all, d_all, paces)
    last = odd if steps % 2 else even
    for t in range(last.shape[0]):
        part[:, columns_of(t)] = last[t, steps : 2 * steps, :]


def north_kernel(steps, paces, halo, c_all, d_all, even_in, odd_in, even, odd, part):
    del even_in, odd_in
    exists = has_band_after()
    rows = c_all.shape[1] - 2 * steps
    place_halves(lambda cols: jnp.where(exists, halo[:steps, cols], 0.0),
                 lambda cols: jnp.where(exists, halo[steps:, cols], 0.0), slice(steps + rows, 2 * steps + rows), even)
    advance_rows(steps, lambda n: (steps + rows - n, 2 * steps + rows - n), (even, odd), c_all, d_all, paces)
    last = odd if steps % 2 else even
    for t in range(last.shape[0]):
        part[:, columns_of(t)] = last[t, 2 * steps : steps + rows, :]


def results_kernel(at, previous, own, other, final_part, *refs):
    defect, final, difference, sems = refs[-4:]
    count, half = previous.shape[0], own.shape[1]
    here = pl.ds(at, count)
    kept = pltpu.make_async_copy(final_part, final.at[here], sems.at[0])
    kept.start()
    is_first = lax.axis_index("tm") % 2 == 0
    follows = lax.axis_index("tm") > 0
    for low in range(0, half, LANES):
        a, b = own[at : at + count, low : low + LANES], other[at : at + count, low : low + LANES]
        for cols, start in (
            (slice(low, low + LANES), jnp.where(is_first, a, b)),
            (slice(half + low, half + low + LANES), jnp.where(is_first, b, a)),
        ):
            difference[:, cols] = start - jnp.where(follows, previous[:, cols], 0.0)
    made = pltpu.make_async_copy(difference, defect.at[here], sems.at[1])
    made.start()
    kept.wait()
    made.wait()


def write_results(at, previous, own, other, final_part, earlier):
    shape = (own.shape[0], 2 * own.shape[1])
    hbm = pl.BlockSpec(memory_space=pltpu.HBM)
    return pl.pallas_call(
        functools.partial(results_kernel, at),
        out_shape=(pltpu.HBM(shape, jnp.float32),) * 2,
        in_specs=[VMEM] * 4 + [hbm] * len(earlier),
        out_specs=(hbm, hbm),
        scratch_shapes=[pltpu.VMEM(previous.shape, jnp.float32), pltpu.SemaphoreType.DMA((2,))],
        input_output_aliases={4 + i: i for i in range(len(earlier))},
        compiler_params=pltpu.CompilerParams(vmem_limit_bytes=4 * 2**20),
    )(*(pltpu.with_memory_space_constraint(v, pltpu.VMEM) for v in (previous, own, other, final_part)), *earlier)


def on_device(control, scales, courant, diffusion, pacing):
    control, scales, courant, diffusion = (v[0] for v in (control, scales, courant, diffusion))
    steps = pacing.shape[1]
    rows, columns = control.shape
    half, tiles = columns // 2, columns // LANES
    windows, bands = lax.axis_size("tm"), lax.axis_size("lat")
    window = lax.axis_index("tm")
    is_first, chip = window % 2 == 0, window // 2
    onward = [(i, (i + 1) % bands) for i in range(bands)]
    backward = [(j, i) for i, j in onward]
    partner = [(i, i ^ 1) for i in range(windows)]
    following = [(i, (i + 1) % windows) for i in range(windows)]
    paces = jnp.broadcast_to(pacing.reshape(steps, 1), (steps, LANES))

    increment = scales * control
    left, right = increment[:, :half], increment[:, half:]
    own = jnp.where(is_first, left, right)
    other = jnp.where(is_first, right, left)

    field = (tiles, rows + 2 * steps, LANES)
    to_onward, to_backward = call(functools.partial(pack_kernel, steps), [(2 * steps, columns)] * 2, (courant, diffusion))
    outer = lax.ppermute(to_onward, "lat", onward), lax.ppermute(to_backward, "lat", backward)

    c_all, d_all = call(functools.partial(coefficients_kernel, steps), [field] * 2,
                        (courant, diffusion, *outer), moved=MOVED)

    pair = own + lax.ppermute(other, "tm", partner)
    total, before = pair, jnp.zeros_like(pair)
    distance = 1
    while 2 * distance < windows:
        swap = [(i, i ^ (2 * distance)) for i in range(windows)]
        arrived = lax.ppermute(total, "tm", swap)
        if 4 * distance >= windows:
            arrived, c_all, d_all = lax.optimization_barrier((arrived, c_all, d_all))
        before = before + jnp.where((chip // distance) % 2 == 1, arrived, 0.0)
        total = total + arrived
        distance *= 2
    through_first = before + own
    arrived = lax.ppermute(jnp.where(is_first, through_first, before), "tm", partner)
    start_own = jnp.where(is_first, through_first, before + pair)
    start_other = arrived + other

    south = lax.ppermute(jnp.concatenate([start_own[rows - steps :], start_other[rows - steps :]]), "lat", onward)
    north = lax.ppermute(jnp.concatenate([start_own[:steps], start_other[:steps]]), "lat", backward)

    work = 16 * steps * steps * columns
    even, odd = call(functools.partial(inner_kernel, steps), [field] * 2,
                     (paces, start_own, start_other, c_all, d_all), work=work)
    even, odd, final_south = call(
        functools.partial(south_kernel, steps), [field, field, (steps, columns)],
        (paces, south, c_all, d_all, even, odd), {4: 0, 5: 1}, work=work)
    previous_south = lax.ppermute(final_south, "tm", following)
    _, _, final_north = call(
        functools.partial(north_kernel, steps), [field, field, (rows - steps, columns)],
        (paces, north, c_all, d_all, even, odd), {4: 0, 5: 1}, work=work)
    previous_north = lax.ppermute(final_north, "tm", following)
    results = write_results(0, previous_south, start_own, start_other, final_south, ())
    defect, final = write_results(steps, previous_north, start_own, start_other, final_north, results)
    return defect[None], final[None]


def solution(mesh):
    whole = P("tm", "lat", None)
    return jax.shard_map(
        on_device,
        mesh=mesh,
        in_specs=(whole, whole, whole, whole, P("tm", None)),
        out_specs=(whole, whole),
        check_vma=False,
    )
```

time: 62.2 us -> 58.9 us (0.947)
  the two profiles are of different devices: /device:TPU:16 before, /device:TPU:0 now
where the time goes in v3:
time: 58.9 us; the launch traced here: 58.7 us
  waiting for transfers between devices  27.4 us (47%)
  starting transfers between devices  14.2 us (24%)
  Pallas kernels  13.1 us (22%)
  other arithmetic  2.35 us (4%)
  between operations  0.82 us (1%)
  local copies, waits for them, and re-layouts  0.81 us (1%)
    pallas_call x5, Pallas kernels, call(): pl.pallas_call(kernel, out_shape=tuple((pltpu.VMEM(shape, jnp.float32) fo...  11.5 us
    ppermute x1, waiting for transfers between devices, on_device(): lax.ppermute(to_backward, 'lat', backward)  10.7 us
    ppermute x2, waiting for transfers between devices, on_device(): arrived = lax.ppermute(total, 'tm', swap)  5.78 us
    ppermute x2, starting transfers between devices, on_device(): arrived = lax.ppermute(total, 'tm', swap)  4.78 us
    ppermute x1, waiting for transfers between devices, on_device(): lax.ppermute(jnp.concatenate([start_own[rows - steps:], start_other[rows...  3.05 us
    ppermute x1, waiting for transfers between devices, on_device(): previous_north = lax.ppermute(final_north, 'tm', following)  3.01 us
    ppermute x1, starting transfers between devices, on_device(): lax.ppermute(to_onward, 'lat', onward)  2.99 us
    ppermute x1, waiting for transfers between devices, on_device(): previous_south = lax.ppermute(final_south, 'tm', following)  2.17 us
  transfers between devices with their start and end apart: 10, of which 7 were waited for; matrix products, arithmetic and copies ran while one was open for 2% of the time, Pallas kernels for 21%

profile of v3, /device:TPU:0, one launch (start us, length us, event | category | flops | bytes accessed | tf_op | source)
XLA Modules:
  0.0 58.7 jit_solution(8248084892325984264)
XLA Ops:
  0.6 0.0 copy-start.1
  0.7 1.3 %multiply_bitcast_fusion = f32[32,4096]{1,0:T(8,128)S(1)} fusion(f32[1,32,4096]{2,1,0:T(8,128)} %param.6, f32[1,32,4096]{2,1,0:T(8,128)} %param.5), kind=kLoop, calls=%fused_computation | loop fusion | flops 131072 | bytes 1572864 | tf_op jit(solution)/shard_map/mul | solution.py:163
  2.0 0.0 copy-start.2
  2.0 0.0 copy-start
  2.0 0.5 collective-permute-start
  2.5 0.0 copy-done.1
  2.6 0.7 %copy-done = f32[1,32,4096]{2,1,0:T(8,128)S(1)} copy-done((f32[1,32,4096]{2,1,0:T(8,128)S(1)}, f32[1,32,4096]{2,1,0:T(8,128)}, u32[]{:S(2)}) %copy-start) | copy-done | bytes 524312
  3.2 0.1 shard_map.68
  3.3 3.0 %collective-permute-start.3 = (f32[32,4096]{1,0:T(8,128)S(1)}, f32[32,4096]{1,0:T(8,128)S(1)}, u32[]{:S(2)}, u32[]{:S(2)}) collective-permute-start(f32[32,4096]{1,0:T(8,128)S(1)} %get-tuple-element.19), channel_id=1, source_target_pairs={{0,1},{1,2},{2,3},{3,0},{4,5},{5,6},{6,7},{7,4},{8,9},{9,10},{10,1... | collective-permute-start | bytes 1572872 | tf_op jit(solution)/shard_map/ppermute | solution.py:170
  6.3 1.0 %collective-permute-start.4 = (f32[32,4096]{1,0:T(8,128)S(1)}, f32[32,4096]{1,0:T(8,128)S(1)}, u32[]{:S(2)}, u32[]{:S(2)}) collective-permute-start(f32[32,4096]{1,0:T(8,128)S(1)} %get-tuple-element.20), channel_id=1, source_target_pairs={{1,0},{2,1},{3,2},{0,3},{5,4},{6,5},{7,6},{4,7},{9,8},{10,9},{11,1... | collective-permute-start | bytes 1572872 | tf_op jit(solution)/shard_map/ppermute | solution.py:170
  7.3 0.0 collective-permute-done
  7.3 0.0 copy-done.2
  7.4 2.1 %collective-permute-start.1 = (f32[32,2048]{1,0:T(8,128)S(1)}, f32[32,2048]{1,0:T(8,128)S(1)}, u32[]{:S(2)}, u32[]{:S(2)}) collective-permute-start(f32[32,2048]{1,0:T(8,128)S(1)} %fusion), channel_id=1, source_target_pairs={{0,8},{4,12},{8,0},{12,4},{16,24},{20,28},{24,16},{28,20},{1,9},{5... | collective-permute-start | bytes 786440 | tf_op jit(solution)/shard_map/ppermute | solution.py:180
  9.4 5.8 %collective-permute-done.1 = f32[32,2048]{1,0:T(8,128)S(1)} collective-permute-done((f32[32,2048]{1,0:T(8,128)S(1)}, f32[32,2048]{1,0:T(8,128)S(1)}, u32[]{:S(2)}, u32[]{:S(2)}) %collective-permute-start.1) | collective-permute-done | bytes 262176 | tf_op jit(solution)/shard_map/ppermute | solution.py:180
  15.2 0.0 copy-start.4
  15.2 0.8 %add.35 = f32[32,2048]{1,0:T(8,128)} add(f32[32,2048]{1,0:T(8,128)S(1)} %fusion, f32[32,2048]{1,0:T(8,128)S(1)} %collective-permute-done.1) | non-fusion elementwise | flops 65536 | bytes 786432 | tf_op jit(solution)/shard_map/add | solution.py:184
  16.0 0.0 copy-done.4
  16.0 2.7 %collective-permute-start.2 = (f32[32,2048]{1,0:T(8,128)}, f32[32,2048]{1,0:T(8,128)}, u32[]{:S(2)}, u32[]{:S(2)}) collective-permute-start(f32[32,2048]{1,0:T(8,128)} %add.35), channel_id=1, source_target_pairs={{0,16},{4,20},{8,24},{12,28},{16,0},{20,4},{24,8},{28,12},{1,17},{... | collective-permute-start | bytes 786440 | tf_op jit(solution)/shard_map/ppermute | solution.py:180
  18.7 0.0 copy-start.3
  18.7 0.0 copy-start.5
  18.7 1.3 %collective-permute-done.3.south = f32[32,4096]{1,0:T(8,128)S(1)} collective-permute-done((f32[32,4096]{1,0:T(8,128)S(1)}, f32[32,4096]{1,0:T(8,128)S(1)}, u32[]{:S(2)}, u32[]{:S(2)}) %collective-permute-start.3) | collective-permute-done | bytes 524320 | tf_op jit(solution)/shard_map/ppermute | solution.py:170
  20.0 10.7 %collective-permute-done.4.north = f32[32,4096]{1,0:T(8,128)S(1)} collective-permute-done((f32[32,4096]{1,0:T(8,128)S(1)}, f32[32,4096]{1,0:T(8,128)S(1)}, u32[]{:S(2)}, u32[]{:S(2)}) %collective-permute-start.4) | collective-permute-done | bytes 524320 | tf_op jit(solution)/shard_map/ppermute | solution.py:170
  30.6 0.2 shard_map.69
  30.8 0.0 collective-permute-done.2
  30.8 0.0 copy-done.3
  30.9 0.0 copy-done.5
  30.9 0.1 add_select_fusion
  31.0 0.1 collective-permute-start.5
  31.1 1.5 %collective-permute-done.5 = f32[32,2048]{1,0:T(8,128)S(1)} collective-permute-done((f32[32,2048]{1,0:T(8,128)S(1)}, f32[32,2048]{1,0:T(8,128)S(1)}, u32[]{:S(2)}, u32[]{:S(2)}) %collective-permute-start.5) | collective-permute-done | bytes 262176 | tf_op jit(solution)/shard_map/ppermute | solution.py:187
  32.6 0.1 fusion.3.other
  32.7 1.5 %collective-permute-start.7 = (f32[32,2048]{1,0:T(8,128)S(1)}, f32[32,2048]{1,0:T(8,128)S(1)}, u32[]{:S(2)}, u32[]{:S(2)}) collective-permute-start(f32[32,2048]{1,0:T(8,128)S(1)} %pad_maximum_fusion.1), channel_id=1, source_target_pairs={{0,1},{1,2},{2,3},{3,0},{4,5},{5,6},{6,7},{7,4},{8,9},{9,10},{10,1... | collective-permute-start | bytes 786440 | tf_op jit(solution)/shard_map/ppermute | solution.py:191
  34.2 0.0 copy-start.6
  34.2 1.5 %collective-permute-start.6 = (f32[32,2048]{1,0:T(8,128)S(1)}, f32[32,2048]{1,0:T(8,128)S(1)}, u32[]{:S(2)}, u32[]{:S(2)}) collective-permute-start(f32[32,2048]{1,0:T(8,128)S(1)} %pad_maximum_fusion), channel_id=1, source_target_pairs={{1,0},{2,1},{3,2},{0,3},{5,4},{6,5},{7,6},{4,7},{9,8},{10,9},{11,1... | collective-permute-start | bytes 786440 | tf_op jit(solution)/shard_map/ppermute | solution.py:192
  35.7 0.0 copy-done.6
  35.7 0.1 broadcast_in_dim.19.paces
  35.8 3.9 %shard_map.70 = (f32[32,64,128]{2,1,0:T(8,128)S(1)}, f32[32,64,128]{2,1,0:T(8,128)S(1)}) custom-call(f32[16,128]{1,0:T(8,128)S(1)} %broadcast_in_dim.19.paces, f32[32,2048]{1,0:T(8,128)S(1)} %get-tuple-element.36.own, f32[32,2048]{1,0:T(8,128)S(1)} %fusion.3.other, f32[32,64,128]{2,1,0:T(8,128)S(1)} %get-tuple-element.24.c_all, ...), custom_call_target="tpu_custom_call" | custom-call | flops 16777216 | tf_op jit(solution)/shard_map/pallas_call | solution.py:16
  39.7 3.0 %collective-permute-done.7.halo = f32[32,2048]{1,0:T(8,128)S(1)} collective-permute-done((f32[32,2048]{1,0:T(8,128)S(1)}, f32[32,2048]{1,0:T(8,128)S(1)}, u32[]{:S(2)}, u32[]{:S(2)}) %collective-permute-start.7) | collective-permute-done | bytes 262176 | tf_op jit(solution)/shard_map/ppermute | solution.py:191
  42.8 3.6 %shard_map.71 = (f32[32,64,128]{2,1,0:T(8,128)S(1)}, f32[32,64,128]{2,1,0:T(8,128)S(1)}, f32[16,4096]{1,0:T(8,128)S(1)}) custom-call(f32[16,128]{1,0:T(8,128)S(1)} %broadcast_in_dim.19.paces, f32[32,2048]{1,0:T(8,128)S(1)} %collective-permute-done.7.halo, f32[32,64,128]{2,1,0:T(8,128)S(1)} %get-tuple-element.24.c_all, ...), custom_call_target="tpu_custom_call", output_to_operand_aliasing={{0}: (4, {}), {1}: (5, {})} | custom-call | flops 16777216 | tf_op jit(solution)/shard_map/pallas_call | solution.py:16
  46.4 0.1 collective-permute-start.9
  46.5 0.0 collective-permute-done.6.halo
  46.5 3.7 %shard_map.72 = (f32[32,64,128]{2,1,0:T(8,128)S(1)}, f32[32,64,128]{2,1,0:T(8,128)S(1)}, f32[16,4096]{1,0:T(8,128)S(1)}) custom-call(f32[16,128]{1,0:T(8,128)S(1)} %broadcast_in_dim.19.paces, f32[32,2048]{1,0:T(8,128)S(1)} %collective-permute-done.6.halo, f32[32,64,128]{2,1,0:T(8,128)S(1)} %get-tuple-element.24.c_all, ...), custom_call_target="tpu_custom_call", output_to_operand_aliasing={{0}: (4, {}), {1}: (5, {})} | custom-call | flops 16777216 | tf_op jit(solution)/shard_map/pallas_call | solution.py:16
  50.2 1.7 %collective-permute-start.8 = (f32[16,4096]{1,0:T(8,128)S(1)}, f32[16,4096]{1,0:T(8,128)S(1)}, u32[]{:S(2)}, u32[]{:S(2)}) collective-permute-start(f32[16,4096]{1,0:T(8,128)S(1)} %get-tuple-element.30.final_part), channel_id=1, source_target_pairs={{0,4},{4,8},{8,12},{12,16},{16,20},{20,24},{24,28},{28,0},{1,5},{5... | collective-permute-start | bytes 786440 | tf_op jit(solution)/shard_map/ppermute | solution.py:204
  51.9 2.2 %collective-permute-done.9.previous = f32[16,4096]{1,0:T(8,128)S(1)} collective-permute-done((f32[16,4096]{1,0:T(8,128)S(1)}, f32[16,4096]{1,0:T(8,128)S(1)}, u32[]{:S(2)}, u32[]{:S(2)}) %collective-permute-start.9) | collective-permute-done | bytes 262176 | tf_op jit(solution)/shard_map/ppermute | solution.py:200
  54.1 0.8 %shard_map.73 = (f32[32,4096]{1,0:T(8,128)}, f32[32,4096]{1,0:T(8,128)}) custom-call(f32[16,4096]{1,0:T(8,128)S(1)} %collective-permute-done.9.previous, f32[32,2048]{1,0:T(8,128)S(1)} %get-tuple-element.36.own, f32[32,2048]{1,0:T(8,128)S(1)} %fusion.3.other, f32[16,4096]{1,0:T(8,128)S(1)} %get-tuple-element.31.final_part), custom_call_target="tpu_custom_call" | custom-call | tf_op jit(solution)/shard_map/pallas_call | solution.py:138
  54.9 3.0 %collective-permute-done.8.previous = f32[16,4096]{1,0:T(8,128)S(1)} collective-permute-done((f32[16,4096]{1,0:T(8,128)S(1)}, f32[16,4096]{1,0:T(8,128)S(1)}, u32[]{:S(2)}, u32[]{:S(2)}) %collective-permute-start.8) | collective-permute-done | bytes 262176 | tf_op jit(solution)/shard_map/ppermute | solution.py:204
  57.9 0.8 %shard_map.74 = (f32[32,4096]{1,0:T(8,128)}, f32[32,4096]{1,0:T(8,128)}) custom-call(f32[16,4096]{1,0:T(8,128)S(1)} %collective-permute-done.8.previous, f32[32,2048]{1,0:T(8,128)S(1)} %get-tuple-element.36.own, f32[32,2048]{1,0:T(8,128)S(1)} %fusion.3.other, ...), custom_call_target="tpu_custom_call", output_to_operand_aliasing={{0}: (4, {}), {1}: (5, {})} | custom-call | tf_op jit(solution)/shard_map/pallas_call | solution.py:138
  (6 shorter events, 0.1 us)
Async XLA Ops:
  0.6 1.9 %copy-start.1 = (f32[1,32,4096]{2,1,0:T(8,128)S(1)}, f32[1,32,4096]{2,1,0:T(8,128)}, u32[]{:S(2)}) copy-start(f32[1,32,4096]{2,1,0:T(8,128)} %param.8) | copy-start | bytes 1572868
  2.0 5.3 %copy-start.2 = (f32[32,4096]{1,0:T(8,128)}, f32[32,4096]{1,0:T(8,128)S(1)}, u32[]{:S(2)}) copy-start(f32[32,4096]{1,0:T(8,128)S(1)} %multiply_bitcast_fusion) | copy-start | bytes 1572868
  2.0 1.2 %copy-start = (f32[1,32,4096]{2,1,0:T(8,128)S(1)}, f32[1,32,4096]{2,1,0:T(8,128)}, u32[]{:S(2)}) copy-start(f32[1,32,4096]{2,1,0:T(8,128)} %param.7) | copy-start | bytes 1572868
  2.0 5.3 %collective-permute-start = (f32[32,2048]{1,0:T(8,128)S(1)}, f32[32,2048]{1,0:T(8,128)S(1)}, u32[]{:S(2)}, u32[]{:S(2)}) collective-permute-start(f32[32,2048]{1,0:T(8,128)S(1)} %slice_select_fusion), channel_id=1, source_target_pairs={{0,4},{4,0},{8,12},{12,8},{16,20},{20,16},{24,28},{28,24},{1,5},{5... | collective-permute-start | bytes 786440 | tf_op jit(solution)/shard_map/ppermute | solution.py:175
  3.3 16.7 %collective-permute-start.3 = (f32[32,4096]{1,0:T(8,128)S(1)}, f32[32,4096]{1,0:T(8,128)S(1)}, u32[]{:S(2)}, u32[]{:S(2)}) collective-permute-start(f32[32,4096]{1,0:T(8,128)S(1)} %get-tuple-element.19), channel_id=1, source_target_pairs={{0,1},{1,2},{2,3},{3,0},{4,5},{5,6},{6,7},{7,4},{8,9},{9,10},{10,1... | collective-permute-start | bytes 1572872 | tf_op jit(solution)/shard_map/ppermute | solution.py:170
  6.3 24.4 %collective-permute-start.4 = (f32[32,4096]{1,0:T(8,128)S(1)}, f32[32,4096]{1,0:T(8,128)S(1)}, u32[]{:S(2)}, u32[]{:S(2)}) collective-permute-start(f32[32,4096]{1,0:T(8,128)S(1)} %get-tuple-element.20), channel_id=1, source_target_pairs={{1,0},{2,1},{3,2},{0,3},{5,4},{6,5},{7,6},{4,7},{9,8},{10,9},{11,1... | collective-permute-start | bytes 1572872 | tf_op jit(solution)/shard_map/ppermute | solution.py:170
  7.4 7.8 %collective-permute-start.1 = (f32[32,2048]{1,0:T(8,128)S(1)}, f32[32,2048]{1,0:T(8,128)S(1)}, u32[]{:S(2)}, u32[]{:S(2)}) collective-permute-start(f32[32,2048]{1,0:T(8,128)S(1)} %fusion), channel_id=1, source_target_pairs={{0,8},{4,12},{8,0},{12,4},{16,24},{20,28},{24,16},{28,20},{1,9},{5... | collective-permute-start | bytes 786440 | tf_op jit(solution)/shard_map/ppermute | solution.py:180
  15.2 0.8 %copy-start.4 = (f32[32,2048]{1,0:T(8,128)}, f32[32,2048]{1,0:T(8,128)S(1)}, u32[]{:S(2)}) copy-start(f32[32,2048]{1,0:T(8,128)S(1)} %collective-permute-done.1) | copy-start | bytes 786436
  16.0 14.9 %collective-permute-start.2 = (f32[32,2048]{1,0:T(8,128)}, f32[32,2048]{1,0:T(8,128)}, u32[]{:S(2)}, u32[]{:S(2)}) collective-permute-start(f32[32,2048]{1,0:T(8,128)} %add.35), channel_id=1, source_target_pairs={{0,16},{4,20},{8,24},{12,28},{16,0},{20,4},{24,8},{28,12},{1,17},{... | collective-permute-start | bytes 786440 | tf_op jit(solution)/shard_map/ppermute | solution.py:180
  18.7 12.1 %copy-start.3 = (f32[32,4096]{1,0:T(8,128)S(1)}, f32[32,4096]{1,0:T(8,128)}, u32[]{:S(2)}) copy-start(f32[32,4096]{1,0:T(8,128)} %copy-done.2) | copy-start | bytes 1572868
  18.7 12.2 %copy-start.5 = (f32[32,2048]{1,0:T(8,128)S(1)}, f32[32,2048]{1,0:T(8,128)}, u32[]{:S(2)}) copy-start(f32[32,2048]{1,0:T(8,128)} %copy-done.4) | copy-start | bytes 786436
  31.0 1.6 %collective-permute-start.5 = (f32[32,2048]{1,0:T(8,128)S(1)}, f32[32,2048]{1,0:T(8,128)S(1)}, u32[]{:S(2)}, u32[]{:S(2)}) collective-permute-start(f32[32,2048]{1,0:T(8,128)S(1)} %get-tuple-element.37), channel_id=1, source_target_pairs={{0,4},{4,0},{8,12},{12,8},{16,20},{20,16},{24,28},{28,24},{1,5},{5... | collective-permute-start | bytes 786440 | tf_op jit(solution)/shard_map/ppermute | solution.py:187
  32.7 10.1 %collective-permute-start.7 = (f32[32,2048]{1,0:T(8,128)S(1)}, f32[32,2048]{1,0:T(8,128)S(1)}, u32[]{:S(2)}, u32[]{:S(2)}) collective-permute-start(f32[32,2048]{1,0:T(8,128)S(1)} %pad_maximum_fusion.1), channel_id=1, source_target_pairs={{0,1},{1,2},{2,3},{3,0},{4,5},{5,6},{6,7},{7,4},{8,9},{9,10},{10,1... | collective-permute-start | bytes 786440 | tf_op jit(solution)/shard_map/ppermute | solution.py:191
  34.2 1.5 %copy-start.6 = (f32[1,16]{1,0:T(1,128)S(1)}, f32[1,16]{1,0:T(1,128)}, u32[]{:S(2)}) copy-start(f32[1,16]{1,0:T(1,128)} %param.9) | copy-start | bytes 196
  34.2 12.2 %collective-permute-start.6 = (f32[32,2048]{1,0:T(8,128)S(1)}, f32[32,2048]{1,0:T(8,128)S(1)}, u32[]{:S(2)}, u32[]{:S(2)}) collective-permute-start(f32[32,2048]{1,0:T(8,128)S(1)} %pad_maximum_fusion), channel_id=1, source_target_pairs={{1,0},{2,1},{3,2},{0,3},{5,4},{6,5},{7,6},{4,7},{9,8},{10,9},{11,1... | collective-permute-start | bytes 786440 | tf_op jit(solution)/shard_map/ppermute | solution.py:192
  46.4 7.6 %collective-permute-start.9 = (f32[16,4096]{1,0:T(8,128)S(1)}, f32[16,4096]{1,0:T(8,128)S(1)}, u32[]{:S(2)}, u32[]{:S(2)}) collective-permute-start(f32[16,4096]{1,0:T(8,128)S(1)} %get-tuple-element.31.final_part), channel_id=1, source_target_pairs={{0,4},{4,8},{8,12},{12,16},{16,20},{20,24},{24,28},{28,0},{1,5},{5... | collective-permute-start | bytes 786440 | tf_op jit(solution)/shard_map/ppermute | solution.py:200
  50.2 7.7 %collective-permute-start.8 = (f32[16,4096]{1,0:T(8,128)S(1)}, f32[16,4096]{1,0:T(8,128)S(1)}, u32[]{:S(2)}, u32[]{:S(2)}) collective-permute-start(f32[16,4096]{1,0:T(8,128)S(1)} %get-tuple-element.30.final_part), channel_id=1, source_target_pairs={{0,4},{4,8},{8,12},{12,16},{16,20},{20,24},{24,28},{28,0},{1,5},{5... | collective-permute-start | bytes 786440 | tf_op jit(solution)/shard_map/ppermute | solution.py:204

commit v4 on v3

--- a/solution.py
+++ b/solution.py
@@ -9,6 +9,7 @@
 
 LANES = 128
 MOVED = 64 * 2**20
+PIECES = 2
 VMEM = pl.BlockSpec(memory_space=pltpu.VMEM)
 
 
@@ -45,7 +46,7 @@
         old, new = old_and_new if step % 2 else old_and_new[::-1]
         pace = paces[step - 1 : step, :]
         lane = lax.broadcasted_iota(jnp.int32, (stop - first, LANES), 1)
-        for t in range(tiles):
+        for t in ((step + i) % tiles for i in range(tiles)):
             x = old[t, first:stop, :]
             east = pltpu.roll(jnp.where(lane == 0, old[(t + 1) % tiles, first:stop, :], x), LANES - 1, 1)
             west = pltpu.roll(jnp.where(lane == LANES - 1, old[(t - 1) % tiles, first:stop, :], x), 1, 1)
@@ -57,6 +58,33 @@
             new[t, first:stop, :] = x + (d * pace) * spread - c * jnp.where(c > 0, behind, ahead)
 
 
+def sum_kernel(a, b, total):
+    total[:, :] = a[:, :] + b[:, :]
+
+
+def prefix_kernel(pieces, steps, own, pair, *refs):
+    brought, (send, start_own, to_onward, to_backward) = refs[:-4], refs[-4:]
+    hops = len(brought) // pieces
+    width = own.shape[1] // pieces
+    is_first, chip = lax.axis_index("tm") % 2 == 0, lax.axis_index("tm") // 2
+    for piece in range(pieces):
+        cols = slice(piece * width, (piece + 1) * width)
+        before = jnp.where(chip % 2 == 1, brought[piece * hops][:, :], 0.0)
+        for hop in range(1, hops):
+            before = before + jnp.where(chip == hop + 1, brought[piece * hops + hop][:, :], 0.0)
+        through_first = before + own[:, cols]
+        send[:, cols] = jnp.where(is_first, through_first, before)
+        start_own[:, cols] = jnp.where(is_first, through_first, before + pair[:, cols])
+    to_onward[:, :] = start_own[own.shape[0] - steps :, :]
+    to_backward[:, :] = start_own[:steps, :]
+
+
+def halo_kernel(steps, other, arrived, start_other, to_onward, to_backward):
+    start_other[:, :] = other[:, :] + arrived[:, :]
+    to_onward[:, :] = start_other[other.shape[0] - steps :, :]
+    to_backward[:, :] = start_other[:steps, :]
+
+
 def pack_kernel(steps, courant, diffusion, onward, backward):
     rows = courant.shape[0]
     for at, field in ((0, courant), (steps, diffusion)):
@@ -64,14 +92,20 @@
         backward[at : at + steps, :] = field[:steps, :]
 
 
-def coefficients_kernel(steps, courant, diffusion, south, north, c_all, d_all):
-    rows, tiles = courant.shape[0], c_all.shape[0]
-    has_before, has_after = has_band_before(), has_band_after()
-    for t in range(tiles):
-        for at, field, whole in ((0, courant, c_all), (steps, diffusion, d_all)):
-            whole[t, steps : steps + rows, :] = field[:, columns_of(t)]
-            whole[t, :steps, :] = jnp.where(has_before, south[at : at + steps, columns_of(t)], 0.0)
-            whole[t, steps + rows :, :] = jnp.where(has_after, north[at : at + steps, columns_of(t)], 0.0)
+def inner_coefficients_kernel(steps, courant, diffusion, c_all, d_all):
+    rows = courant.shape[0]
+    for t in range(c_all.shape[0]):
+        c_all[t, steps : steps + rows, :] = courant[:, columns_of(t)]
+        d_all[t, steps : steps + rows, :] = diffusion[:, columns_of(t)]
+
+
+def outer_coefficients_kernel(steps, at, side, c_in, d_in, c_all, d_all):
+    del c_in, d_in
+    exists = has_band_before() if at == 0 else has_band_after()
+    for t in range(c_all.shape[0]):
+        for which, whole in enumerate((c_all, d_all)):
+            rows = side[which * steps : (which + 1) * steps, columns_of(t)]
+            whole[t, at : at + steps, :] = jnp.where(exists, rows, 0.0)
 
 
 def place_halves(own, other, rows, whole):
@@ -88,23 +122,23 @@
     advance_rows(steps, lambda n: (steps + n, steps + rows - n), (even, odd), c_all, d_all, paces)
 
 
-def south_kernel(steps, paces, halo, c_all, d_all, even_in, odd_in, even, odd, part):
+def south_kernel(steps, paces, own, other, c_all, d_all, even_in, odd_in, even, odd, part):
     del even_in, odd_in
     exists = has_band_before()
-    place_halves(lambda cols: jnp.where(exists, halo[:steps, cols], 0.0),
-                 lambda cols: jnp.where(exists, halo[steps:, cols], 0.0), slice(0, steps), even)
+    place_halves(lambda cols: jnp.where(exists, own[:, cols], 0.0),
+                 lambda cols: jnp.where(exists, other[:, cols], 0.0), slice(0, steps), even)
     advance_rows(steps, lambda n: (n, steps + n), (even, odd), c_all, d_all, paces)
     last = odd if steps % 2 else even
     for t in range(last.shape[0]):
         part[:, columns_of(t)] = last[t, steps : 2 * steps, :]
 
 
-def north_kernel(steps, paces, halo, c_all, d_all, even_in, odd_in, even, odd, part):
+def north_kernel(steps, paces, own, other, c_all, d_all, even_in, odd_in, even, odd, part):
     del even_in, odd_in
     exists = has_band_after()
     rows = c_all.shape[1] - 2 * steps
-    place_halves(lambda cols: jnp.where(exists, halo[:steps, cols], 0.0),
-                 lambda cols: jnp.where(exists, halo[steps:, cols], 0.0), slice(steps + rows, 2 * steps + rows), even)
+    place_halves(lambda cols: jnp.where(exists, own[:, cols], 0.0),
+                 lambda cols: jnp.where(exists, other[:, cols], 0.0), slice(steps + rows, 2 * steps + rows), even)
     advance_rows(steps, lambda n: (steps + rows - n, 2 * steps + rows - n), (even, odd), c_all, d_all, paces)
     last = odd if steps % 2 else even
     for t in range(last.shape[0]):
@@ -153,7 +187,7 @@
     half, tiles = columns // 2, columns // LANES
     windows, bands = lax.axis_size("tm"), lax.axis_size("lat")
     window = lax.axis_index("tm")
-    is_first, chip = window % 2 == 0, window // 2
+    is_first = window % 2 == 0
     onward = [(i, (i + 1) % bands) for i in range(bands)]
     backward = [(j, i) for i, j in onward]
     partner = [(i, i ^ 1) for i in range(windows)]
@@ -167,41 +201,50 @@
 
     field = (tiles, rows + 2 * steps, LANES)
     to_onward, to_backward = call(functools.partial(pack_kernel, steps), [(2 * steps, columns)] * 2, (courant, diffusion))
-    outer = lax.ppermute(to_onward, "lat", onward), lax.ppermute(to_backward, "lat", backward)
-
-    c_all, d_all = call(functools.partial(coefficients_kernel, steps), [field] * 2,
-                        (courant, diffusion, *outer), moved=MOVED)
-
-    pair = own + lax.ppermute(other, "tm", partner)
-    total, before = pair, jnp.zeros_like(pair)
-    distance = 1
-    while 2 * distance < windows:
-        swap = [(i, i ^ (2 * distance)) for i in range(windows)]
-        arrived = lax.ppermute(total, "tm", swap)
-        if 4 * distance >= windows:
-            arrived, c_all, d_all = lax.optimization_barrier((arrived, c_all, d_all))
-        before = before + jnp.where((chip // distance) % 2 == 1, arrived, 0.0)
-        total = total + arrived
-        distance *= 2
-    through_first = before + own
-    arrived = lax.ppermute(jnp.where(is_first, through_first, before), "tm", partner)
-    start_own = jnp.where(is_first, through_first, before + pair)
-    start_other = arrived + other
-
-    south = lax.ppermute(jnp.concatenate([start_own[rows - steps :], start_other[rows - steps :]]), "lat", onward)
-    north = lax.ppermute(jnp.concatenate([start_own[:steps], start_other[:steps]]), "lat", backward)
+    coef_south, coef_north = lax.ppermute(to_onward, "lat", onward), lax.ppermute(to_backward, "lat", backward)
+    c_all, d_all = call(functools.partial(inner_coefficients_kernel, steps), [field] * 2, (courant, diffusion))
+    c_all, d_all = call(functools.partial(outer_coefficients_kernel, steps, 0), [field] * 2,
+                        (coef_south, c_all, d_all), {1: 0, 2: 1}, moved=MOVED)
+
+    (pair,) = call(sum_kernel, [own.shape], (own, lax.ppermute(other, "tm", partner)))
+    width, chips = half // PIECES, windows // 2
+    parts = [pair[:, i * width : (i + 1) * width] for i in range(PIECES)]
+    brought = [[lax.ppermute(part, "tm", [(i, i ^ 2) for i in range(windows)])] for part in parts]
+    totals = [call(sum_kernel, [part.shape], (part, more))[0] for part, (more,) in zip(parts, brought)]
+    carried = totals
+    for hop in range(1, chips - 1):
+        swap = [(i + 2 * a, i + 2 * b) for i in range(2) for a, b in ((hop, hop + 1), (hop + 1, hop))]
+        moved = [lax.ppermute(part, "tm", swap) for part in carried]
+        for earlier, more in zip(brought, moved):
+            earlier.append(more)
+        carried = moved if hop % 2 else [
+            call(sum_kernel, [more.shape], (more, part))[0] for more, part in zip(moved, totals)
+        ]
+    (*brought[-1], c_all, d_all) = lax.optimization_barrier((*brought[-1], c_all, d_all))
+    edge = (steps, half)
+    send, start_own, to_onward, to_backward = call(
+        functools.partial(prefix_kernel, PIECES, steps), [own.shape, own.shape, edge, edge],
+        (own, pair, *(v for earlier in brought for v in earlier)))
+    south_own, north_own = lax.ppermute(to_onward, "lat", onward), lax.ppermute(to_backward, "lat", backward)
+    arrived = lax.ppermute(send, "tm", partner)
+    c_all, coef_north, south_own = lax.optimization_barrier((c_all, coef_north, south_own))
+    start_other, to_onward, to_backward = call(
+        functools.partial(halo_kernel, steps), [own.shape, edge, edge], (other, arrived))
+    south_other, north_other = lax.ppermute(to_onward, "lat", onward), lax.ppermute(to_backward, "lat", backward)
 
     work = 16 * steps * steps * columns
     even, odd = call(functools.partial(inner_kernel, steps), [field] * 2,
                      (paces, start_own, start_other, c_all, d_all), work=work)
     even, odd, final_south = call(
         functools.partial(south_kernel, steps), [field, field, (steps, columns)],
-        (paces, south, c_all, d_all, even, odd), {4: 0, 5: 1}, work=work)
+        (paces, south_own, south_other, c_all, d_all, even, odd), {5: 0, 6: 1}, work=work)
     previous_south = lax.ppermute(final_south, "tm", following)
+    c_all, d_all = call(functools.partial(outer_coefficients_kernel, steps, steps + rows), [field] * 2,
+                        (coef_north, c_all, d_all), {1: 0, 2: 1})
     _, _, final_north = call(
         functools.partial(north_kernel, steps), [field, field, (rows - steps, columns)],
-        (paces, north, c_all, d_all, even, odd), {4: 0, 5: 1}, work=work)
-    previous_north = lax.ppermute(final_north, "tm", following)
+        (paces, north_own, north_other, c_all, d_all, even, odd), {5: 0, 6: 1}, work=work)
+    previous_north = lax.ppermute(final_north, "tm", following[:-1])
     results = write_results(0, previous_south, start_own, start_other, final_south, ())
     defect, final = write_results(steps, previous_north, start_own, start_other, final_north, results)
     return defect[None], final[None]

time: 58.9 us -> 54.6 us (0.927)
  the two profiles are of different devices: /device:TPU:0 before, /device:TPU:16 now
where the time goes in v4:
time: 54.6 us; the launch traced here: 53.9 us
  starting transfers between devices  24.8 us (45%)
  waiting for transfers between devices  15.5 us (28%)
  Pallas kernels  10.2 us (19%)
  other arithmetic  1.29 us (2%)
  local copies, waits for them, and re-layouts  1.16 us (2%)
  between operations  0.87 us (2%)
    ppermute x4, starting transfers between devices, on_device(): moved = [lax.ppermute(part, 'tm', swap) for part in carried]  11.7 us
    pallas_call x12, Pallas kernels, call(): pl.pallas_call(kernel, out_shape=tuple((pltpu.VMEM(shape, jnp.float32) fo...  8.57 us
    ppermute x1, waiting for transfers between devices, on_device(): previous_north = lax.ppermute(final_north, 'tm', following[:-1])  4.94 us
    ppermute x3, starting transfers between devices, on_device(): lax.ppermute(to_onward, 'lat', onward)  4.61 us
    ppermute x3, starting transfers between devices, on_device(): lax.ppermute(to_backward, 'lat', backward)  4.35 us
    ppermute x2, waiting for transfers between devices, on_device(): lax.ppermute(part, 'tm', [(i, i ^ 2) for i in range(windows)])  4.34 us
    ppermute x4, waiting for transfers between devices, on_device(): moved = [lax.ppermute(part, 'tm', swap) for part in carried]  2.76 us
    ppermute x3, waiting for transfers between devices, on_device(): lax.ppermute(to_backward, 'lat', backward)  2.23 us
  transfers between devices with their start and end apart: 16, of which 6 were waited for; matrix products, arithmetic and copies ran while one was open for 0% of the time, Pallas kernels for 17%

profile of v4, /device:TPU:16, one launch (start us, length us, event | category | flops | bytes accessed | tf_op | source)
XLA Modules:
  0.0 53.9 jit_solution(5488304121214411560)
XLA Ops:
  0.6 1.3 %multiply_bitcast_fusion = f32[32,4096]{1,0:T(8,128)S(1)} fusion(f32[1,32,4096]{2,1,0:T(8,128)} %param.6, f32[1,32,4096]{2,1,0:T(8,128)} %param.5), kind=kLoop, calls=%fused_computation | loop fusion | flops 131072 | bytes 1572864 | tf_op jit(solution)/shard_map/mul | solution.py:197
  1.9 0.0 copy-start
  1.9 0.0 copy-start.1
  2.0 0.1 collective-permute-start
  2.0 0.9 %copy-done = f32[1,32,4096]{2,1,0:T(8,128)S(1)} copy-done((f32[1,32,4096]{2,1,0:T(8,128)S(1)}, f32[1,32,4096]{2,1,0:T(8,128)}, u32[]{:S(2)}) %copy-start) | copy-done | bytes 524312
  2.9 0.2 copy-done.1
  3.1 0.1 shard_map.71
  3.2 1.5 %collective-permute-start.7 = (f32[32,4096]{1,0:T(8,128)S(1)}, f32[32,4096]{1,0:T(8,128)S(1)}, u32[]{:S(2)}, u32[]{:S(2)}) collective-permute-start(f32[32,4096]{1,0:T(8,128)S(1)} %get-tuple-element.35), channel_id=1, source_target_pairs={{0,1},{1,2},{2,3},{3,0},{4,5},{5,6},{6,7},{7,4},{8,9},{9,10},{10,1... | collective-permute-start | bytes 1572872 | tf_op jit(solution)/shard_map/ppermute | solution.py:204
  4.7 0.0 collective-permute-done.b
  4.8 1.6 %collective-permute-start.4 = (f32[32,1024]{1,0:T(8,128)S(1)}, f32[32,1024]{1,0:T(8,128)S(1)}, u32[]{:S(2)}, u32[]{:S(2)}) collective-permute-start(f32[32,1024]{1,0:T(8,128)S(1)} %get-tuple-element.70.a), channel_id=1, source_target_pairs={{0,8},{4,12},{8,0},{12,4},{16,24},{20,28},{24,16},{28,20},{1,9},{5... | collective-permute-start | bytes 393224 | tf_op jit(solution)/shard_map/ppermute | solution.py:212
  6.4 0.4 collective-permute-start.1
  6.9 4.3 %collective-permute-done.4.b.refs_3_ = f32[32,1024]{1,0:T(8,128)S(1)} collective-permute-done((f32[32,1024]{1,0:T(8,128)S(1)}, f32[32,1024]{1,0:T(8,128)S(1)}, u32[]{:S(2)}, u32[]{:S(2)}) %collective-permute-start.4) | collective-permute-done | bytes 131104 | tf_op jit(solution)/shard_map/ppermute | solution.py:212
  11.2 2.4 %collective-permute-start.5 = (f32[32,1024]{1,0:T(8,128)S(1)}, f32[32,1024]{1,0:T(8,128)S(1)}, u32[]{:S(2)}, u32[]{:S(2)}) collective-permute-start(f32[32,1024]{1,0:T(8,128)S(1)} %shard_map.70), channel_id=1, source_target_pairs={{8,16},{16,8},{12,20},{20,12},{9,17},{17,9},{13,21},{21,13},{10,18... | collective-permute-start | bytes 393224 | tf_op jit(solution)/shard_map/ppermute | solution.py:217
  13.6 0.0 collective-permute-done.1.b.refs_0_
  13.6 3.5 %collective-permute-start.2 = (f32[32,1024]{1,0:T(8,128)S(1)}, f32[32,1024]{1,0:T(8,128)S(1)}, u32[]{:S(2)}, u32[]{:S(2)}) collective-permute-start(f32[32,1024]{1,0:T(8,128)S(1)} %shard_map.69), channel_id=1, source_target_pairs={{8,16},{16,8},{12,20},{20,12},{9,17},{17,9},{13,21},{21,13},{10,18... | collective-permute-start | bytes 393224 | tf_op jit(solution)/shard_map/ppermute | solution.py:217
  17.1 1.5 %collective-permute-start.11 = (f32[32,4096]{1,0:T(8,128)S(1)}, f32[32,4096]{1,0:T(8,128)S(1)}, u32[]{:S(2)}, u32[]{:S(2)}) collective-permute-start(f32[32,4096]{1,0:T(8,128)S(1)} %get-tuple-element.47), channel_id=1, source_target_pairs={{1,0},{2,1},{3,2},{0,3},{5,4},{6,5},{7,6},{4,7},{9,8},{10,9},{11,1... | collective-permute-start | bytes 1572872 | tf_op jit(solution)/shard_map/ppermute | solution.py:204
  18.6 0.0 collective-permute-done.5.refs_4_
  18.6 1.9 %collective-permute-start.6 = (f32[32,1024]{1,0:T(8,128)S(1)}, f32[32,1024]{1,0:T(8,128)S(1)}, u32[]{:S(2)}, u32[]{:S(2)}) collective-permute-start(f32[32,1024]{1,0:T(8,128)S(1)} %collective-permute-done.5.refs_4_), channel_id=1, source_target_pairs={{16,24},{24,16},{20,28},{28,20},{17,25},{25,17},{21,29},{29,21},{1... | collective-permute-start | bytes 393224 | tf_op jit(solution)/shard_map/ppermute | solution.py:217
  20.5 0.0 collective-permute-done.2.refs_1_
  20.5 3.9 %collective-permute-start.3 = (f32[32,1024]{1,0:T(8,128)S(1)}, f32[32,1024]{1,0:T(8,128)S(1)}, u32[]{:S(2)}, u32[]{:S(2)}) collective-permute-start(f32[32,1024]{1,0:T(8,128)S(1)} %collective-permute-done.2.refs_1_), channel_id=1, source_target_pairs={{16,24},{24,16},{20,28},{28,20},{17,25},{25,17},{21,29},{29,21},{1... | collective-permute-start | bytes 393224 | tf_op jit(solution)/shard_map/ppermute | solution.py:217
  24.5 0.1 shard_map.72
  24.6 0.0 collective-permute-done.7.side
  24.6 0.1 shard_map.73
  24.6 0.8 %collective-permute-done.6.refs_5_ = f32[32,1024]{1,0:T(8,128)S(1)} collective-permute-done((f32[32,1024]{1,0:T(8,128)S(1)}, f32[32,1024]{1,0:T(8,128)S(1)}, u32[]{:S(2)}, u32[]{:S(2)}) %collective-permute-start.6) | collective-permute-done | bytes 131104 | tf_op jit(solution)/shard_map/ppermute | solution.py:217
  25.5 1.9 %collective-permute-done.3.refs_2_ = f32[32,1024]{1,0:T(8,128)S(1)} collective-permute-done((f32[32,1024]{1,0:T(8,128)S(1)}, f32[32,1024]{1,0:T(8,128)S(1)}, u32[]{:S(2)}, u32[]{:S(2)}) %collective-permute-start.3) | collective-permute-done | bytes 131104 | tf_op jit(solution)/shard_map/ppermute | solution.py:217
  27.4 0.1 shard_map.74
  27.5 0.1 collective-permute-start.9
  27.6 1.5 %collective-permute-start.12 = (f32[16,2048]{1,0:T(8,128)S(1)}, f32[16,2048]{1,0:T(8,128)S(1)}, u32[]{:S(2)}, u32[]{:S(2)}) collective-permute-start(f32[16,2048]{1,0:T(8,128)S(1)} %get-tuple-element.48), channel_id=1, source_target_pairs={{0,1},{1,2},{2,3},{3,0},{4,5},{5,6},{6,7},{7,4},{8,9},{9,10},{10,1... | collective-permute-start | bytes 393224 | tf_op jit(solution)/shard_map/ppermute | solution.py:228
  29.1 0.0 collective-permute-done.9.arrived
  29.2 1.6 %collective-permute-start.13 = (f32[16,2048]{1,0:T(8,128)S(1)}, f32[16,2048]{1,0:T(8,128)S(1)}, u32[]{:S(2)}, u32[]{:S(2)}) collective-permute-start(f32[16,2048]{1,0:T(8,128)S(1)} %get-tuple-element.55), channel_id=1, source_target_pairs={{0,1},{1,2},{2,3},{3,0},{4,5},{5,6},{6,7},{7,4},{8,9},{9,10},{10,1... | collective-permute-start | bytes 393224 | tf_op jit(solution)/shard_map/ppermute | solution.py:233
  30.7 1.4 %collective-permute-start.8 = (f32[16,2048]{1,0:T(8,128)S(1)}, f32[16,2048]{1,0:T(8,128)S(1)}, u32[]{:S(2)}, u32[]{:S(2)}) collective-permute-start(f32[16,2048]{1,0:T(8,128)S(1)} %get-tuple-element.43), channel_id=1, source_target_pairs={{1,0},{2,1},{3,2},{0,3},{5,4},{6,5},{7,6},{4,7},{9,8},{10,9},{11,1... | collective-permute-start | bytes 393224 | tf_op jit(solution)/shard_map/ppermute | solution.py:228
  32.2 1.4 %collective-permute-start.10 = (f32[16,2048]{1,0:T(8,128)S(1)}, f32[16,2048]{1,0:T(8,128)S(1)}, u32[]{:S(2)}, u32[]{:S(2)}) collective-permute-start(f32[16,2048]{1,0:T(8,128)S(1)} %get-tuple-element.45), channel_id=1, source_target_pairs={{1,0},{2,1},{3,2},{0,3},{5,4},{6,5},{7,6},{4,7},{9,8},{10,9},{11,1... | collective-permute-start | bytes 393224 | tf_op jit(solution)/shard_map/ppermute | solution.py:233
  33.6 0.0 collective-permute-done.11.side
  33.6 1.2 %collective-permute-done.12.own = f32[16,2048]{1,0:T(8,128)S(1)} collective-permute-done((f32[16,2048]{1,0:T(8,128)S(1)}, f32[16,2048]{1,0:T(8,128)S(1)}, u32[]{:S(2)}, u32[]{:S(2)}) %collective-permute-start.12) | collective-permute-done | bytes 131104 | tf_op jit(solution)/shard_map/ppermute | solution.py:228
  34.9 0.1 broadcast_in_dim.14.paces
  34.9 3.0 %shard_map.77 = (f32[32,64,128]{2,1,0:T(8,128)S(1)}, f32[32,64,128]{2,1,0:T(8,128)S(1)}) custom-call(f32[16,128]{1,0:T(8,128)S(1)} %broadcast_in_dim.14.paces, f32[32,2048]{1,0:T(8,128)S(1)} %get-tuple-element.56.own, f32[32,2048]{1,0:T(8,128)S(1)} %get-tuple-element.57.other, f32[32,64,128]{2,1,0:T(8,128)S(1)} %get-tuple-element.50.c_in.c_all, ...), custom_call_target="tpu_custom_call" | custom-call | flops 16777216 | tf_op jit(solution)/shard_map/pallas_call | solution.py:17
  38.0 0.0 collective-permute-done.13.other
  38.0 2.5 %shard_map.78 = (f32[32,64,128]{2,1,0:T(8,128)S(1)}, f32[32,64,128]{2,1,0:T(8,128)S(1)}, f32[16,4096]{1,0:T(8,128)S(1)}) custom-call(f32[16,128]{1,0:T(8,128)S(1)} %broadcast_in_dim.14.paces, f32[16,2048]{1,0:T(8,128)S(1)} %collective-permute-done.12.own, ...), custom_call_target="tpu_custom_call", output_to_operand_aliasing={{0}: (5, {}), {1}: (6, {})} | custom-call | flops 16777216 | tf_op jit(solution)/shard_map/pallas_call | solution.py:17
  40.5 0.1 shard_map.76
  40.6 0.1 collective-permute-start.15
  40.7 0.0 collective-permute-done.8.own
  40.7 2.2 %collective-permute-done.10.other = f32[16,2048]{1,0:T(8,128)S(1)} collective-permute-done((f32[16,2048]{1,0:T(8,128)S(1)}, f32[16,2048]{1,0:T(8,128)S(1)}, u32[]{:S(2)}, u32[]{:S(2)}) %collective-permute-start.10) | collective-permute-done | bytes 131104 | tf_op jit(solution)/shard_map/ppermute | solution.py:233
  42.9 2.5 %shard_map.79 = (f32[32,64,128]{2,1,0:T(8,128)S(1)}, f32[32,64,128]{2,1,0:T(8,128)S(1)}, f32[16,4096]{1,0:T(8,128)S(1)}) custom-call(f32[16,128]{1,0:T(8,128)S(1)} %broadcast_in_dim.14.paces, f32[16,2048]{1,0:T(8,128)S(1)} %collective-permute-done.8.own, f32[16,2048]{1,0:T(8,128)S(1)} %collective-permute-done.10.other, ...), custom_call_target="tpu_custom_call", output_to_operand_aliasing={{0}: (5, {}), {1}: (6, {})} | custom-call | flops 16777216 | tf_op jit(solution)/shard_map/pallas_call | solution.py:17
  45.4 1.9 %collective-permute-start.14 = (f32[16,4096]{1,0:T(8,128)S(1)}, f32[16,4096]{1,0:T(8,128)S(1)}, u32[]{:S(2)}, u32[]{:S(2)}) collective-permute-start(f32[16,4096]{1,0:T(8,128)S(1)} %get-tuple-element.62.final_part), channel_id=1, source_target_pairs={{0,4},{4,8},{8,12},{12,16},{16,20},{20,24},{24,28},{1,5},{5,9},{9,... | collective-permute-start | bytes 786440 | tf_op jit(solution)/shard_map/ppermute | solution.py:247
  47.3 0.0 collective-permute-done.15.previous
  47.3 0.8 %shard_map.80 = (f32[32,4096]{1,0:T(8,128)}, f32[32,4096]{1,0:T(8,128)}) custom-call(f32[16,4096]{1,0:T(8,128)S(1)} %collective-permute-done.15.previous, f32[32,2048]{1,0:T(8,128)S(1)} %get-tuple-element.56.own, f32[32,2048]{1,0:T(8,128)S(1)} %get-tuple-element.57.other, f32[16,4096]{1,0:T(8,128)S(1)} %get-tuple-element.63.final_part), custom_call_target="tpu_custom_call" | custom-call | tf_op jit(solution)/shard_map/pallas_call | solution.py:172
  48.1 4.9 %collective-permute-done.14.previous = f32[16,4096]{1,0:T(8,128)S(1)} collective-permute-done((f32[16,4096]{1,0:T(8,128)S(1)}, f32[16,4096]{1,0:T(8,128)S(1)}, u32[]{:S(2)}, u32[]{:S(2)}) %collective-permute-start.14) | collective-permute-done | bytes 262176 | tf_op jit(solution)/shard_map/ppermute | solution.py:247
  53.1 0.8 %shard_map.81 = (f32[32,4096]{1,0:T(8,128)}, f32[32,4096]{1,0:T(8,128)}) custom-call(f32[16,4096]{1,0:T(8,128)S(1)} %collective-permute-done.14.previous, f32[32,2048]{1,0:T(8,128)S(1)} %get-tuple-element.56.own, f32[32,2048]{1,0:T(8,128)S(1)} %get-tuple-element.57.other, ...), custom_call_target="tpu_custom_call", output_to_operand_aliasing={{0}: (4, {}), {1}: (5, {})} | custom-call | tf_op jit(solution)/shard_map/pallas_call | solution.py:172
  (8 shorter events, 0.2 us)
Async XLA Ops:
  1.9 1.0 %copy-start = (f32[1,32,4096]{2,1,0:T(8,128)S(1)}, f32[1,32,4096]{2,1,0:T(8,128)}, u32[]{:S(2)}) copy-start(f32[1,32,4096]{2,1,0:T(8,128)} %param.7) | copy-start | bytes 1572868
  1.9 1.2 %copy-start.1 = (f32[1,32,4096]{2,1,0:T(8,128)S(1)}, f32[1,32,4096]{2,1,0:T(8,128)}, u32[]{:S(2)}) copy-start(f32[1,32,4096]{2,1,0:T(8,128)} %param.8) | copy-start | bytes 1572868
  2.0 2.8 %collective-permute-start = (f32[32,2048]{1,0:T(8,128)S(1)}, f32[32,2048]{1,0:T(8,128)S(1)}, u32[]{:S(2)}, u32[]{:S(2)}) collective-permute-start(f32[32,2048]{1,0:T(8,128)S(1)} %get-tuple-element.68.other), channel_id=1, source_target_pairs={{0,4},{4,0},{8,12},{12,8},{16,20},{20,16},{24,28},{28,24},{1,5},{5... | collective-permute-start | bytes 786440 | tf_op jit(solution)/shard_map/ppermute | solution.py:209
  3.2 21.4 %collective-permute-start.7 = (f32[32,4096]{1,0:T(8,128)S(1)}, f32[32,4096]{1,0:T(8,128)S(1)}, u32[]{:S(2)}, u32[]{:S(2)}) collective-permute-start(f32[32,4096]{1,0:T(8,128)S(1)} %get-tuple-element.35), channel_id=1, source_target_pairs={{0,1},{1,2},{2,3},{3,0},{4,5},{5,6},{6,7},{7,4},{8,9},{9,10},{10,1... | collective-permute-start | bytes 1572872 | tf_op jit(solution)/shard_map/ppermute | solution.py:204
  4.8 6.4 %collective-permute-start.4 = (f32[32,1024]{1,0:T(8,128)S(1)}, f32[32,1024]{1,0:T(8,128)S(1)}, u32[]{:S(2)}, u32[]{:S(2)}) collective-permute-start(f32[32,1024]{1,0:T(8,128)S(1)} %get-tuple-element.70.a), channel_id=1, source_target_pairs={{0,8},{4,12},{8,0},{12,4},{16,24},{20,28},{24,16},{28,20},{1,9},{5... | collective-permute-start | bytes 393224 | tf_op jit(solution)/shard_map/ppermute | solution.py:212
  6.4 7.2 %collective-permute-start.1 = (f32[32,1024]{1,0:T(8,128)S(1)}, f32[32,1024]{1,0:T(8,128)S(1)}, u32[]{:S(2)}, u32[]{:S(2)}) collective-permute-start(f32[32,1024]{1,0:T(8,128)S(1)} %get-tuple-element.71.a), channel_id=1, source_target_pairs={{0,8},{4,12},{8,0},{12,4},{16,24},{20,28},{24,16},{28,20},{1,9},{5... | collective-permute-start | bytes 393224 | tf_op jit(solution)/shard_map/ppermute | solution.py:212
  11.2 7.4 %collective-permute-start.5 = (f32[32,1024]{1,0:T(8,128)S(1)}, f32[32,1024]{1,0:T(8,128)S(1)}, u32[]{:S(2)}, u32[]{:S(2)}) collective-permute-start(f32[32,1024]{1,0:T(8,128)S(1)} %shard_map.70), channel_id=1, source_target_pairs={{8,16},{16,8},{12,20},{20,12},{9,17},{17,9},{13,21},{21,13},{10,18... | collective-permute-start | bytes 393224 | tf_op jit(solution)/shard_map/ppermute | solution.py:217
  13.6 6.9 %collective-permute-start.2 = (f32[32,1024]{1,0:T(8,128)S(1)}, f32[32,1024]{1,0:T(8,128)S(1)}, u32[]{:S(2)}, u32[]{:S(2)}) collective-permute-start(f32[32,1024]{1,0:T(8,128)S(1)} %shard_map.69), channel_id=1, source_target_pairs={{8,16},{16,8},{12,20},{20,12},{9,17},{17,9},{13,21},{21,13},{10,18... | collective-permute-start | bytes 393224 | tf_op jit(solution)/shard_map/ppermute | solution.py:217
  17.1 16.5 %collective-permute-start.11 = (f32[32,4096]{1,0:T(8,128)S(1)}, f32[32,4096]{1,0:T(8,128)S(1)}, u32[]{:S(2)}, u32[]{:S(2)}) collective-permute-start(f32[32,4096]{1,0:T(8,128)S(1)} %get-tuple-element.47), channel_id=1, source_target_pairs={{1,0},{2,1},{3,2},{0,3},{5,4},{6,5},{7,6},{4,7},{9,8},{10,9},{11,1... | collective-permute-start | bytes 1572872 | tf_op jit(solution)/shard_map/ppermute | solution.py:204
  18.6 6.9 %collective-permute-start.6 = (f32[32,1024]{1,0:T(8,128)S(1)}, f32[32,1024]{1,0:T(8,128)S(1)}, u32[]{:S(2)}, u32[]{:S(2)}) collective-permute-start(f32[32,1024]{1,0:T(8,128)S(1)} %collective-permute-done.5.refs_4_), channel_id=1, source_target_pairs={{16,24},{24,16},{20,28},{28,20},{17,25},{25,17},{21,29},{29,21},{1... | collective-permute-start | bytes 393224 | tf_op jit(solution)/shard_map/ppermute | solution.py:217
  20.5 6.9 %collective-permute-start.3 = (f32[32,1024]{1,0:T(8,128)S(1)}, f32[32,1024]{1,0:T(8,128)S(1)}, u32[]{:S(2)}, u32[]{:S(2)}) collective-permute-start(f32[32,1024]{1,0:T(8,128)S(1)} %collective-permute-done.2.refs_1_), channel_id=1, source_target_pairs={{16,24},{24,16},{20,28},{28,20},{17,25},{25,17},{21,29},{29,21},{1... | collective-permute-start | bytes 393224 | tf_op jit(solution)/shard_map/ppermute | solution.py:217
  27.5 1.6 %collective-permute-start.9 = (f32[32,2048]{1,0:T(8,128)S(1)}, f32[32,2048]{1,0:T(8,128)S(1)}, u32[]{:S(2)}, u32[]{:S(2)}) collective-permute-start(f32[32,2048]{1,0:T(8,128)S(1)} %get-tuple-element.44), channel_id=1, source_target_pairs={{0,4},{4,0},{8,12},{12,8},{16,20},{20,16},{24,28},{28,24},{1,5},{5... | collective-permute-start | bytes 786440 | tf_op jit(solution)/shard_map/ppermute | solution.py:229
  27.6 7.2 %collective-permute-start.12 = (f32[16,2048]{1,0:T(8,128)S(1)}, f32[16,2048]{1,0:T(8,128)S(1)}, u32[]{:S(2)}, u32[]{:S(2)}) collective-permute-start(f32[16,2048]{1,0:T(8,128)S(1)} %get-tuple-element.48), channel_id=1, source_target_pairs={{0,1},{1,2},{2,3},{3,0},{4,5},{5,6},{6,7},{7,4},{8,9},{9,10},{10,1... | collective-permute-start | bytes 393224 | tf_op jit(solution)/shard_map/ppermute | solution.py:228
  29.2 8.8 %collective-permute-start.13 = (f32[16,2048]{1,0:T(8,128)S(1)}, f32[16,2048]{1,0:T(8,128)S(1)}, u32[]{:S(2)}, u32[]{:S(2)}) collective-permute-start(f32[16,2048]{1,0:T(8,128)S(1)} %get-tuple-element.55), channel_id=1, source_target_pairs={{0,1},{1,2},{2,3},{3,0},{4,5},{5,6},{6,7},{7,4},{8,9},{9,10},{10,1... | collective-permute-start | bytes 393224 | tf_op jit(solution)/shard_map/ppermute | solution.py:233
  30.7 9.9 %collective-permute-start.8 = (f32[16,2048]{1,0:T(8,128)S(1)}, f32[16,2048]{1,0:T(8,128)S(1)}, u32[]{:S(2)}, u32[]{:S(2)}) collective-permute-start(f32[16,2048]{1,0:T(8,128)S(1)} %get-tuple-element.43), channel_id=1, source_target_pairs={{1,0},{2,1},{3,2},{0,3},{5,4},{6,5},{7,6},{4,7},{9,8},{10,9},{11,1... | collective-permute-start | bytes 393224 | tf_op jit(solution)/shard_map/ppermute | solution.py:228
  32.2 2.7 %copy-start.2 = (f32[1,16]{1,0:T(1,128)S(1)}, f32[1,16]{1,0:T(1,128)}, u32[]{:S(2)}) copy-start(f32[1,16]{1,0:T(1,128)} %param.9) | copy-start | bytes 196
  32.2 10.7 %collective-permute-start.10 = (f32[16,2048]{1,0:T(8,128)S(1)}, f32[16,2048]{1,0:T(8,128)S(1)}, u32[]{:S(2)}, u32[]{:S(2)}) collective-permute-start(f32[16,2048]{1,0:T(8,128)S(1)} %get-tuple-element.45), channel_id=1, source_target_pairs={{1,0},{2,1},{3,2},{0,3},{5,4},{6,5},{7,6},{4,7},{9,8},{10,9},{11,1... | collective-permute-start | bytes 393224 | tf_op jit(solution)/shard_map/ppermute | solution.py:233
  40.6 6.7 %collective-permute-start.15 = (f32[16,4096]{1,0:T(8,128)S(1)}, f32[16,4096]{1,0:T(8,128)S(1)}, u32[]{:S(2)}, u32[]{:S(2)}) collective-permute-start(f32[16,4096]{1,0:T(8,128)S(1)} %get-tuple-element.63.final_part), channel_id=1, source_target_pairs={{0,4},{4,8},{8,12},{12,16},{16,20},{20,24},{24,28},{28,0},{1,5},{5... | collective-permute-start | bytes 786440 | tf_op jit(solution)/shard_map/ppermute | solution.py:241
  45.4 7.7 %collective-permute-start.14 = (f32[16,4096]{1,0:T(8,128)S(1)}, f32[16,4096]{1,0:T(8,128)S(1)}, u32[]{:S(2)}, u32[]{:S(2)}) collective-permute-start(f32[16,4096]{1,0:T(8,128)S(1)} %get-tuple-element.62.final_part), channel_id=1, source_target_pairs={{0,4},{4,8},{8,12},{12,16},{16,20},{20,24},{24,28},{1,5},{5,9},{9,... | collective-permute-start | bytes 786440 | tf_op jit(solution)/shard_map/ppermute | solution.py:247

commit v5 on v4

--- a/solution.py
+++ b/solution.py
@@ -8,19 +8,18 @@
 from jax.sharding import PartitionSpec as P
 
 LANES = 128
-MOVED = 64 * 2**20
 PIECES = 2
 VMEM = pl.BlockSpec(memory_space=pltpu.VMEM)
 
 
-def call(kernel, out_shapes, args, aliases=None, work=0, moved=0):
+def call(kernel, out_shapes, args, aliases=None, work=0):
     return pl.pallas_call(
         kernel,
         out_shape=tuple(pltpu.VMEM(shape, jnp.float32) for shape in out_shapes),
         in_specs=[VMEM] * len(args),
         out_specs=(VMEM,) * len(out_shapes),
         input_output_aliases=aliases or {},
-        cost_estimate=pl.CostEstimate(flops=work, bytes_accessed=moved, transcendentals=0),
+        cost_estimate=pl.CostEstimate(flops=work, bytes_accessed=0, transcendentals=0),
         compiler_params=pltpu.CompilerParams(vmem_limit_bytes=4 * 2**20),
     )(*(pltpu.with_memory_space_constraint(v, pltpu.VMEM) for v in args))
 
@@ -186,8 +185,7 @@
     rows, columns = control.shape
     half, tiles = columns // 2, columns // LANES
     windows, bands = lax.axis_size("tm"), lax.axis_size("lat")
-    window = lax.axis_index("tm")
-    is_first = window % 2 == 0
+    is_first = lax.axis_index("tm") % 2 == 0
     onward = [(i, (i + 1) % bands) for i in range(bands)]
     backward = [(j, i) for i, j in onward]
     partner = [(i, i ^ 1) for i in range(windows)]
@@ -204,7 +202,7 @@
     coef_south, coef_north = lax.ppermute(to_onward, "lat", onward), lax.ppermute(to_backward, "lat", backward)
     c_all, d_all = call(functools.partial(inner_coefficients_kernel, steps), [field] * 2, (courant, diffusion))
     c_all, d_all = call(functools.partial(outer_coefficients_kernel, steps, 0), [field] * 2,
-                        (coef_south, c_all, d_all), {1: 0, 2: 1}, moved=MOVED)
+                        (coef_south, c_all, d_all), {1: 0, 2: 1})
 
     (pair,) = call(sum_kernel, [own.shape], (own, lax.ppermute(other, "tm", partner)))
     width, chips = half // PIECES, windows // 2
@@ -220,14 +218,14 @@
         carried = moved if hop % 2 else [
             call(sum_kernel, [more.shape], (more, part))[0] for more, part in zip(moved, totals)
         ]
-    (*brought[-1], c_all, d_all) = lax.optimization_barrier((*brought[-1], c_all, d_all))
     edge = (steps, half)
     send, start_own, to_onward, to_backward = call(
         functools.partial(prefix_kernel, PIECES, steps), [own.shape, own.shape, edge, edge],
         (own, pair, *(v for earlier in brought for v in earlier)))
     south_own, north_own = lax.ppermute(to_onward, "lat", onward), lax.ppermute(to_backward, "lat", backward)
     arrived = lax.ppermute(send, "tm", partner)
-    c_all, coef_north, south_own = lax.optimization_barrier((c_all, coef_north, south_own))
+    arrived, c_all, d_all = lax.optimization_barrier((arrived, c_all, d_all))
+    c_all, coef_north = lax.optimization_barrier((c_all, coef_north))
     start_other, to_onward, to_backward = call(
         functools.partial(halo_kernel, steps), [own.shape, edge, edge], (other, arrived))
     south_other, north_other = lax.ppermute(to_onward, "lat", onward), lax.ppermute(to_backward, "lat", backward)

time: 54.6 us -> 54.3 us (level)
  local copies, waits for them, and re-layouts: 1.16 us -> 0.1 us
  starting transfers between devices: 24.8 us -> 25.8 us
    ppermute x2, waiting for transfers between devices: 4.34 us -> 2.69 us  [on_device(): lax.ppermute(part, 'tm', [(i, i ^ 2) for i in range(windows)])]
    ppermute x1, waiting for transfers between devices: 0.01 us -> 1.52 us  [on_device(): lax.ppermute(other, 'tm', partner)]
    unnamed x6, local copies, waits for them, and re-layouts: 1.07 us -> 0.01 us
    ppermute x3, starting transfers between devices: 4.35 us -> 5.28 us  [on_device(): lax.ppermute(to_backward, 'lat', backward)]
  transfers between devices with their start and end apart: 16 -> 16, of which waited for: 6 -> 8; matrix products, arithmetic and copies ran while one was open for 0% -> 0% of each run, Pallas kernels for 17% -> 17%
where the time goes in v5:
time: 54.3 us; the launch traced here: 54.1 us
  starting transfers between devices  25.8 us (48%)
  waiting for transfers between devices  15.9 us (29%)
  Pallas kernels  10.2 us (19%)
  other arithmetic  1.29 us (2%)
  between operations  0.85 us (2%)
    ppermute x4, starting transfers between devices, on_device(): moved = [lax.ppermute(part, 'tm', swap) for part in carried]  11.7 us
    pallas_call x12, Pallas kernels, call(): pl.pallas_call(kernel, out_shape=tuple((pltpu.VMEM(shape, jnp.float32) fo...  8.55 us
    ppermute x3, starting transfers between devices, on_device(): lax.ppermute(to_backward, 'lat', backward)  5.28 us
    ppermute x1, waiting for transfers between devices, on_device(): previous_north = lax.ppermute(final_north, 'tm', following[:-1])  4.94 us
    ppermute x3, starting transfers between devices, on_device(): lax.ppermute(to_onward, 'lat', onward)  4.63 us
    ppermute x4, waiting for transfers between devices, on_device(): moved = [lax.ppermute(part, 'tm', swap) for part in carried]  3.07 us
    ppermute x2, waiting for transfers between devices, on_device(): lax.ppermute(part, 'tm', [(i, i ^ 2) for i in range(windows)])  2.69 us
    ppermute x3, waiting for transfers between devices, on_device(): lax.ppermute(to_backward, 'lat', backward)  2.6 us
  transfers between devices with their start and end apart: 16, of which 8 were waited for; matrix products, arithmetic and copies ran while one was open for 0% of the time, Pallas kernels for 17%

profile of v5, /device:TPU:16, one launch (start us, length us, event | category | flops | bytes accessed | tf_op | source)
XLA Modules:
  0.0 54.1 jit_solution(4740650371839482921)
XLA Ops:
  0.6 1.3 %multiply_bitcast_fusion = f32[32,4096]{1,0:T(8,128)S(1)} fusion(f32[1,32,4096]{2,1,0:T(8,128)} %param.6, f32[1,32,4096]{2,1,0:T(8,128)} %param.5), kind=kLoop, calls=%fused_computation | loop fusion | flops 131072 | bytes 1572864 | tf_op jit(solution)/shard_map/mul | solution.py:195
  1.9 0.1 collective-permute-start
  2.0 1.5 %collective-permute-done.b = f32[32,2048]{1,0:T(8,128)S(1)} collective-permute-done((f32[32,2048]{1,0:T(8,128)S(1)}, f32[32,2048]{1,0:T(8,128)S(1)}, u32[]{:S(2)}, u32[]{:S(2)}) %collective-permute-start) | collective-permute-done | bytes 262176 | tf_op jit(solution)/shard_map/ppermute | solution.py:207
  3.5 0.0 copy-start
  3.6 1.6 %collective-permute-start.4 = (f32[32,1024]{1,0:T(8,128)S(1)}, f32[32,1024]{1,0:T(8,128)S(1)}, u32[]{:S(2)}, u32[]{:S(2)}) collective-permute-start(f32[32,1024]{1,0:T(8,128)S(1)} %get-tuple-element.64.a), channel_id=1, source_target_pairs={{0,8},{4,12},{8,0},{12,4},{16,24},{20,28},{24,16},{28,20},{1,9},{5... | collective-permute-start | bytes 393224 | tf_op jit(solution)/shard_map/ppermute | solution.py:210
  5.3 0.4 collective-permute-start.1
  5.7 0.0 copy-done
  5.7 0.0 copy-done.1
  5.7 0.1 shard_map.72
  5.8 1.5 %collective-permute-start.9 = (f32[32,4096]{1,0:T(8,128)S(1)}, f32[32,4096]{1,0:T(8,128)S(1)}, u32[]{:S(2)}, u32[]{:S(2)}) collective-permute-start(f32[32,4096]{1,0:T(8,128)S(1)} %get-tuple-element.34), channel_id=1, source_target_pairs={{0,1},{1,2},{2,3},{3,0},{4,5},{5,6},{6,7},{7,4},{8,9},{9,10},{10,1... | collective-permute-start | bytes 1572872 | tf_op jit(solution)/shard_map/ppermute | solution.py:202
  7.3 2.7 %collective-permute-done.4.b.refs_3_ = f32[32,1024]{1,0:T(8,128)S(1)} collective-permute-done((f32[32,1024]{1,0:T(8,128)S(1)}, f32[32,1024]{1,0:T(8,128)S(1)}, u32[]{:S(2)}, u32[]{:S(2)}) %collective-permute-start.4) | collective-permute-done | bytes 131104 | tf_op jit(solution)/shard_map/ppermute | solution.py:210
  10.0 2.4 %collective-permute-start.5 = (f32[32,1024]{1,0:T(8,128)S(1)}, f32[32,1024]{1,0:T(8,128)S(1)}, u32[]{:S(2)}, u32[]{:S(2)}) collective-permute-start(f32[32,1024]{1,0:T(8,128)S(1)} %shard_map.70), channel_id=1, source_target_pairs={{8,16},{16,8},{12,20},{20,12},{9,17},{17,9},{13,21},{21,13},{10,18... | collective-permute-start | bytes 393224 | tf_op jit(solution)/shard_map/ppermute | solution.py:215
  12.4 0.0 collective-permute-done.1.b.refs_0_
  12.4 3.5 %collective-permute-start.2 = (f32[32,1024]{1,0:T(8,128)S(1)}, f32[32,1024]{1,0:T(8,128)S(1)}, u32[]{:S(2)}, u32[]{:S(2)}) collective-permute-start(f32[32,1024]{1,0:T(8,128)S(1)} %shard_map.69), channel_id=1, source_target_pairs={{8,16},{16,8},{12,20},{20,12},{9,17},{17,9},{13,21},{21,13},{10,18... | collective-permute-start | bytes 393224 | tf_op jit(solution)/shard_map/ppermute | solution.py:215
  15.9 2.5 %collective-permute-start.11 = (f32[32,4096]{1,0:T(8,128)S(1)}, f32[32,4096]{1,0:T(8,128)S(1)}, u32[]{:S(2)}, u32[]{:S(2)}) collective-permute-start(f32[32,4096]{1,0:T(8,128)S(1)} %get-tuple-element.42), channel_id=1, source_target_pairs={{1,0},{2,1},{3,2},{0,3},{5,4},{6,5},{7,6},{4,7},{9,8},{10,9},{11,1... | collective-permute-start | bytes 1572872 | tf_op jit(solution)/shard_map/ppermute | solution.py:202
  18.4 0.0 collective-permute-done.5.refs_4_
  18.4 1.9 %collective-permute-start.6 = (f32[32,1024]{1,0:T(8,128)S(1)}, f32[32,1024]{1,0:T(8,128)S(1)}, u32[]{:S(2)}, u32[]{:S(2)}) collective-permute-start(f32[32,1024]{1,0:T(8,128)S(1)} %collective-permute-done.5.refs_4_), channel_id=1, source_target_pairs={{16,24},{24,16},{20,28},{28,20},{17,25},{25,17},{21,29},{29,21},{1... | collective-permute-start | bytes 393224 | tf_op jit(solution)/shard_map/ppermute | solution.py:215
  20.3 0.0 collective-permute-done.2.refs_1_
  20.4 3.9 %collective-permute-start.3 = (f32[32,1024]{1,0:T(8,128)S(1)}, f32[32,1024]{1,0:T(8,128)S(1)}, u32[]{:S(2)}, u32[]{:S(2)}) collective-permute-start(f32[32,1024]{1,0:T(8,128)S(1)} %collective-permute-done.2.refs_1_), channel_id=1, source_target_pairs={{16,24},{24,16},{20,28},{28,20},{17,25},{25,17},{21,29},{29,21},{1... | collective-permute-start | bytes 393224 | tf_op jit(solution)/shard_map/ppermute | solution.py:215
  24.3 1.7 %collective-permute-done.6.refs_5_ = f32[32,1024]{1,0:T(8,128)S(1)} collective-permute-done((f32[32,1024]{1,0:T(8,128)S(1)}, f32[32,1024]{1,0:T(8,128)S(1)}, u32[]{:S(2)}, u32[]{:S(2)}) %collective-permute-start.6) | collective-permute-done | bytes 131104 | tf_op jit(solution)/shard_map/ppermute | solution.py:215
  26.0 1.4 %collective-permute-done.3.refs_2_ = f32[32,1024]{1,0:T(8,128)S(1)} collective-permute-done((f32[32,1024]{1,0:T(8,128)S(1)}, f32[32,1024]{1,0:T(8,128)S(1)}, u32[]{:S(2)}, u32[]{:S(2)}) %collective-permute-start.3) | collective-permute-done | bytes 131104 | tf_op jit(solution)/shard_map/ppermute | solution.py:215
  27.4 0.1 shard_map.71
  27.5 0.1 collective-permute-start.8
  27.6 0.1 shard_map.73
  27.6 0.0 collective-permute-done.9.side
  27.6 0.1 shard_map.74
  27.7 1.5 %collective-permute-start.12 = (f32[16,2048]{1,0:T(8,128)S(1)}, f32[16,2048]{1,0:T(8,128)S(1)}, u32[]{:S(2)}, u32[]{:S(2)}) collective-permute-start(f32[16,2048]{1,0:T(8,128)S(1)} %get-tuple-element.48), channel_id=1, source_target_pairs={{0,1},{1,2},{2,3},{3,0},{4,5},{5,6},{6,7},{7,4},{8,9},{9,10},{10,1... | collective-permute-start | bytes 393224 | tf_op jit(solution)/shard_map/ppermute | solution.py:225
  29.3 0.0 collective-permute-done.8.arrived
  29.3 1.5 %collective-permute-start.13 = (f32[16,2048]{1,0:T(8,128)S(1)}, f32[16,2048]{1,0:T(8,128)S(1)}, u32[]{:S(2)}, u32[]{:S(2)}) collective-permute-start(f32[16,2048]{1,0:T(8,128)S(1)} %get-tuple-element.49), channel_id=1, source_target_pairs={{0,1},{1,2},{2,3},{3,0},{4,5},{5,6},{6,7},{7,4},{8,9},{9,10},{10,1... | collective-permute-start | bytes 393224 | tf_op jit(solution)/shard_map/ppermute | solution.py:231
  30.9 1.4 %collective-permute-start.7 = (f32[16,2048]{1,0:T(8,128)S(1)}, f32[16,2048]{1,0:T(8,128)S(1)}, u32[]{:S(2)}, u32[]{:S(2)}) collective-permute-start(f32[16,2048]{1,0:T(8,128)S(1)} %get-tuple-element.32), channel_id=1, source_target_pairs={{1,0},{2,1},{3,2},{0,3},{5,4},{6,5},{7,6},{4,7},{9,8},{10,9},{11,1... | collective-permute-start | bytes 393224 | tf_op jit(solution)/shard_map/ppermute | solution.py:225
  32.3 1.3 %collective-permute-start.10 = (f32[16,2048]{1,0:T(8,128)S(1)}, f32[16,2048]{1,0:T(8,128)S(1)}, u32[]{:S(2)}, u32[]{:S(2)}) collective-permute-start(f32[16,2048]{1,0:T(8,128)S(1)} %get-tuple-element.40), channel_id=1, source_target_pairs={{1,0},{2,1},{3,2},{0,3},{5,4},{6,5},{7,6},{4,7},{9,8},{10,9},{11,1... | collective-permute-start | bytes 393224 | tf_op jit(solution)/shard_map/ppermute | solution.py:231
  33.7 0.0 collective-permute-done.11.side
  33.7 0.0 copy-done.2
  33.7 0.1 broadcast_in_dim.14.paces
  33.7 3.0 %shard_map.77 = (f32[32,64,128]{2,1,0:T(8,128)S(1)}, f32[32,64,128]{2,1,0:T(8,128)S(1)}) custom-call(f32[16,128]{1,0:T(8,128)S(1)} %broadcast_in_dim.14.paces, f32[32,2048]{1,0:T(8,128)S(1)} %get-tuple-element.50.own, f32[32,2048]{1,0:T(8,128)S(1)} %get-tuple-element.51.other, f32[32,64,128]{2,1,0:T(8,128)S(1)} %get-tuple-element.44.c_in.c_all, ...), custom_call_target="tpu_custom_call" | custom-call | flops 16777216 | tf_op jit(solution)/shard_map/pallas_call | solution.py:16
  36.8 0.0 collective-permute-done.12.own
  36.8 1.0 %collective-permute-done.13.other = f32[16,2048]{1,0:T(8,128)S(1)} collective-permute-done((f32[16,2048]{1,0:T(8,128)S(1)}, f32[16,2048]{1,0:T(8,128)S(1)}, u32[]{:S(2)}, u32[]{:S(2)}) %collective-permute-start.13) | collective-permute-done | bytes 131104 | tf_op jit(solution)/shard_map/ppermute | solution.py:231
  37.8 2.5 %shard_map.78 = (f32[32,64,128]{2,1,0:T(8,128)S(1)}, f32[32,64,128]{2,1,0:T(8,128)S(1)}, f32[16,4096]{1,0:T(8,128)S(1)}) custom-call(f32[16,128]{1,0:T(8,128)S(1)} %broadcast_in_dim.14.paces, f32[16,2048]{1,0:T(8,128)S(1)} %collective-permute-done.12.own, ...), custom_call_target="tpu_custom_call", output_to_operand_aliasing={{0}: (5, {}), {1}: (6, {})} | custom-call | flops 16777216 | tf_op jit(solution)/shard_map/pallas_call | solution.py:16
  40.3 0.1 shard_map.76
  40.4 0.1 collective-permute-start.15
  40.5 0.2 collective-permute-done.7.own
  40.7 2.4 %collective-permute-done.10.other = f32[16,2048]{1,0:T(8,128)S(1)} collective-permute-done((f32[16,2048]{1,0:T(8,128)S(1)}, f32[16,2048]{1,0:T(8,128)S(1)}, u32[]{:S(2)}, u32[]{:S(2)}) %collective-permute-start.10) | collective-permute-done | bytes 131104 | tf_op jit(solution)/shard_map/ppermute | solution.py:231
  43.1 2.5 %shard_map.79 = (f32[32,64,128]{2,1,0:T(8,128)S(1)}, f32[32,64,128]{2,1,0:T(8,128)S(1)}, f32[16,4096]{1,0:T(8,128)S(1)}) custom-call(f32[16,128]{1,0:T(8,128)S(1)} %broadcast_in_dim.14.paces, f32[16,2048]{1,0:T(8,128)S(1)} %collective-permute-done.7.own, f32[16,2048]{1,0:T(8,128)S(1)} %collective-permute-done.10.other, ...), custom_call_target="tpu_custom_call", output_to_operand_aliasing={{0}: (5, {}), {1}: (6, {})} | custom-call | flops 16777216 | tf_op jit(solution)/shard_map/pallas_call | solution.py:16
  45.6 1.9 %collective-permute-start.14 = (f32[16,4096]{1,0:T(8,128)S(1)}, f32[16,4096]{1,0:T(8,128)S(1)}, u32[]{:S(2)}, u32[]{:S(2)}) collective-permute-start(f32[16,4096]{1,0:T(8,128)S(1)} %get-tuple-element.56.final_part), channel_id=1, source_target_pairs={{0,4},{4,8},{8,12},{12,16},{16,20},{20,24},{24,28},{1,5},{5,9},{9,... | collective-permute-start | bytes 786440 | tf_op jit(solution)/shard_map/ppermute | solution.py:245
  47.5 0.0 collective-permute-done.15.previous
  47.5 0.8 %shard_map.80 = (f32[32,4096]{1,0:T(8,128)}, f32[32,4096]{1,0:T(8,128)}) custom-call(f32[16,4096]{1,0:T(8,128)S(1)} %collective-permute-done.15.previous, f32[32,2048]{1,0:T(8,128)S(1)} %get-tuple-element.50.own, f32[32,2048]{1,0:T(8,128)S(1)} %get-tuple-element.51.other, f32[16,4096]{1,0:T(8,128)S(1)} %get-tuple-element.57.final_part), custom_call_target="tpu_custom_call" | custom-call | tf_op jit(solution)/shard_map/pallas_call | solution.py:171
  48.3 4.9 %collective-permute-done.14.previous = f32[16,4096]{1,0:T(8,128)S(1)} collective-permute-done((f32[16,4096]{1,0:T(8,128)S(1)}, f32[16,4096]{1,0:T(8,128)S(1)}, u32[]{:S(2)}, u32[]{:S(2)}) %collective-permute-start.14) | collective-permute-done | bytes 262176 | tf_op jit(solution)/shard_map/ppermute | solution.py:245
  53.3 0.8 %shard_map.81 = (f32[32,4096]{1,0:T(8,128)}, f32[32,4096]{1,0:T(8,128)}) custom-call(f32[16,4096]{1,0:T(8,128)S(1)} %collective-permute-done.14.previous, f32[32,2048]{1,0:T(8,128)S(1)} %get-tuple-element.50.own, f32[32,2048]{1,0:T(8,128)S(1)} %get-tuple-element.51.other, ...), custom_call_target="tpu_custom_call", output_to_operand_aliasing={{0}: (4, {}), {1}: (5, {})} | custom-call | tf_op jit(solution)/shard_map/pallas_call | solution.py:171
  (8 shorter events, 0.2 us)
Async XLA Ops:
  1.9 1.6 %collective-permute-start = (f32[32,2048]{1,0:T(8,128)S(1)}, f32[32,2048]{1,0:T(8,128)S(1)}, u32[]{:S(2)}, u32[]{:S(2)}) collective-permute-start(f32[32,2048]{1,0:T(8,128)S(1)} %get-tuple-element.62.other), channel_id=1, source_target_pairs={{0,4},{4,0},{8,12},{12,8},{16,20},{20,16},{24,28},{28,24},{1,5},{5... | collective-permute-start | bytes 786440 | tf_op jit(solution)/shard_map/ppermute | solution.py:207
  3.5 2.2 %copy-start = (f32[1,32,4096]{2,1,0:T(8,128)S(1)}, f32[1,32,4096]{2,1,0:T(8,128)}, u32[]{:S(2)}) copy-start(f32[1,32,4096]{2,1,0:T(8,128)} %param.7) | copy-start | bytes 1572868
  3.5 2.2 %copy-start.1 = (f32[1,32,4096]{2,1,0:T(8,128)S(1)}, f32[1,32,4096]{2,1,0:T(8,128)}, u32[]{:S(2)}) copy-start(f32[1,32,4096]{2,1,0:T(8,128)} %param.8) | copy-start | bytes 1572868
  3.6 6.4 %collective-permute-start.4 = (f32[32,1024]{1,0:T(8,128)S(1)}, f32[32,1024]{1,0:T(8,128)S(1)}, u32[]{:S(2)}, u32[]{:S(2)}) collective-permute-start(f32[32,1024]{1,0:T(8,128)S(1)} %get-tuple-element.64.a), channel_id=1, source_target_pairs={{0,8},{4,12},{8,0},{12,4},{16,24},{20,28},{24,16},{28,20},{1,9},{5... | collective-permute-start | bytes 393224 | tf_op jit(solution)/shard_map/ppermute | solution.py:210
  5.3 7.2 %collective-permute-start.1 = (f32[32,1024]{1,0:T(8,128)S(1)}, f32[32,1024]{1,0:T(8,128)S(1)}, u32[]{:S(2)}, u32[]{:S(2)}) collective-permute-start(f32[32,1024]{1,0:T(8,128)S(1)} %get-tuple-element.65.a), channel_id=1, source_target_pairs={{0,8},{4,12},{8,0},{12,4},{16,24},{20,28},{24,16},{28,20},{1,9},{5... | collective-permute-start | bytes 393224 | tf_op jit(solution)/shard_map/ppermute | solution.py:210
  5.8 21.9 %collective-permute-start.9 = (f32[32,4096]{1,0:T(8,128)S(1)}, f32[32,4096]{1,0:T(8,128)S(1)}, u32[]{:S(2)}, u32[]{:S(2)}) collective-permute-start(f32[32,4096]{1,0:T(8,128)S(1)} %get-tuple-element.34), channel_id=1, source_target_pairs={{0,1},{1,2},{2,3},{3,0},{4,5},{5,6},{6,7},{7,4},{8,9},{9,10},{10,1... | collective-permute-start | bytes 1572872 | tf_op jit(solution)/shard_map/ppermute | solution.py:202
  10.0 8.4 %collective-permute-start.5 = (f32[32,1024]{1,0:T(8,128)S(1)}, f32[32,1024]{1,0:T(8,128)S(1)}, u32[]{:S(2)}, u32[]{:S(2)}) collective-permute-start(f32[32,1024]{1,0:T(8,128)S(1)} %shard_map.70), channel_id=1, source_target_pairs={{8,16},{16,8},{12,20},{20,12},{9,17},{17,9},{13,21},{21,13},{10,18... | collective-permute-start | bytes 393224 | tf_op jit(solution)/shard_map/ppermute | solution.py:215
  12.4 7.9 %collective-permute-start.2 = (f32[32,1024]{1,0:T(8,128)S(1)}, f32[32,1024]{1,0:T(8,128)S(1)}, u32[]{:S(2)}, u32[]{:S(2)}) collective-permute-start(f32[32,1024]{1,0:T(8,128)S(1)} %shard_map.69), channel_id=1, source_target_pairs={{8,16},{16,8},{12,20},{20,12},{9,17},{17,9},{13,21},{21,13},{10,18... | collective-permute-start | bytes 393224 | tf_op jit(solution)/shard_map/ppermute | solution.py:215
  15.9 17.7 %collective-permute-start.11 = (f32[32,4096]{1,0:T(8,128)S(1)}, f32[32,4096]{1,0:T(8,128)S(1)}, u32[]{:S(2)}, u32[]{:S(2)}) collective-permute-start(f32[32,4096]{1,0:T(8,128)S(1)} %get-tuple-element.42), channel_id=1, source_target_pairs={{1,0},{2,1},{3,2},{0,3},{5,4},{6,5},{7,6},{4,7},{9,8},{10,9},{11,1... | collective-permute-start | bytes 1572872 | tf_op jit(solution)/shard_map/ppermute | solution.py:202
  18.4 7.5 %collective-permute-start.6 = (f32[32,1024]{1,0:T(8,128)S(1)}, f32[32,1024]{1,0:T(8,128)S(1)}, u32[]{:S(2)}, u32[]{:S(2)}) collective-permute-start(f32[32,1024]{1,0:T(8,128)S(1)} %collective-permute-done.5.refs_4_), channel_id=1, source_target_pairs={{16,24},{24,16},{20,28},{28,20},{17,25},{25,17},{21,29},{29,21},{1... | collective-permute-start | bytes 393224 | tf_op jit(solution)/shard_map/ppermute | solution.py:215
  20.4 7.0 %collective-permute-start.3 = (f32[32,1024]{1,0:T(8,128)S(1)}, f32[32,1024]{1,0:T(8,128)S(1)}, u32[]{:S(2)}, u32[]{:S(2)}) collective-permute-start(f32[32,1024]{1,0:T(8,128)S(1)} %collective-permute-done.2.refs_1_), channel_id=1, source_target_pairs={{16,24},{24,16},{20,28},{28,20},{17,25},{25,17},{21,29},{29,21},{1... | collective-permute-start | bytes 393224 | tf_op jit(solution)/shard_map/ppermute | solution.py:215
  27.5 1.8 %collective-permute-start.8 = (f32[32,2048]{1,0:T(8,128)S(1)}, f32[32,2048]{1,0:T(8,128)S(1)}, u32[]{:S(2)}, u32[]{:S(2)}) collective-permute-start(f32[32,2048]{1,0:T(8,128)S(1)} %get-tuple-element.33), channel_id=1, source_target_pairs={{0,4},{4,0},{8,12},{12,8},{16,20},{20,16},{24,28},{28,24},{1,5},{5... | collective-permute-start | bytes 786440 | tf_op jit(solution)/shard_map/ppermute | solution.py:226
  27.7 9.0 %collective-permute-start.12 = (f32[16,2048]{1,0:T(8,128)S(1)}, f32[16,2048]{1,0:T(8,128)S(1)}, u32[]{:S(2)}, u32[]{:S(2)}) collective-permute-start(f32[16,2048]{1,0:T(8,128)S(1)} %get-tuple-element.48), channel_id=1, source_target_pairs={{0,1},{1,2},{2,3},{3,0},{4,5},{5,6},{6,7},{7,4},{8,9},{9,10},{10,1... | collective-permute-start | bytes 393224 | tf_op jit(solution)/shard_map/ppermute | solution.py:225
  29.3 8.5 %collective-permute-start.13 = (f32[16,2048]{1,0:T(8,128)S(1)}, f32[16,2048]{1,0:T(8,128)S(1)}, u32[]{:S(2)}, u32[]{:S(2)}) collective-permute-start(f32[16,2048]{1,0:T(8,128)S(1)} %get-tuple-element.49), channel_id=1, source_target_pairs={{0,1},{1,2},{2,3},{3,0},{4,5},{5,6},{6,7},{7,4},{8,9},{9,10},{10,1... | collective-permute-start | bytes 393224 | tf_op jit(solution)/shard_map/ppermute | solution.py:231
  30.9 9.8 %collective-permute-start.7 = (f32[16,2048]{1,0:T(8,128)S(1)}, f32[16,2048]{1,0:T(8,128)S(1)}, u32[]{:S(2)}, u32[]{:S(2)}) collective-permute-start(f32[16,2048]{1,0:T(8,128)S(1)} %get-tuple-element.32), channel_id=1, source_target_pairs={{1,0},{2,1},{3,2},{0,3},{5,4},{6,5},{7,6},{4,7},{9,8},{10,9},{11,1... | collective-permute-start | bytes 393224 | tf_op jit(solution)/shard_map/ppermute | solution.py:225
  32.3 1.4 %copy-start.2 = (f32[1,16]{1,0:T(1,128)S(1)}, f32[1,16]{1,0:T(1,128)}, u32[]{:S(2)}) copy-start(f32[1,16]{1,0:T(1,128)} %param.9) | copy-start | bytes 196
  32.3 10.8 %collective-permute-start.10 = (f32[16,2048]{1,0:T(8,128)S(1)}, f32[16,2048]{1,0:T(8,128)S(1)}, u32[]{:S(2)}, u32[]{:S(2)}) collective-permute-start(f32[16,2048]{1,0:T(8,128)S(1)} %get-tuple-element.40), channel_id=1, source_target_pairs={{1,0},{2,1},{3,2},{0,3},{5,4},{6,5},{7,6},{4,7},{9,8},{10,9},{11,1... | collective-permute-start | bytes 393224 | tf_op jit(solution)/shard_map/ppermute | solution.py:231
  40.4 7.1 %collective-permute-start.15 = (f32[16,4096]{1,0:T(8,128)S(1)}, f32[16,4096]{1,0:T(8,128)S(1)}, u32[]{:S(2)}, u32[]{:S(2)}) collective-permute-start(f32[16,4096]{1,0:T(8,128)S(1)} %get-tuple-element.57.final_part), channel_id=1, source_target_pairs={{0,4},{4,8},{8,12},{12,16},{16,20},{20,24},{24,28},{28,0},{1,5},{5... | collective-permute-start | bytes 786440 | tf_op jit(solution)/shard_map/ppermute | solution.py:239
  45.6 7.7 %collective-permute-start.14 = (f32[16,4096]{1,0:T(8,128)S(1)}, f32[16,4096]{1,0:T(8,128)S(1)}, u32[]{:S(2)}, u32[]{:S(2)}) collective-permute-start(f32[16,4096]{1,0:T(8,128)S(1)} %get-tuple-element.56.final_part), channel_id=1, source_target_pairs={{0,4},{4,8},{8,12},{12,16},{16,20},{20,24},{24,28},{1,5},{5,9},{9,... | collective-permute-start | bytes 786440 | tf_op jit(solution)/shard_map/ppermute | solution.py:245

commit v6 on v5

--- a/solution.py
+++ b/solution.py
@@ -144,12 +144,16 @@
         part[:, columns_of(t)] = last[t, 2 * steps : steps + rows, :]
 
 
-def results_kernel(at, previous, own, other, final_part, *refs):
-    defect, final, difference, sems = refs[-4:]
+def results_kernel(at, copied, previous, own, other, *refs):
+    parts, (difference, sems) = refs[:copied], refs[-2:]
+    defect, *final = refs[copied:-2] if copied else refs[copied + 1 : -2]
     count, half = previous.shape[0], own.shape[1]
-    here = pl.ds(at, count)
-    kept = pltpu.make_async_copy(final_part, final.at[here], sems.at[0])
-    kept.start()
+    copies, below = [], 0
+    for part in parts:
+        height = part.shape[0]
+        copies.append(pltpu.make_async_copy(part, final[0].at[pl.ds(below, height)], sems.at[len(copies) + 1]))
+        copies[-1].start()
+        below += height
     is_first = lax.axis_index("tm") % 2 == 0
     follows = lax.axis_index("tm") > 0
     for low in range(0, half, LANES):
@@ -159,24 +163,27 @@
             (slice(half + low, half + low + LANES), jnp.where(is_first, b, a)),
         ):
             difference[:, cols] = start - jnp.where(follows, previous[:, cols], 0.0)
-    made = pltpu.make_async_copy(difference, defect.at[here], sems.at[1])
-    made.start()
-    kept.wait()
-    made.wait()
-
-
-def write_results(at, previous, own, other, final_part, earlier):
+    copies.append(pltpu.make_async_copy(difference, defect.at[pl.ds(at, count)], sems.at[0]))
+    copies[-1].start()
+    for copy in copies:
+        copy.wait()
+
+
+def write_results(at, previous, own, other, parts=(), defect=None):
     shape = (own.shape[0], 2 * own.shape[1])
     hbm = pl.BlockSpec(memory_space=pltpu.HBM)
+    earlier = () if defect is None else (defect,)
+    results = 2 if parts else 1
+    in_vmem = (previous, own, other, *parts)
     return pl.pallas_call(
-        functools.partial(results_kernel, at),
-        out_shape=(pltpu.HBM(shape, jnp.float32),) * 2,
-        in_specs=[VMEM] * 4 + [hbm] * len(earlier),
-        out_specs=(hbm, hbm),
-        scratch_shapes=[pltpu.VMEM(previous.shape, jnp.float32), pltpu.SemaphoreType.DMA((2,))],
-        input_output_aliases={4 + i: i for i in range(len(earlier))},
+        functools.partial(results_kernel, at, len(parts)),
+        out_shape=(pltpu.HBM(shape, jnp.float32),) * results,
+        in_specs=[VMEM] * len(in_vmem) + [hbm] * len(earlier),
+        out_specs=(hbm,) * results,
+        scratch_shapes=[pltpu.VMEM(previous.shape, jnp.float32), pltpu.SemaphoreType.DMA((1 + len(parts),))],
+        input_output_aliases={len(in_vmem): 0} if earlier else {},
         compiler_params=pltpu.CompilerParams(vmem_limit_bytes=4 * 2**20),
-    )(*(pltpu.with_memory_space_constraint(v, pltpu.VMEM) for v in (previous, own, other, final_part)), *earlier)
+    )(*(pltpu.with_memory_space_constraint(v, pltpu.VMEM) for v in in_vmem), *earlier)
 
 
 def on_device(control, scales, courant, diffusion, pacing):
@@ -211,8 +218,8 @@
     totals = [call(sum_kernel, [part.shape], (part, more))[0] for part, (more,) in zip(parts, brought)]
     carried = totals
     for hop in range(1, chips - 1):
-        swap = [(i + 2 * a, i + 2 * b) for i in range(2) for a, b in ((hop, hop + 1), (hop + 1, hop))]
-        moved = [lax.ppermute(part, "tm", swap) for part in carried]
+        step = [(2 * hop + i, 2 * hop + 2 + i) for i in range(2)]
+        moved = [lax.ppermute(part, "tm", step) for part in carried]
         for earlier, more in zip(brought, moved):
             earlier.append(more)
         carried = moved if hop % 2 else [
@@ -223,8 +230,8 @@
         functools.partial(prefix_kernel, PIECES, steps), [own.shape, own.shape, edge, edge],
         (own, pair, *(v for earlier in brought for v in earlier)))
     south_own, north_own = lax.ppermute(to_onward, "lat", onward), lax.ppermute(to_backward, "lat", backward)
+    send, c_all, d_all = lax.optimization_barrier((send, c_all, d_all))
     arrived = lax.ppermute(send, "tm", partner)
-    arrived, c_all, d_all = lax.optimization_barrier((arrived, c_all, d_all))
     c_all, coef_north = lax.optimization_barrier((c_all, coef_north))
     start_other, to_onward, to_backward = call(
         functools.partial(halo_kernel, steps), [own.shape, edge, edge], (other, arrived))
@@ -243,8 +250,8 @@
         functools.partial(north_kernel, steps), [field, field, (rows - steps, columns)],
         (paces, north_own, north_other, c_all, d_all, even, odd), {5: 0, 6: 1}, work=work)
     previous_north = lax.ppermute(final_north, "tm", following[:-1])
-    results = write_results(0, previous_south, start_own, start_other, final_south, ())
-    defect, final = write_results(steps, previous_north, start_own, start_other, final_north, results)
+    defect, final = write_results(0, previous_south, start_own, start_other, (final_south, final_north))
+    (defect,) = write_results(steps, previous_north, start_own, start_other, defect=defect)
     return defect[None], final[None]
 
 

time: 54.3 us -> 52.1 us (0.959); the launches traced: 54.1 us -> 51.3 us
  starting transfers between devices: 25.8 us -> 19.6 us
  waiting for transfers between devices: 15.9 us -> 18.2 us
  local copies, waits for them, and re-layouts: 0.1 us -> 1.16 us
    ppermute x4, starting transfers between devices: 11.7 us -> 5.16 us  [on_device(): moved = [lax.ppermute(part, 'tm', step) for part in carried]]
    ppermute x4, waiting for transfers between devices: 3.07 us -> 5.14 us  [on_device(): moved = [lax.ppermute(part, 'tm', step) for part in carried]]
    ppermute x2, waiting for transfers between devices: 2.69 us -> 4.42 us  [on_device(): lax.ppermute(part, 'tm', [(i, i ^ 2) for i in range(windows)])]
    ppermute x1, waiting for transfers between devices: 1.52 us -> 0.01 us  [on_device(): lax.ppermute(other, 'tm', partner)]
    unnamed x6, local copies, waits for them, and re-layouts: 0.01 us -> 1.07 us
  transfers between devices with their start and end apart: 16 -> 16, of which waited for: 8 -> 10; matrix products, arithmetic and copies ran while one was open for 0% -> 0% of each run, Pallas kernels for 17% -> 18%
where the time goes in v6:
time: 52.1 us; the launch traced here: 51.3 us
  starting transfers between devices  19.6 us (38%)
  waiting for transfers between devices  18.2 us (35%)
  Pallas kernels  10.2 us (20%)
  other arithmetic  1.29 us (2%)
  local copies, waits for them, and re-layouts  1.16 us (2%)
  between operations  0.85 us (2%)
    pallas_call x12, Pallas kernels, call(): pl.pallas_call(kernel, out_shape=tuple((pltpu.VMEM(shape, jnp.float32) fo...  8.55 us
    ppermute x3, starting transfers between devices, on_device(): lax.ppermute(to_backward, 'lat', backward)  5.61 us
    ppermute x4, starting transfers between devices, on_device(): moved = [lax.ppermute(part, 'tm', step) for part in carried]  5.16 us
    ppermute x4, waiting for transfers between devices, on_device(): moved = [lax.ppermute(part, 'tm', step) for part in carried]  5.14 us
    ppermute x1, waiting for transfers between devices, on_device(): previous_north = lax.ppermute(final_north, 'tm', following[:-1])  4.84 us
    ppermute x3, starting transfers between devices, on_device(): lax.ppermute(to_onward, 'lat', onward)  4.63 us
    ppermute x2, waiting for transfers between devices, on_device(): lax.ppermute(part, 'tm', [(i, i ^ 2) for i in range(windows)])  4.42 us
    ppermute x3, waiting for transfers between devices, on_device(): lax.ppermute(to_backward, 'lat', backward)  2.53 us
  transfers between devices with their start and end apart: 16, of which 10 were waited for; matrix products, arithmetic and copies ran while one was open for 0% of the time, Pallas kernels for 18%

profile of v6, /device:TPU:16, one launch (start us, length us, event | category | flops | bytes accessed | tf_op | source)
XLA Modules:
  0.0 51.3 jit_solution(3092710324882051546)
XLA Ops:
  0.6 1.3 %multiply_bitcast_fusion = f32[32,4096]{1,0:T(8,128)S(1)} fusion(f32[1,32,4096]{2,1,0:T(8,128)} %param.6, f32[1,32,4096]{2,1,0:T(8,128)} %param.5), kind=kLoop, calls=%fused_computation | loop fusion | flops 131072 | bytes 1572864 | tf_op jit(solution)/shard_map/mul | solution.py:202
  1.9 0.0 copy-start
  1.9 0.0 copy-start.1
  2.0 0.1 collective-permute-start
  2.0 0.9 %copy-done = f32[1,32,4096]{2,1,0:T(8,128)S(1)} copy-done((f32[1,32,4096]{2,1,0:T(8,128)S(1)}, f32[1,32,4096]{2,1,0:T(8,128)}, u32[]{:S(2)}) %copy-start) | copy-done | bytes 524312
  2.9 0.2 copy-done.1
  3.1 0.1 shard_map.72
  3.2 1.5 %collective-permute-start.8 = (f32[32,4096]{1,0:T(8,128)S(1)}, f32[32,4096]{1,0:T(8,128)S(1)}, u32[]{:S(2)}, u32[]{:S(2)}) collective-permute-start(f32[32,4096]{1,0:T(8,128)S(1)} %get-tuple-element.32), channel_id=1, source_target_pairs={{0,1},{1,2},{2,3},{3,0},{4,5},{5,6},{6,7},{7,4},{8,9},{9,10},{10,1... | collective-permute-start | bytes 1572872 | tf_op jit(solution)/shard_map/ppermute | solution.py:209
  4.7 0.0 collective-permute-done.b
  4.8 1.6 %collective-permute-start.4 = (f32[32,1024]{1,0:T(8,128)S(1)}, f32[32,1024]{1,0:T(8,128)S(1)}, u32[]{:S(2)}, u32[]{:S(2)}) collective-permute-start(f32[32,1024]{1,0:T(8,128)S(1)} %get-tuple-element.60.a), channel_id=1, source_target_pairs={{0,8},{4,12},{8,0},{12,4},{16,24},{20,28},{24,16},{28,20},{1,9},{5... | collective-permute-start | bytes 393224 | tf_op jit(solution)/shard_map/ppermute | solution.py:217
  6.4 0.4 collective-permute-start.1
  6.9 4.3 %collective-permute-done.4.b.refs_3_ = f32[32,1024]{1,0:T(8,128)S(1)} collective-permute-done((f32[32,1024]{1,0:T(8,128)S(1)}, f32[32,1024]{1,0:T(8,128)S(1)}, u32[]{:S(2)}, u32[]{:S(2)}) %collective-permute-start.4) | collective-permute-done | bytes 131104 | tf_op jit(solution)/shard_map/ppermute | solution.py:217
  11.2 1.3 %collective-permute-start.5 = (f32[32,1024]{1,0:T(8,128)S(1)}, f32[32,1024]{1,0:T(8,128)S(1)}, u32[]{:S(2)}, u32[]{:S(2)}) collective-permute-start(f32[32,1024]{1,0:T(8,128)S(1)} %shard_map.70), channel_id=1, source_target_pairs={{8,16},{12,20},{9,17},{13,21},{10,18},{14,22},{11,19},{15,23}} | collective-permute-start | bytes 393224 | tf_op jit(solution)/shard_map/ppermute | solution.py:222
  12.5 0.1 collective-permute-done.1.b.refs_0_
  12.6 1.3 %collective-permute-start.2 = (f32[32,1024]{1,0:T(8,128)S(1)}, f32[32,1024]{1,0:T(8,128)S(1)}, u32[]{:S(2)}, u32[]{:S(2)}) collective-permute-start(f32[32,1024]{1,0:T(8,128)S(1)} %shard_map.69), channel_id=1, source_target_pairs={{8,16},{12,20},{9,17},{13,21},{10,18},{14,22},{11,19},{15,23}} | collective-permute-start | bytes 393224 | tf_op jit(solution)/shard_map/ppermute | solution.py:222
  13.9 1.9 %collective-permute-start.11 = (f32[32,4096]{1,0:T(8,128)S(1)}, f32[32,4096]{1,0:T(8,128)S(1)}, u32[]{:S(2)}, u32[]{:S(2)}) collective-permute-start(f32[32,4096]{1,0:T(8,128)S(1)} %get-tuple-element.40), channel_id=1, source_target_pairs={{1,0},{2,1},{3,2},{0,3},{5,4},{6,5},{7,6},{4,7},{9,8},{10,9},{11,1... | collective-permute-start | bytes 1572872 | tf_op jit(solution)/shard_map/ppermute | solution.py:209
  15.9 2.7 %collective-permute-done.5.refs_4_ = f32[32,1024]{1,0:T(8,128)S(1)} collective-permute-done((f32[32,1024]{1,0:T(8,128)S(1)}, f32[32,1024]{1,0:T(8,128)S(1)}, u32[]{:S(2)}, u32[]{:S(2)}) %collective-permute-start.5) | collective-permute-done | bytes 131104 | tf_op jit(solution)/shard_map/ppermute | solution.py:222
  18.6 1.3 %collective-permute-start.6 = (f32[32,1024]{1,0:T(8,128)S(1)}, f32[32,1024]{1,0:T(8,128)S(1)}, u32[]{:S(2)}, u32[]{:S(2)}) collective-permute-start(f32[32,1024]{1,0:T(8,128)S(1)} %collective-permute-done.5.refs_4_), channel_id=1, source_target_pairs={{16,24},{20,28},{17,25},{21,29},{18,26},{22,30},{19,27},{23,31}} | collective-permute-start | bytes 393224 | tf_op jit(solution)/shard_map/ppermute | solution.py:222
  19.9 0.1 collective-permute-done.2.refs_1_
  20.0 1.3 %collective-permute-start.3 = (f32[32,1024]{1,0:T(8,128)S(1)}, f32[32,1024]{1,0:T(8,128)S(1)}, u32[]{:S(2)}, u32[]{:S(2)}) collective-permute-start(f32[32,1024]{1,0:T(8,128)S(1)} %collective-permute-done.2.refs_1_), channel_id=1, source_target_pairs={{16,24},{20,28},{17,25},{21,29},{18,26},{22,30},{19,27},{23,31}} | collective-permute-start | bytes 393224 | tf_op jit(solution)/shard_map/ppermute | solution.py:222
  21.3 0.1 shard_map.73
  21.4 0.0 collective-permute-done.8.side
  21.4 0.1 shard_map.74
  21.4 0.9 %collective-permute-done.6.refs_5_ = f32[32,1024]{1,0:T(8,128)S(1)} collective-permute-done((f32[32,1024]{1,0:T(8,128)S(1)}, f32[32,1024]{1,0:T(8,128)S(1)}, u32[]{:S(2)}, u32[]{:S(2)}) %collective-permute-start.6) | collective-permute-done | bytes 131104 | tf_op jit(solution)/shard_map/ppermute | solution.py:222
  22.4 1.4 %collective-permute-done.3.refs_2_ = f32[32,1024]{1,0:T(8,128)S(1)} collective-permute-done((f32[32,1024]{1,0:T(8,128)S(1)}, f32[32,1024]{1,0:T(8,128)S(1)}, u32[]{:S(2)}, u32[]{:S(2)}) %collective-permute-start.3) | collective-permute-done | bytes 131104 | tf_op jit(solution)/shard_map/ppermute | solution.py:222
  23.8 0.1 shard_map.71
  23.9 0.1 collective-permute-start.9
  24.0 1.5 %collective-permute-start.12 = (f32[16,2048]{1,0:T(8,128)S(1)}, f32[16,2048]{1,0:T(8,128)S(1)}, u32[]{:S(2)}, u32[]{:S(2)}) collective-permute-start(f32[16,2048]{1,0:T(8,128)S(1)} %get-tuple-element.46), channel_id=1, source_target_pairs={{0,1},{1,2},{2,3},{3,0},{4,5},{5,6},{6,7},{7,4},{8,9},{9,10},{10,1... | collective-permute-start | bytes 393224 | tf_op jit(solution)/shard_map/ppermute | solution.py:232
  25.5 0.0 collective-permute-done.9.arrived
  25.6 1.5 %collective-permute-start.13 = (f32[16,2048]{1,0:T(8,128)S(1)}, f32[16,2048]{1,0:T(8,128)S(1)}, u32[]{:S(2)}, u32[]{:S(2)}) collective-permute-start(f32[16,2048]{1,0:T(8,128)S(1)} %get-tuple-element.47), channel_id=1, source_target_pairs={{0,1},{1,2},{2,3},{3,0},{4,5},{5,6},{6,7},{7,4},{8,9},{9,10},{10,1... | collective-permute-start | bytes 393224 | tf_op jit(solution)/shard_map/ppermute | solution.py:238
  27.1 1.7 %collective-permute-start.7 = (f32[16,2048]{1,0:T(8,128)S(1)}, f32[16,2048]{1,0:T(8,128)S(1)}, u32[]{:S(2)}, u32[]{:S(2)}) collective-permute-start(f32[16,2048]{1,0:T(8,128)S(1)} %get-tuple-element.30), channel_id=1, source_target_pairs={{1,0},{2,1},{3,2},{0,3},{5,4},{6,5},{7,6},{4,7},{9,8},{10,9},{11,1... | collective-permute-start | bytes 393224 | tf_op jit(solution)/shard_map/ppermute | solution.py:232
  28.8 2.0 %collective-permute-start.10 = (f32[16,2048]{1,0:T(8,128)S(1)}, f32[16,2048]{1,0:T(8,128)S(1)}, u32[]{:S(2)}, u32[]{:S(2)}) collective-permute-start(f32[16,2048]{1,0:T(8,128)S(1)} %get-tuple-element.38), channel_id=1, source_target_pairs={{1,0},{2,1},{3,2},{0,3},{5,4},{6,5},{7,6},{4,7},{9,8},{10,9},{11,1... | collective-permute-start | bytes 393224 | tf_op jit(solution)/shard_map/ppermute | solution.py:238
  30.8 0.0 collective-permute-done.11.side
  30.8 0.1 broadcast_in_dim.14.paces
  30.9 3.0 %shard_map.77 = (f32[32,64,128]{2,1,0:T(8,128)S(1)}, f32[32,64,128]{2,1,0:T(8,128)S(1)}) custom-call(f32[16,128]{1,0:T(8,128)S(1)} %broadcast_in_dim.14.paces, f32[32,2048]{1,0:T(8,128)S(1)} %get-tuple-element.48.own, f32[32,2048]{1,0:T(8,128)S(1)} %get-tuple-element.49.other, f32[32,64,128]{2,1,0:T(8,128)S(1)} %get-tuple-element.42.c_in.c_all, ...), custom_call_target="tpu_custom_call" | custom-call | flops 16777216 | tf_op jit(solution)/shard_map/pallas_call | solution.py:16
  33.9 0.0 collective-permute-done.12.own
  33.9 1.2 %collective-permute-done.13.other = f32[16,2048]{1,0:T(8,128)S(1)} collective-permute-done((f32[16,2048]{1,0:T(8,128)S(1)}, f32[16,2048]{1,0:T(8,128)S(1)}, u32[]{:S(2)}, u32[]{:S(2)}) %collective-permute-start.13) | collective-permute-done | bytes 131104 | tf_op jit(solution)/shard_map/ppermute | solution.py:238
  35.1 2.5 %shard_map.78 = (f32[32,64,128]{2,1,0:T(8,128)S(1)}, f32[32,64,128]{2,1,0:T(8,128)S(1)}, f32[16,4096]{1,0:T(8,128)S(1)}) custom-call(f32[16,128]{1,0:T(8,128)S(1)} %broadcast_in_dim.14.paces, f32[16,2048]{1,0:T(8,128)S(1)} %collective-permute-done.12.own, ...), custom_call_target="tpu_custom_call", output_to_operand_aliasing={{0}: (5, {}), {1}: (6, {})} | custom-call | flops 16777216 | tf_op jit(solution)/shard_map/pallas_call | solution.py:16
  37.6 0.1 shard_map.76
  37.7 0.1 collective-permute-start.15
  37.8 0.7 %collective-permute-done.7.own = f32[16,2048]{1,0:T(8,128)S(1)} collective-permute-done((f32[16,2048]{1,0:T(8,128)S(1)}, f32[16,2048]{1,0:T(8,128)S(1)}, u32[]{:S(2)}, u32[]{:S(2)}) %collective-permute-start.7) | collective-permute-done | bytes 131104 | tf_op jit(solution)/shard_map/ppermute | solution.py:232
  38.5 1.8 %collective-permute-done.10.other = f32[16,2048]{1,0:T(8,128)S(1)} collective-permute-done((f32[16,2048]{1,0:T(8,128)S(1)}, f32[16,2048]{1,0:T(8,128)S(1)}, u32[]{:S(2)}, u32[]{:S(2)}) %collective-permute-start.10) | collective-permute-done | bytes 131104 | tf_op jit(solution)/shard_map/ppermute | solution.py:238
  40.3 2.5 %shard_map.79 = (f32[32,64,128]{2,1,0:T(8,128)S(1)}, f32[32,64,128]{2,1,0:T(8,128)S(1)}, f32[16,4096]{1,0:T(8,128)S(1)}) custom-call(f32[16,128]{1,0:T(8,128)S(1)} %broadcast_in_dim.14.paces, f32[16,2048]{1,0:T(8,128)S(1)} %collective-permute-done.7.own, f32[16,2048]{1,0:T(8,128)S(1)} %collective-permute-done.10.other, ...), custom_call_target="tpu_custom_call", output_to_operand_aliasing={{0}: (5, {}), {1}: (6, {})} | custom-call | flops 16777216 | tf_op jit(solution)/shard_map/pallas_call | solution.py:16
  42.8 1.9 %collective-permute-start.14 = (f32[16,4096]{1,0:T(8,128)S(1)}, f32[16,4096]{1,0:T(8,128)S(1)}, u32[]{:S(2)}, u32[]{:S(2)}) collective-permute-start(f32[16,4096]{1,0:T(8,128)S(1)} %get-tuple-element.54.refs_1_), channel_id=1, source_target_pairs={{0,4},{4,8},{8,12},{12,16},{16,20},{20,24},{24,28},{1,5},{5,9},{9,... | collective-permute-start | bytes 786440 | tf_op jit(solution)/shard_map/ppermute | solution.py:252
  44.8 0.0 collective-permute-done.15.previous
  44.8 0.9 %shard_map.80 = (f32[32,4096]{1,0:T(8,128)}, f32[32,4096]{1,0:T(8,128)}) custom-call(f32[16,4096]{1,0:T(8,128)S(1)} %collective-permute-done.15.previous, f32[32,2048]{1,0:T(8,128)S(1)} %get-tuple-element.48.own, f32[32,2048]{1,0:T(8,128)S(1)} %get-tuple-element.49.other, f32[16,4096]{1,0:T(8,128)S(1)} %get-tuple-element.55.refs_0_, ...), custom_call_target="tpu_custom_call" | custom-call | tf_op jit(solution)/shard_map/pallas_call | solution.py:178
  45.7 4.8 %collective-permute-done.14.previous = f32[16,4096]{1,0:T(8,128)S(1)} collective-permute-done((f32[16,4096]{1,0:T(8,128)S(1)}, f32[16,4096]{1,0:T(8,128)S(1)}, u32[]{:S(2)}, u32[]{:S(2)}) %collective-permute-start.14) | collective-permute-done | bytes 262176 | tf_op jit(solution)/shard_map/ppermute | solution.py:252
  50.5 0.7 %shard_map.81 = f32[32,4096]{1,0:T(8,128)} custom-call(f32[16,4096]{1,0:T(8,128)S(1)} %collective-permute-done.14.previous, f32[32,2048]{1,0:T(8,128)S(1)} %get-tuple-element.48.own, f32[32,2048]{1,0:T(8,128)S(1)} %get-tuple-element.49.other, f32[32,4096]{1,0:T(8,128)} %get-tuple-element.56.refs_0_), custom_call_target="tpu_custom_call", output_to_operand_aliasing={{}: (3, {})} | custom-call | tf_op jit(solution)/shard_map/pallas_call | solution.py:178
  (8 shorter events, 0.2 us)
Async XLA Ops:
  1.9 1.0 %copy-start = (f32[1,32,4096]{2,1,0:T(8,128)S(1)}, f32[1,32,4096]{2,1,0:T(8,128)}, u32[]{:S(2)}) copy-start(f32[1,32,4096]{2,1,0:T(8,128)} %param.7) | copy-start | bytes 1572868
  1.9 1.2 %copy-start.1 = (f32[1,32,4096]{2,1,0:T(8,128)S(1)}, f32[1,32,4096]{2,1,0:T(8,128)}, u32[]{:S(2)}) copy-start(f32[1,32,4096]{2,1,0:T(8,128)} %param.8) | copy-start | bytes 1572868
  2.0 2.8 %collective-permute-start = (f32[32,2048]{1,0:T(8,128)S(1)}, f32[32,2048]{1,0:T(8,128)S(1)}, u32[]{:S(2)}, u32[]{:S(2)}) collective-permute-start(f32[32,2048]{1,0:T(8,128)S(1)} %get-tuple-element.58.other), channel_id=1, source_target_pairs={{0,4},{4,0},{8,12},{12,8},{16,20},{20,16},{24,28},{28,24},{1,5},{5... | collective-permute-start | bytes 786440 | tf_op jit(solution)/shard_map/ppermute | solution.py:214
  3.2 18.2 %collective-permute-start.8 = (f32[32,4096]{1,0:T(8,128)S(1)}, f32[32,4096]{1,0:T(8,128)S(1)}, u32[]{:S(2)}, u32[]{:S(2)}) collective-permute-start(f32[32,4096]{1,0:T(8,128)S(1)} %get-tuple-element.32), channel_id=1, source_target_pairs={{0,1},{1,2},{2,3},{3,0},{4,5},{5,6},{6,7},{7,4},{8,9},{9,10},{10,1... | collective-permute-start | bytes 1572872 | tf_op jit(solution)/shard_map/ppermute | solution.py:209
  4.8 6.4 %collective-permute-start.4 = (f32[32,1024]{1,0:T(8,128)S(1)}, f32[32,1024]{1,0:T(8,128)S(1)}, u32[]{:S(2)}, u32[]{:S(2)}) collective-permute-start(f32[32,1024]{1,0:T(8,128)S(1)} %get-tuple-element.60.a), channel_id=1, source_target_pairs={{0,8},{4,12},{8,0},{12,4},{16,24},{20,28},{24,16},{28,20},{1,9},{5... | collective-permute-start | bytes 393224 | tf_op jit(solution)/shard_map/ppermute | solution.py:217
  6.4 6.2 %collective-permute-start.1 = (f32[32,1024]{1,0:T(8,128)S(1)}, f32[32,1024]{1,0:T(8,128)S(1)}, u32[]{:S(2)}, u32[]{:S(2)}) collective-permute-start(f32[32,1024]{1,0:T(8,128)S(1)} %get-tuple-element.61.a), channel_id=1, source_target_pairs={{0,8},{4,12},{8,0},{12,4},{16,24},{20,28},{24,16},{28,20},{1,9},{5... | collective-permute-start | bytes 393224 | tf_op jit(solution)/shard_map/ppermute | solution.py:217
  11.2 7.3 %collective-permute-start.5 = (f32[32,1024]{1,0:T(8,128)S(1)}, f32[32,1024]{1,0:T(8,128)S(1)}, u32[]{:S(2)}, u32[]{:S(2)}) collective-permute-start(f32[32,1024]{1,0:T(8,128)S(1)} %shard_map.70), channel_id=1, source_target_pairs={{8,16},{12,20},{9,17},{13,21},{10,18},{14,22},{11,19},{15,23}} | collective-permute-start | bytes 393224 | tf_op jit(solution)/shard_map/ppermute | solution.py:222
  12.6 7.3 %collective-permute-start.2 = (f32[32,1024]{1,0:T(8,128)S(1)}, f32[32,1024]{1,0:T(8,128)S(1)}, u32[]{:S(2)}, u32[]{:S(2)}) collective-permute-start(f32[32,1024]{1,0:T(8,128)S(1)} %shard_map.69), channel_id=1, source_target_pairs={{8,16},{12,20},{9,17},{13,21},{10,18},{14,22},{11,19},{15,23}} | collective-permute-start | bytes 393224 | tf_op jit(solution)/shard_map/ppermute | solution.py:222
  13.9 16.9 %collective-permute-start.11 = (f32[32,4096]{1,0:T(8,128)S(1)}, f32[32,4096]{1,0:T(8,128)S(1)}, u32[]{:S(2)}, u32[]{:S(2)}) collective-permute-start(f32[32,4096]{1,0:T(8,128)S(1)} %get-tuple-element.40), channel_id=1, source_target_pairs={{1,0},{2,1},{3,2},{0,3},{5,4},{6,5},{7,6},{4,7},{9,8},{10,9},{11,1... | collective-permute-start | bytes 1572872 | tf_op jit(solution)/shard_map/ppermute | solution.py:209
  18.6 3.8 %collective-permute-start.6 = (f32[32,1024]{1,0:T(8,128)S(1)}, f32[32,1024]{1,0:T(8,128)S(1)}, u32[]{:S(2)}, u32[]{:S(2)}) collective-permute-start(f32[32,1024]{1,0:T(8,128)S(1)} %collective-permute-done.5.refs_4_), channel_id=1, source_target_pairs={{16,24},{20,28},{17,25},{21,29},{18,26},{22,30},{19,27},{23,31}} | collective-permute-start | bytes 393224 | tf_op jit(solution)/shard_map/ppermute | solution.py:222
  20.0 3.8 %collective-permute-start.3 = (f32[32,1024]{1,0:T(8,128)S(1)}, f32[32,1024]{1,0:T(8,128)S(1)}, u32[]{:S(2)}, u32[]{:S(2)}) collective-permute-start(f32[32,1024]{1,0:T(8,128)S(1)} %collective-permute-done.2.refs_1_), channel_id=1, source_target_pairs={{16,24},{20,28},{17,25},{21,29},{18,26},{22,30},{19,27},{23,31}} | collective-permute-start | bytes 393224 | tf_op jit(solution)/shard_map/ppermute | solution.py:222
  23.9 1.6 %collective-permute-start.9 = (f32[32,2048]{1,0:T(8,128)S(1)}, f32[32,2048]{1,0:T(8,128)S(1)}, u32[]{:S(2)}, u32[]{:S(2)}) collective-permute-start(f32[32,2048]{1,0:T(8,128)S(1)} %get-tuple-element.37), channel_id=1, source_target_pairs={{0,4},{4,0},{8,12},{12,8},{16,20},{20,16},{24,28},{28,24},{1,5},{5... | collective-permute-start | bytes 786440 | tf_op jit(solution)/shard_map/ppermute | solution.py:234
  24.0 9.9 %collective-permute-start.12 = (f32[16,2048]{1,0:T(8,128)S(1)}, f32[16,2048]{1,0:T(8,128)S(1)}, u32[]{:S(2)}, u32[]{:S(2)}) collective-permute-start(f32[16,2048]{1,0:T(8,128)S(1)} %get-tuple-element.46), channel_id=1, source_target_pairs={{0,1},{1,2},{2,3},{3,0},{4,5},{5,6},{6,7},{7,4},{8,9},{9,10},{10,1... | collective-permute-start | bytes 393224 | tf_op jit(solution)/shard_map/ppermute | solution.py:232
  25.6 9.6 %collective-permute-start.13 = (f32[16,2048]{1,0:T(8,128)S(1)}, f32[16,2048]{1,0:T(8,128)S(1)}, u32[]{:S(2)}, u32[]{:S(2)}) collective-permute-start(f32[16,2048]{1,0:T(8,128)S(1)} %get-tuple-element.47), channel_id=1, source_target_pairs={{0,1},{1,2},{2,3},{3,0},{4,5},{5,6},{6,7},{7,4},{8,9},{9,10},{10,1... | collective-permute-start | bytes 393224 | tf_op jit(solution)/shard_map/ppermute | solution.py:238
  27.1 11.4 %collective-permute-start.7 = (f32[16,2048]{1,0:T(8,128)S(1)}, f32[16,2048]{1,0:T(8,128)S(1)}, u32[]{:S(2)}, u32[]{:S(2)}) collective-permute-start(f32[16,2048]{1,0:T(8,128)S(1)} %get-tuple-element.30), channel_id=1, source_target_pairs={{1,0},{2,1},{3,2},{0,3},{5,4},{6,5},{7,6},{4,7},{9,8},{10,9},{11,1... | collective-permute-start | bytes 393224 | tf_op jit(solution)/shard_map/ppermute | solution.py:232
  28.8 2.0 %copy-start.2 = (f32[1,16]{1,0:T(1,128)S(1)}, f32[1,16]{1,0:T(1,128)}, u32[]{:S(2)}) copy-start(f32[1,16]{1,0:T(1,128)} %param.9) | copy-start | bytes 196
  28.8 11.5 %collective-permute-start.10 = (f32[16,2048]{1,0:T(8,128)S(1)}, f32[16,2048]{1,0:T(8,128)S(1)}, u32[]{:S(2)}, u32[]{:S(2)}) collective-permute-start(f32[16,2048]{1,0:T(8,128)S(1)} %get-tuple-element.38), channel_id=1, source_target_pairs={{1,0},{2,1},{3,2},{0,3},{5,4},{6,5},{7,6},{4,7},{9,8},{10,9},{11,1... | collective-permute-start | bytes 393224 | tf_op jit(solution)/shard_map/ppermute | solution.py:238
  37.7 7.0 %collective-permute-start.15 = (f32[16,4096]{1,0:T(8,128)S(1)}, f32[16,4096]{1,0:T(8,128)S(1)}, u32[]{:S(2)}, u32[]{:S(2)}) collective-permute-start(f32[16,4096]{1,0:T(8,128)S(1)} %get-tuple-element.55.refs_0_), channel_id=1, source_target_pairs={{0,4},{4,8},{8,12},{12,16},{16,20},{20,24},{24,28},{28,0},{1,5},{5... | collective-permute-start | bytes 786440 | tf_op jit(solution)/shard_map/ppermute | solution.py:246
  42.8 7.7 %collective-permute-start.14 = (f32[16,4096]{1,0:T(8,128)S(1)}, f32[16,4096]{1,0:T(8,128)S(1)}, u32[]{:S(2)}, u32[]{:S(2)}) collective-permute-start(f32[16,4096]{1,0:T(8,128)S(1)} %get-tuple-element.54.refs_1_), channel_id=1, source_target_pairs={{0,4},{4,8},{8,12},{12,16},{16,20},{20,24},{24,28},{1,5},{5,9},{9,... | collective-permute-start | bytes 786440 | tf_op jit(solution)/shard_map/ppermute | solution.py:252

commit v7 on v6

--- a/solution.py
+++ b/solution.py
@@ -45,15 +45,21 @@
         old, new = old_and_new if step % 2 else old_and_new[::-1]
         pace = paces[step - 1 : step, :]
         lane = lax.broadcasted_iota(jnp.int32, (stop - first, LANES), 1)
+
+        def eastward(t):
+            x = old[t, first:stop, :]
+            return x, pltpu.roll(jnp.where(lane == 0, old[(t + 1) % tiles, first:stop, :], x), LANES - 1, 1) - x
+
+        _, west_of = eastward((step - 1) % tiles)
         for t in ((step + i) % tiles for i in range(tiles)):
-            x = old[t, first:stop, :]
-            east = pltpu.roll(jnp.where(lane == 0, old[(t + 1) % tiles, first:stop, :], x), LANES - 1, 1)
-            west = pltpu.roll(jnp.where(lane == LANES - 1, old[(t - 1) % tiles, first:stop, :], x), 1, 1)
+            x, east = eastward(t)
+            west = pltpu.roll(jnp.where(lane == LANES - 1, west_of, east), 1, 1)
+            west_of = east
             ahead = old[t, first + 1 : stop + 1, :] - x
             behind = x - old[t, first - 1 : stop - 1, :]
             c = c_all[t, first:stop, :]
             d = d_all[t, first:stop, :]
-            spread = ((east - x) + (west - x)) + (ahead - behind)
+            spread = (east - west) + (ahead - behind)
             new[t, first:stop, :] = x + (d * pace) * spread - c * jnp.where(c > 0, behind, ahead)
 
 

time: 52.1 us -> 75.3 us (1.45)
  Pallas kernels: 10.2 us -> 36.2 us
  waiting for transfers between devices: 18.2 us -> 11.9 us
  starting transfers between devices: 19.6 us -> 22.3 us
    pallas_call x12, Pallas kernels: 8.55 us -> 34.6 us  [call(): pl.pallas_call(kernel, out_shape=tuple((pltpu.VMEM(shape, jnp.float32) fo...]
    ppermute x1, starting transfers between devices: 1.92 us -> 4.47 us  [on_device(): previous_north = lax.ppermute(final_north, 'tm', following[:-1])]
    ppermute x1, waiting for transfers between devices: 4.84 us -> 2.29 us  [on_device(): previous_north = lax.ppermute(final_north, 'tm', following[:-1])]
    ppermute x3, waiting for transfers between devices: 2.53 us -> 0.01 us  [on_device(): lax.ppermute(to_backward, 'lat', backward)]
    ppermute x3, waiting for transfers between devices: 1.22 us -> 0.01 us  [on_device(): lax.ppermute(to_onward, 'lat', onward)]
  transfers between devices with their start and end apart: 16 -> 16, of which waited for: 10 -> 7; matrix products, arithmetic and copies ran while one was open for 0% -> 0% of each run, Pallas kernels for 18% -> 48%
where the time goes in v7:
time: 75.3 us; the launch traced here: 73.9 us
  Pallas kernels  36.2 us (48%)
  starting transfers between devices  22.3 us (30%)
  waiting for transfers between devices  11.9 us (16%)
  other arithmetic  1.29 us (2%)
  local copies, waits for them, and re-layouts  1.16 us (2%)
  between operations  1.04 us (1%)
    pallas_call x12, Pallas kernels, call(): pl.pallas_call(kernel, out_shape=tuple((pltpu.VMEM(shape, jnp.float32) fo...  34.6 us
    ppermute x3, starting transfers between devices, on_device(): lax.ppermute(to_backward, 'lat', backward)  5.61 us
    ppermute x4, starting transfers between devices, on_device(): moved = [lax.ppermute(part, 'tm', step) for part in carried]  5.16 us
    ppermute x4, waiting for transfers between devices, on_device(): moved = [lax.ppermute(part, 'tm', step) for part in carried]  5.14 us
    ppermute x3, starting transfers between devices, on_device(): lax.ppermute(to_onward, 'lat', onward)  4.63 us
    ppermute x1, starting transfers between devices, on_device(): previous_north = lax.ppermute(final_north, 'tm', following[:-1])  4.47 us
    ppermute x2, waiting for transfers between devices, on_device(): lax.ppermute(part, 'tm', [(i, i ^ 2) for i in range(windows)])  4.42 us
    ppermute x1, waiting for transfers between devices, on_device(): previous_north = lax.ppermute(final_north, 'tm', following[:-1])  2.29 us
  transfers between devices with their start and end apart: 16, of which 7 were waited for; matrix products, arithmetic and copies ran while one was open for 0% of the time, Pallas kernels for 48%

profile of v7, /device:TPU:16, one launch (start us, length us, event | category | flops | bytes accessed | tf_op | source)
XLA Modules:
  0.0 73.9 jit_solution(9861334613799310463)
XLA Ops:
  0.6 1.3 %multiply_bitcast_fusion = f32[32,4096]{1,0:T(8,128)S(1)} fusion(f32[1,32,4096]{2,1,0:T(8,128)} %param.6, f32[1,32,4096]{2,1,0:T(8,128)} %param.5), kind=kLoop, calls=%fused_computation | loop fusion | flops 131072 | bytes 1572864 | tf_op jit(solution)/shard_map/mul | solution.py:208
  1.9 0.0 copy-start
  1.9 0.0 copy-start.1
  2.0 0.1 collective-permute-start
  2.0 0.9 %copy-done = f32[1,32,4096]{2,1,0:T(8,128)S(1)} copy-done((f32[1,32,4096]{2,1,0:T(8,128)S(1)}, f32[1,32,4096]{2,1,0:T(8,128)}, u32[]{:S(2)}) %copy-start) | copy-done | bytes 524312
  2.9 0.2 copy-done.1
  3.1 0.1 shard_map.72
  3.2 1.5 %collective-permute-start.8 = (f32[32,4096]{1,0:T(8,128)S(1)}, f32[32,4096]{1,0:T(8,128)S(1)}, u32[]{:S(2)}, u32[]{:S(2)}) collective-permute-start(f32[32,4096]{1,0:T(8,128)S(1)} %get-tuple-element.32), channel_id=1, source_target_pairs={{0,1},{1,2},{2,3},{3,0},{4,5},{5,6},{6,7},{7,4},{8,9},{9,10},{10,1... | collective-permute-start | bytes 1572872 | tf_op jit(solution)/shard_map/ppermute | solution.py:215
  4.7 0.0 collective-permute-done.b
  4.8 1.6 %collective-permute-start.4 = (f32[32,1024]{1,0:T(8,128)S(1)}, f32[32,1024]{1,0:T(8,128)S(1)}, u32[]{:S(2)}, u32[]{:S(2)}) collective-permute-start(f32[32,1024]{1,0:T(8,128)S(1)} %get-tuple-element.60.a), channel_id=1, source_target_pairs={{0,8},{4,12},{8,0},{12,4},{16,24},{20,28},{24,16},{28,20},{1,9},{5... | collective-permute-start | bytes 393224 | tf_op jit(solution)/shard_map/ppermute | solution.py:223
  6.4 0.4 collective-permute-start.1
  6.9 4.3 %collective-permute-done.4.b.refs_3_ = f32[32,1024]{1,0:T(8,128)S(1)} collective-permute-done((f32[32,1024]{1,0:T(8,128)S(1)}, f32[32,1024]{1,0:T(8,128)S(1)}, u32[]{:S(2)}, u32[]{:S(2)}) %collective-permute-start.4) | collective-permute-done | bytes 131104 | tf_op jit(solution)/shard_map/ppermute | solution.py:223
  11.2 1.3 %collective-permute-start.5 = (f32[32,1024]{1,0:T(8,128)S(1)}, f32[32,1024]{1,0:T(8,128)S(1)}, u32[]{:S(2)}, u32[]{:S(2)}) collective-permute-start(f32[32,1024]{1,0:T(8,128)S(1)} %shard_map.70), channel_id=1, source_target_pairs={{8,16},{12,20},{9,17},{13,21},{10,18},{14,22},{11,19},{15,23}} | collective-permute-start | bytes 393224 | tf_op jit(solution)/shard_map/ppermute | solution.py:228
  12.5 0.1 collective-permute-done.1.b.refs_0_
  12.6 1.3 %collective-permute-start.2 = (f32[32,1024]{1,0:T(8,128)S(1)}, f32[32,1024]{1,0:T(8,128)S(1)}, u32[]{:S(2)}, u32[]{:S(2)}) collective-permute-start(f32[32,1024]{1,0:T(8,128)S(1)} %shard_map.69), channel_id=1, source_target_pairs={{8,16},{12,20},{9,17},{13,21},{10,18},{14,22},{11,19},{15,23}} | collective-permute-start | bytes 393224 | tf_op jit(solution)/shard_map/ppermute | solution.py:228
  13.9 1.9 %collective-permute-start.11 = (f32[32,4096]{1,0:T(8,128)S(1)}, f32[32,4096]{1,0:T(8,128)S(1)}, u32[]{:S(2)}, u32[]{:S(2)}) collective-permute-start(f32[32,4096]{1,0:T(8,128)S(1)} %get-tuple-element.40), channel_id=1, source_target_pairs={{1,0},{2,1},{3,2},{0,3},{5,4},{6,5},{7,6},{4,7},{9,8},{10,9},{11,1... | collective-permute-start | bytes 1572872 | tf_op jit(solution)/shard_map/ppermute | solution.py:215
  15.9 2.7 %collective-permute-done.5.refs_4_ = f32[32,1024]{1,0:T(8,128)S(1)} collective-permute-done((f32[32,1024]{1,0:T(8,128)S(1)}, f32[32,1024]{1,0:T(8,128)S(1)}, u32[]{:S(2)}, u32[]{:S(2)}) %collective-permute-start.5) | collective-permute-done | bytes 131104 | tf_op jit(solution)/shard_map/ppermute | solution.py:228
  18.6 1.3 %collective-permute-start.6 = (f32[32,1024]{1,0:T(8,128)S(1)}, f32[32,1024]{1,0:T(8,128)S(1)}, u32[]{:S(2)}, u32[]{:S(2)}) collective-permute-start(f32[32,1024]{1,0:T(8,128)S(1)} %collective-permute-done.5.refs_4_), channel_id=1, source_target_pairs={{16,24},{20,28},{17,25},{21,29},{18,26},{22,30},{19,27},{23,31}} | collective-permute-start | bytes 393224 | tf_op jit(solution)/shard_map/ppermute | solution.py:228
  19.9 0.1 collective-permute-done.2.refs_1_
  20.0 1.3 %collective-permute-start.3 = (f32[32,1024]{1,0:T(8,128)S(1)}, f32[32,1024]{1,0:T(8,128)S(1)}, u32[]{:S(2)}, u32[]{:S(2)}) collective-permute-start(f32[32,1024]{1,0:T(8,128)S(1)} %collective-permute-done.2.refs_1_), channel_id=1, source_target_pairs={{16,24},{20,28},{17,25},{21,29},{18,26},{22,30},{19,27},{23,31}} | collective-permute-start | bytes 393224 | tf_op jit(solution)/shard_map/ppermute | solution.py:228
  21.3 0.1 shard_map.73
  21.4 0.0 collective-permute-done.8.side
  21.4 0.1 shard_map.74
  21.4 0.9 %collective-permute-done.6.refs_5_ = f32[32,1024]{1,0:T(8,128)S(1)} collective-permute-done((f32[32,1024]{1,0:T(8,128)S(1)}, f32[32,1024]{1,0:T(8,128)S(1)}, u32[]{:S(2)}, u32[]{:S(2)}) %collective-permute-start.6) | collective-permute-done | bytes 131104 | tf_op jit(solution)/shard_map/ppermute | solution.py:228
  22.4 1.4 %collective-permute-done.3.refs_2_ = f32[32,1024]{1,0:T(8,128)S(1)} collective-permute-done((f32[32,1024]{1,0:T(8,128)S(1)}, f32[32,1024]{1,0:T(8,128)S(1)}, u32[]{:S(2)}, u32[]{:S(2)}) %collective-permute-start.3) | collective-permute-done | bytes 131104 | tf_op jit(solution)/shard_map/ppermute | solution.py:228
  23.8 0.1 shard_map.71
  23.9 0.1 collective-permute-start.9
  24.0 1.5 %collective-permute-start.12 = (f32[16,2048]{1,0:T(8,128)S(1)}, f32[16,2048]{1,0:T(8,128)S(1)}, u32[]{:S(2)}, u32[]{:S(2)}) collective-permute-start(f32[16,2048]{1,0:T(8,128)S(1)} %get-tuple-element.46), channel_id=1, source_target_pairs={{0,1},{1,2},{2,3},{3,0},{4,5},{5,6},{6,7},{7,4},{8,9},{9,10},{10,1... | collective-permute-start | bytes 393224 | tf_op jit(solution)/shard_map/ppermute | solution.py:238
  25.5 0.0 collective-permute-done.9.arrived
  25.6 1.5 %collective-permute-start.13 = (f32[16,2048]{1,0:T(8,128)S(1)}, f32[16,2048]{1,0:T(8,128)S(1)}, u32[]{:S(2)}, u32[]{:S(2)}) collective-permute-start(f32[16,2048]{1,0:T(8,128)S(1)} %get-tuple-element.47), channel_id=1, source_target_pairs={{0,1},{1,2},{2,3},{3,0},{4,5},{5,6},{6,7},{7,4},{8,9},{9,10},{10,1... | collective-permute-start | bytes 393224 | tf_op jit(solution)/shard_map/ppermute | solution.py:244
  27.1 1.7 %collective-permute-start.7 = (f32[16,2048]{1,0:T(8,128)S(1)}, f32[16,2048]{1,0:T(8,128)S(1)}, u32[]{:S(2)}, u32[]{:S(2)}) collective-permute-start(f32[16,2048]{1,0:T(8,128)S(1)} %get-tuple-element.30), channel_id=1, source_target_pairs={{1,0},{2,1},{3,2},{0,3},{5,4},{6,5},{7,6},{4,7},{9,8},{10,9},{11,1... | collective-permute-start | bytes 393224 | tf_op jit(solution)/shard_map/ppermute | solution.py:238
  28.8 2.0 %collective-permute-start.10 = (f32[16,2048]{1,0:T(8,128)S(1)}, f32[16,2048]{1,0:T(8,128)S(1)}, u32[]{:S(2)}, u32[]{:S(2)}) collective-permute-start(f32[16,2048]{1,0:T(8,128)S(1)} %get-tuple-element.38), channel_id=1, source_target_pairs={{1,0},{2,1},{3,2},{0,3},{5,4},{6,5},{7,6},{4,7},{9,8},{10,9},{11,1... | collective-permute-start | bytes 393224 | tf_op jit(solution)/shard_map/ppermute | solution.py:244
  30.8 0.0 collective-permute-done.11.side
  30.8 0.1 broadcast_in_dim.14.paces
  30.9 22.7 %shard_map.77 = (f32[32,64,128]{2,1,0:T(8,128)S(1)}, f32[32,64,128]{2,1,0:T(8,128)S(1)}) custom-call(f32[16,128]{1,0:T(8,128)S(1)} %broadcast_in_dim.14.paces, f32[32,2048]{1,0:T(8,128)S(1)} %get-tuple-element.48.own, f32[32,2048]{1,0:T(8,128)S(1)} %get-tuple-element.49.other, f32[32,64,128]{2,1,0:T(8,128)S(1)} %get-tuple-element.42.c_in.c_all, ...), custom_call_target="tpu_custom_call" | custom-call | flops 16777216 | tf_op jit(solution)/shard_map/pallas_call | solution.py:16
  53.6 0.0 collective-permute-done.12.own
  53.6 0.0 collective-permute-done.13.other
  53.6 5.7 %shard_map.78 = (f32[32,64,128]{2,1,0:T(8,128)S(1)}, f32[32,64,128]{2,1,0:T(8,128)S(1)}, f32[16,4096]{1,0:T(8,128)S(1)}) custom-call(f32[16,128]{1,0:T(8,128)S(1)} %broadcast_in_dim.14.paces, f32[16,2048]{1,0:T(8,128)S(1)} %collective-permute-done.12.own, ...), custom_call_target="tpu_custom_call", output_to_operand_aliasing={{0}: (5, {}), {1}: (6, {})} | custom-call | flops 16777216 | tf_op jit(solution)/shard_map/pallas_call | solution.py:16
  59.3 0.1 shard_map.76
  59.4 0.2 collective-permute-start.15
  59.6 0.0 collective-permute-done.7.own
  59.6 0.0 collective-permute-done.10.other
  59.6 5.7 %shard_map.79 = (f32[32,64,128]{2,1,0:T(8,128)S(1)}, f32[32,64,128]{2,1,0:T(8,128)S(1)}, f32[16,4096]{1,0:T(8,128)S(1)}) custom-call(f32[16,128]{1,0:T(8,128)S(1)} %broadcast_in_dim.14.paces, f32[16,2048]{1,0:T(8,128)S(1)} %collective-permute-done.7.own, f32[16,2048]{1,0:T(8,128)S(1)} %collective-permute-done.10.other, ...), custom_call_target="tpu_custom_call", output_to_operand_aliasing={{0}: (5, {}), {1}: (6, {})} | custom-call | flops 16777216 | tf_op jit(solution)/shard_map/pallas_call | solution.py:16
  65.3 4.5 %collective-permute-start.14 = (f32[16,4096]{1,0:T(8,128)S(1)}, f32[16,4096]{1,0:T(8,128)S(1)}, u32[]{:S(2)}, u32[]{:S(2)}) collective-permute-start(f32[16,4096]{1,0:T(8,128)S(1)} %get-tuple-element.54.refs_1_), channel_id=1, source_target_pairs={{0,4},{4,8},{8,12},{12,16},{16,20},{20,24},{24,28},{1,5},{5,9},{9,... | collective-permute-start | bytes 786440 | tf_op jit(solution)/shard_map/ppermute | solution.py:258
  69.8 0.0 collective-permute-done.15.previous
  69.8 0.9 %shard_map.80 = (f32[32,4096]{1,0:T(8,128)}, f32[32,4096]{1,0:T(8,128)}) custom-call(f32[16,4096]{1,0:T(8,128)S(1)} %collective-permute-done.15.previous, f32[32,2048]{1,0:T(8,128)S(1)} %get-tuple-element.48.own, f32[32,2048]{1,0:T(8,128)S(1)} %get-tuple-element.49.other, f32[16,4096]{1,0:T(8,128)S(1)} %get-tuple-element.55.refs_0_, ...), custom_call_target="tpu_custom_call" | custom-call | tf_op jit(solution)/shard_map/pallas_call | solution.py:184
  70.7 2.3 %collective-permute-done.14.previous = f32[16,4096]{1,0:T(8,128)S(1)} collective-permute-done((f32[16,4096]{1,0:T(8,128)S(1)}, f32[16,4096]{1,0:T(8,128)S(1)}, u32[]{:S(2)}, u32[]{:S(2)}) %collective-permute-start.14) | collective-permute-done | bytes 262176 | tf_op jit(solution)/shard_map/ppermute | solution.py:258
  73.0 0.7 %shard_map.81 = f32[32,4096]{1,0:T(8,128)} custom-call(f32[16,4096]{1,0:T(8,128)S(1)} %collective-permute-done.14.previous, f32[32,2048]{1,0:T(8,128)S(1)} %get-tuple-element.48.own, f32[32,2048]{1,0:T(8,128)S(1)} %get-tuple-element.49.other, f32[32,4096]{1,0:T(8,128)} %get-tuple-element.56.refs_0_), custom_call_target="tpu_custom_call", output_to_operand_aliasing={{}: (3, {})} | custom-call | tf_op jit(solution)/shard_map/pallas_call | solution.py:184
  (8 shorter events, 0.2 us)
Async XLA Ops:
  1.9 1.0 %copy-start = (f32[1,32,4096]{2,1,0:T(8,128)S(1)}, f32[1,32,4096]{2,1,0:T(8,128)}, u32[]{:S(2)}) copy-start(f32[1,32,4096]{2,1,0:T(8,128)} %param.7) | copy-start | bytes 1572868
  1.9 1.2 %copy-start.1 = (f32[1,32,4096]{2,1,0:T(8,128)S(1)}, f32[1,32,4096]{2,1,0:T(8,128)}, u32[]{:S(2)}) copy-start(f32[1,32,4096]{2,1,0:T(8,128)} %param.8) | copy-start | bytes 1572868
  2.0 2.8 %collective-permute-start = (f32[32,2048]{1,0:T(8,128)S(1)}, f32[32,2048]{1,0:T(8,128)S(1)}, u32[]{:S(2)}, u32[]{:S(2)}) collective-permute-start(f32[32,2048]{1,0:T(8,128)S(1)} %get-tuple-element.58.other), channel_id=1, source_target_pairs={{0,4},{4,0},{8,12},{12,8},{16,20},{20,16},{24,28},{28,24},{1,5},{5... | collective-permute-start | bytes 786440 | tf_op jit(solution)/shard_map/ppermute | solution.py:220
  3.2 18.2 %collective-permute-start.8 = (f32[32,4096]{1,0:T(8,128)S(1)}, f32[32,4096]{1,0:T(8,128)S(1)}, u32[]{:S(2)}, u32[]{:S(2)}) collective-permute-start(f32[32,4096]{1,0:T(8,128)S(1)} %get-tuple-element.32), channel_id=1, source_target_pairs={{0,1},{1,2},{2,3},{3,0},{4,5},{5,6},{6,7},{7,4},{8,9},{9,10},{10,1... | collective-permute-start | bytes 1572872 | tf_op jit(solution)/shard_map/ppermute | solution.py:215
  4.8 6.4 %collective-permute-start.4 = (f32[32,1024]{1,0:T(8,128)S(1)}, f32[32,1024]{1,0:T(8,128)S(1)}, u32[]{:S(2)}, u32[]{:S(2)}) collective-permute-start(f32[32,1024]{1,0:T(8,128)S(1)} %get-tuple-element.60.a), channel_id=1, source_target_pairs={{0,8},{4,12},{8,0},{12,4},{16,24},{20,28},{24,16},{28,20},{1,9},{5... | collective-permute-start | bytes 393224 | tf_op jit(solution)/shard_map/ppermute | solution.py:223
  6.4 6.2 %collective-permute-start.1 = (f32[32,1024]{1,0:T(8,128)S(1)}, f32[32,1024]{1,0:T(8,128)S(1)}, u32[]{:S(2)}, u32[]{:S(2)}) collective-permute-start(f32[32,1024]{1,0:T(8,128)S(1)} %get-tuple-element.61.a), channel_id=1, source_target_pairs={{0,8},{4,12},{8,0},{12,4},{16,24},{20,28},{24,16},{28,20},{1,9},{5... | collective-permute-start | bytes 393224 | tf_op jit(solution)/shard_map/ppermute | solution.py:223
  11.2 7.3 %collective-permute-start.5 = (f32[32,1024]{1,0:T(8,128)S(1)}, f32[32,1024]{1,0:T(8,128)S(1)}, u32[]{:S(2)}, u32[]{:S(2)}) collective-permute-start(f32[32,1024]{1,0:T(8,128)S(1)} %shard_map.70), channel_id=1, source_target_pairs={{8,16},{12,20},{9,17},{13,21},{10,18},{14,22},{11,19},{15,23}} | collective-permute-start | bytes 393224 | tf_op jit(solution)/shard_map/ppermute | solution.py:228
  12.6 7.3 %collective-permute-start.2 = (f32[32,1024]{1,0:T(8,128)S(1)}, f32[32,1024]{1,0:T(8,128)S(1)}, u32[]{:S(2)}, u32[]{:S(2)}) collective-permute-start(f32[32,1024]{1,0:T(8,128)S(1)} %shard_map.69), channel_id=1, source_target_pairs={{8,16},{12,20},{9,17},{13,21},{10,18},{14,22},{11,19},{15,23}} | collective-permute-start | bytes 393224 | tf_op jit(solution)/shard_map/ppermute | solution.py:228
  13.9 16.9 %collective-permute-start.11 = (f32[32,4096]{1,0:T(8,128)S(1)}, f32[32,4096]{1,0:T(8,128)S(1)}, u32[]{:S(2)}, u32[]{:S(2)}) collective-permute-start(f32[32,4096]{1,0:T(8,128)S(1)} %get-tuple-element.40), channel_id=1, source_target_pairs={{1,0},{2,1},{3,2},{0,3},{5,4},{6,5},{7,6},{4,7},{9,8},{10,9},{11,1... | collective-permute-start | bytes 1572872 | tf_op jit(solution)/shard_map/ppermute | solution.py:215
  18.6 3.8 %collective-permute-start.6 = (f32[32,1024]{1,0:T(8,128)S(1)}, f32[32,1024]{1,0:T(8,128)S(1)}, u32[]{:S(2)}, u32[]{:S(2)}) collective-permute-start(f32[32,1024]{1,0:T(8,128)S(1)} %collective-permute-done.5.refs_4_), channel_id=1, source_target_pairs={{16,24},{20,28},{17,25},{21,29},{18,26},{22,30},{19,27},{23,31}} | collective-permute-start | bytes 393224 | tf_op jit(solution)/shard_map/ppermute | solution.py:228
  20.0 3.8 %collective-permute-start.3 = (f32[32,1024]{1,0:T(8,128)S(1)}, f32[32,1024]{1,0:T(8,128)S(1)}, u32[]{:S(2)}, u32[]{:S(2)}) collective-permute-start(f32[32,1024]{1,0:T(8,128)S(1)} %collective-permute-done.2.refs_1_), channel_id=1, source_target_pairs={{16,24},{20,28},{17,25},{21,29},{18,26},{22,30},{19,27},{23,31}} | collective-permute-start | bytes 393224 | tf_op jit(solution)/shard_map/ppermute | solution.py:228
  23.9 1.6 %collective-permute-start.9 = (f32[32,2048]{1,0:T(8,128)S(1)}, f32[32,2048]{1,0:T(8,128)S(1)}, u32[]{:S(2)}, u32[]{:S(2)}) collective-permute-start(f32[32,2048]{1,0:T(8,128)S(1)} %get-tuple-element.37), channel_id=1, source_target_pairs={{0,4},{4,0},{8,12},{12,8},{16,20},{20,16},{24,28},{28,24},{1,5},{5... | collective-permute-start | bytes 786440 | tf_op jit(solution)/shard_map/ppermute | solution.py:240
  24.0 29.6 %collective-permute-start.12 = (f32[16,2048]{1,0:T(8,128)S(1)}, f32[16,2048]{1,0:T(8,128)S(1)}, u32[]{:S(2)}, u32[]{:S(2)}) collective-permute-start(f32[16,2048]{1,0:T(8,128)S(1)} %get-tuple-element.46), channel_id=1, source_target_pairs={{0,1},{1,2},{2,3},{3,0},{4,5},{5,6},{6,7},{7,4},{8,9},{9,10},{10,1... | collective-permute-start | bytes 393224 | tf_op jit(solution)/shard_map/ppermute | solution.py:238
  25.6 28.0 %collective-permute-start.13 = (f32[16,2048]{1,0:T(8,128)S(1)}, f32[16,2048]{1,0:T(8,128)S(1)}, u32[]{:S(2)}, u32[]{:S(2)}) collective-permute-start(f32[16,2048]{1,0:T(8,128)S(1)} %get-tuple-element.47), channel_id=1, source_target_pairs={{0,1},{1,2},{2,3},{3,0},{4,5},{5,6},{6,7},{7,4},{8,9},{9,10},{10,1... | collective-permute-start | bytes 393224 | tf_op jit(solution)/shard_map/ppermute | solution.py:244
  27.1 32.5 %collective-permute-start.7 = (f32[16,2048]{1,0:T(8,128)S(1)}, f32[16,2048]{1,0:T(8,128)S(1)}, u32[]{:S(2)}, u32[]{:S(2)}) collective-permute-start(f32[16,2048]{1,0:T(8,128)S(1)} %get-tuple-element.30), channel_id=1, source_target_pairs={{1,0},{2,1},{3,2},{0,3},{5,4},{6,5},{7,6},{4,7},{9,8},{10,9},{11,1... | collective-permute-start | bytes 393224 | tf_op jit(solution)/shard_map/ppermute | solution.py:238
  28.8 2.0 %copy-start.2 = (f32[1,16]{1,0:T(1,128)S(1)}, f32[1,16]{1,0:T(1,128)}, u32[]{:S(2)}) copy-start(f32[1,16]{1,0:T(1,128)} %param.9) | copy-start | bytes 196
  28.8 30.8 %collective-permute-start.10 = (f32[16,2048]{1,0:T(8,128)S(1)}, f32[16,2048]{1,0:T(8,128)S(1)}, u32[]{:S(2)}, u32[]{:S(2)}) collective-permute-start(f32[16,2048]{1,0:T(8,128)S(1)} %get-tuple-element.38), channel_id=1, source_target_pairs={{1,0},{2,1},{3,2},{0,3},{5,4},{6,5},{7,6},{4,7},{9,8},{10,9},{11,1... | collective-permute-start | bytes 393224 | tf_op jit(solution)/shard_map/ppermute | solution.py:244
  59.4 10.4 %collective-permute-start.15 = (f32[16,4096]{1,0:T(8,128)S(1)}, f32[16,4096]{1,0:T(8,128)S(1)}, u32[]{:S(2)}, u32[]{:S(2)}) collective-permute-start(f32[16,4096]{1,0:T(8,128)S(1)} %get-tuple-element.55.refs_0_), channel_id=1, source_target_pairs={{0,4},{4,8},{8,12},{12,16},{16,20},{20,24},{24,28},{28,0},{1,5},{5... | collective-permute-start | bytes 786440 | tf_op jit(solution)/shard_map/ppermute | solution.py:252
  65.3 7.7 %collective-permute-start.14 = (f32[16,4096]{1,0:T(8,128)S(1)}, f32[16,4096]{1,0:T(8,128)S(1)}, u32[]{:S(2)}, u32[]{:S(2)}) collective-permute-start(f32[16,4096]{1,0:T(8,128)S(1)} %get-tuple-element.54.refs_1_), channel_id=1, source_target_pairs={{0,4},{4,8},{8,12},{12,16},{16,20},{20,24},{24,28},{1,5},{5,9},{9,... | collective-permute-start | bytes 786440 | tf_op jit(solution)/shard_map/ppermute | solution.py:258
